TPU v7x, 128 devices: a whole 4x4x4 slice. The times are simulated.
128 devices in a mesh: fsdp: 16 (over z, y_lo, core), tp: 8 (over y_hi, x).
Axes of the slice: x: 4, y: 4 (y_hi: 2, y_lo: 2; y = y_hi * 2 + y_lo), z: 4, core: 2. Of those that a mesh axis runs over, the one named last changes fastest.
Arguments:
- tokens: bfloat16 [2, 2304, 8192], P(None, 'fsdp'), may hold values from -6 to 6
- w_query: bfloat16 [8192, 8192], P('fsdp', 'tp'), may hold values from -0.0625 to 0.0625
- w_keyval: bfloat16 [8192, 2, 1024], P('fsdp', None, 'tp'), may hold values from -0.0625 to 0.0625
- b_query: bfloat16 [8192], P('tp')
- b_keyval: bfloat16 [2, 1024], P(None, 'tp'), may hold values from -3 to 3
- rotary_perm: int32 [128], replicated, may hold values from 0 to 127, each once
- cache: bfloat16 [2, 2304, 8, 256, 128], P(None, 'fsdp', 'tp')
- lengths: int32 [2304], P('fsdp'), may hold values from 2 to 256
Outputs:
- attention: bfloat16 [2, 2304, 8192], P(None, 'fsdp', 'tp')
All inputs are finite; a program needn't handle non-finite values.
Results may differ from a plain program's by a relative error of at most 0.0063.
Values may be sent and summed in bfloat16 or wider, within the bound.
No kernel may reach another device: no remote copies, remote signals or barrier semaphores. Data moves between devices by JAX's collectives and lax.ppermute only.
A program may use at most 128 MiB of HBM per device.

v0:
```python
import jax
import jax.numpy as jnp
from jax import lax
from jax.sharding import PartitionSpec as P

HQ = 64
HK = 8


rope_base = 1000000.0
neg_large = -1e30


def passed_along(value, axis, by):
    length = lax.axis_size(axis)
    return lax.ppermute(value, axis, [(i, (i + by) % length) for i in range(length)])


def rotate(vectors, position):
    head_size = vectors.shape[-1]
    half_size = head_size // 2
    pair_index = jnp.arange(half_size, dtype=jnp.float32)
    inverse = rope_base ** (-2.0 * pair_index / head_size)
    angles = position * inverse
    cos_part = jnp.cos(angles)
    sin_part = jnp.sin(angles)
    first_half = vectors[..., :half_size]
    second = vectors[..., half_size:]
    return jnp.concatenate(
        [first_half * cos_part - second * sin_part, second * cos_part + first_half * sin_part],
        axis=-1,
    )


def attend(queries, key_new, value_new, cache, lengths):
    score_scale = queries.shape[-1] ** (-0.5)
    cached_scores = (
        jnp.einsum("srgqd,rgcd->srgqc", queries, cache[0], preferred_element_type=jnp.float32)
        * score_scale
    )
    fresh_scores = (
        jnp.einsum("srgqd,trgd->srgqt", queries, key_new, preferred_element_type=jnp.float32)
        * score_scale
    )
    slots = jnp.arange(cache.shape[3], dtype=jnp.int32)
    visible_old = (slots[None, :] < lengths[:, None])[None, :, None, None, :]
    step_ids = jnp.arange(queries.shape[0], dtype=jnp.int32)
    visible_new = (step_ids[None, :] <= step_ids[:, None])[:, None, None, None, :]
    cached_scores = jnp.where(visible_old, cached_scores, neg_large)
    fresh_scores = jnp.where(visible_new, fresh_scores, neg_large)
    row_max = jnp.maximum(jnp.max(cached_scores, axis=-1), jnp.max(fresh_scores, axis=-1))[
        ..., None
    ]
    cached_exp = jnp.exp(cached_scores - row_max)
    fresh_exp = jnp.exp(fresh_scores - row_max)
    denominator = jnp.sum(cached_exp, axis=-1, keepdims=True) + jnp.sum(
        fresh_exp, axis=-1, keepdims=True
    )
    cached_weights = (cached_exp / denominator).astype(jnp.bfloat16)
    fresh_weights = (fresh_exp / denominator).astype(jnp.bfloat16)
    result = jnp.einsum(
        "srgqc,rgcd->srgqd", cached_weights, cache[1], preferred_element_type=jnp.float32
    )
    result = result + jnp.einsum(
        "srgqt,trgd->srgqd", fresh_weights, value_new, preferred_element_type=jnp.float32
    )
    return result.astype(jnp.bfloat16)


def reverse_groups(tensor, dim_index, group_count):
    old_shape = tensor.shape
    width_each = old_shape[dim_index] // group_count
    split_view = tensor.reshape(
        old_shape[:dim_index] + (group_count, width_each) + old_shape[dim_index + 1 :]
    )
    return jnp.flip(split_view, axis=dim_index).reshape(old_shape)


def project(flattened, w_query, w_keyval, b_query, b_keyval):
    query_sum = jnp.dot(
        flattened,
        lax.all_gather(w_query, "fsdp", axis=0, tiled=True),
        preferred_element_type=jnp.float32,
    )
    keyval_sum = jnp.einsum(
        "rd,dkc->krc",
        flattened,
        lax.all_gather(w_keyval, "fsdp", axis=0, tiled=True),
        preferred_element_type=jnp.float32,
    )
    query_sum, keyval_sum = (query_sum, keyval_sum)
    queries = (query_sum + b_query.astype(jnp.float32)).astype(jnp.bfloat16)
    key_value = (keyval_sum + b_keyval.astype(jnp.float32)[:, None, :]).astype(jnp.bfloat16)
    return (queries, key_value)


def body(tokens, w_query, w_keyval, b_query, b_keyval, rotary_perm, cache, lengths):
    step_count, row_count, model_width = tokens.shape
    per_group = HQ // HK
    head_size = rotary_perm.shape[0]
    group_count = cache.shape[2]
    half_way = lax.axis_size("tp") // 2
    flattened = tokens.reshape(step_count * row_count, model_width)
    moved = passed_along((w_query, w_keyval, b_query, b_keyval), "tp", half_way)
    queries, key_value = project(flattened, moved[0], moved[1], moved[2], moved[3])
    queries = reverse_groups(queries, 1, group_count)
    key_value = reverse_groups(key_value, 2, group_count)
    queries = queries.reshape(step_count, row_count, group_count, per_group, head_size)
    queries = jnp.take(queries, rotary_perm, axis=4)
    key_value = key_value.reshape(2, step_count, row_count, group_count, head_size)
    key_part = jnp.take(key_value[0], rotary_perm, axis=3)
    value_part = key_value[1]
    positions = (lengths[None, :] + jnp.arange(step_count, dtype=jnp.int32)[:, None]).astype(
        jnp.float32
    )
    query_rot = rotate(queries.astype(jnp.float32), positions[:, :, None, None, None]).astype(
        jnp.bfloat16
    )
    key_rot = rotate(key_part.astype(jnp.float32), positions[:, :, None, None]).astype(jnp.bfloat16)
    result = attend(query_rot, key_rot, value_part, cache, lengths)
    return result.reshape(step_count, row_count, group_count * per_group * head_size)


def solution(mesh):
    placed = (
        P(None, "fsdp", None),
        P("fsdp", "tp"),
        P("fsdp", None, "tp"),
        P("tp"),
        P(None, "tp"),
        P(),
        P(None, "fsdp", "tp", None, None),
        P("fsdp"),
    )
    return jax.shard_map(
        body, mesh=mesh, in_specs=placed, out_specs=P(None, "fsdp", "tp"), check_vma=False
    )
```

profile of v0, /device:TPU:1, one launch (start us, length us, event | category | flops | bytes accessed | tf_op | source)
XLA Modules:
  0.0 199.2 jit_solution(9655364884669363061)
XLA Ops:
  6.5 0.0 all-gather.5.cloned.1.call-start
  6.5 1.0 copy.17
  7.5 3.8 %collective-permute-start.2 = (bf16[512,2,128]{2,0,1:T(8,128)(2,1)S(1)}, bf16[512,2,128]{2,0,1:T(8,128)(2,1)S(1)}, u32[]{:S(2)}, u32[]{:S(2)}) collective-permute-start(bf16[512,2,128]{2,0,1:T(8,128)(2,1)S(1)} %copy.17), channel_id=1, source_target_pairs={{0,4},{1,5},{2,6},{3,7},{4,0},{5,1},{6,2},{7,3},{8,12},{9,13},{10,... | collective-permute-start | bytes 786440 | tf_op jit(solution)/shard_map/ppermute | solution.py:16
  11.3 5.8 %collective-permute-done.2 = bf16[512,2,128]{2,0,1:T(8,128)(2,1)S(1)} collective-permute-done((bf16[512,2,128]{2,0,1:T(8,128)(2,1)S(1)}, bf16[512,2,128]{2,0,1:T(8,128)(2,1)S(1)}, u32[]{:S(2)}, u32[]{:S(2)}) %collective-permute-start.2) | collective-permute-done | bytes 262176 | tf_op jit(solution)/shard_map/ppermute | solution.py:16
  17.1 0.0 copy-start.1
  17.1 0.7 copy-done.1
  17.8 0.0 all-gather.5.cloned.1.call-update
  17.8 0.0 all-gather.3.cloned.1.call-start
  17.9 3.0 %collective-permute-start = (bf16[512,1024]{1,0:T(8,128)(2,1)}, bf16[512,1024]{1,0:T(8,128)(2,1)S(1)}, u32[]{:S(2)}, u32[]{:S(2)}) collective-permute-start(bf16[512,1024]{1,0:T(8,128)(2,1)} %param.9), channel_id=1, source_target_pairs={{0,4},{1,5},{2,6},{3,7},{4,0},{5,1},{6,2},{7,3},{8,12},{9,13},{10,... | collective-permute-start | bytes 3145736 | tf_op jit(solution)/shard_map/ppermute | solution.py:16
  20.9 32.7 %collective-permute-done = bf16[512,1024]{1,0:T(8,128)(2,1)S(1)} collective-permute-done((bf16[512,1024]{1,0:T(8,128)(2,1)}, bf16[512,1024]{1,0:T(8,128)(2,1)S(1)}, u32[]{:S(2)}, u32[]{:S(2)}) %collective-permute-start) | collective-permute-done | bytes 1048608 | tf_op jit(solution)/shard_map/ppermute | solution.py:16
  53.6 0.0 copy-start
  53.6 1.0 copy-done
  54.5 0.0 all-gather.3.cloned.1.call-update
  54.6 3.7 %collective-permute-start.1 = (bf16[1024]{0:T(1024)(128)(2,1)}, bf16[1024]{0:T(1024)(128)(2,1)S(1)}, u32[]{:S(2)}, u32[]{:S(2)}) collective-permute-start(bf16[1024]{0:T(1024)(128)(2,1)} %param.11), channel_id=1, source_target_pairs={{0,4},{1,5},{2,6},{3,7},{4,0},{5,1},{6,2},{7,3},{8,12},{9,13},{10,... | collective-permute-start | bytes 6152 | tf_op jit(solution)/shard_map/ppermute | solution.py:16
  58.2 0.1 collective-permute-start.3
  58.4 0.7 compare_select_fusion
  59.0 0.7 compare_and_fusion
  59.7 0.8 iota_compare_fusion
  60.5 0.8 add_convert_fusion.1
  61.2 2.4 %multiply_cosine_fusion.1 = (f32[2,144,64]{2,0,1:T(2,128)S(1)}, f32[2,144,64]{2,0,1:T(2,128)S(1)}) fusion(f32[64]{0:T(128)S(1)} %multiply_power_fusion, f32[2,144]{0,1:T(8,128)S(1)} %add_convert_fusion.1), kind=kLoop, calls=%fused_computation.42 | loop fusion | flops 18432 | bytes 148864 | tf_op jit(solution)/shard_map/cos | solution.py:25
  63.7 0.0 collective-permute-done.3
  63.7 0.0 collective-permute-done.1
  63.7 4.6 %all-gather.5.cloned.1.call-done = bf16[8192,2,128]{2,0,1:T(8,128)(2,1)} async-done(((bf16[512,2,128]{2,0,1:T(8,128)(2,1)}), bf16[8192,2,128]{2,0,1:T(8,128)(2,1)}) %all-gather.5.cloned.1.call-update) | async-done | bytes 4194320 | tf_op jit(solution)/shard_map/all_gather | solution.py:88
  68.4 5.0 %fusion.17 = bf16[2,288,128]{2,1,0:T(8,128)(2,1)S(1)} fusion(bf16[288,8192,1]{1,0,2:T(8,128)(2,1)} %bitcast.115, bf16[8192,2,128]{2,0,1:T(8,128)(2,1)} %all-gather.5.cloned.1.call-done, f32[2,128]{1,0:T(2,128)S(1)} %convert_element_type.76), kind=kOutput, calls=%fused_computation.30 | convolution fusion | flops 1208107008 | bytes 9061376 | tf_op jit(solution)/shard_map/rd,dkc->krc/dot_general | solution.py:85
  73.4 0.1 copy.18
  73.6 0.9 gather_fusion.1
  74.4 0.1 copy.19
  74.6 0.1 fusion.33
  74.6 2.7 %fusion.37 = (bf16[2,144,64]{2,0,1:T(2,128)(2,1)S(1)}, bf16[2,144,64]{2,0,1:T(2,128)(2,1)S(1)}) fusion(f32[2,144,1,128]{3,0,1,2:T(2,128)S(1)} %fusion.33, f32[64]{0:T(128)S(1)} %multiply_power_fusion, f32[2,144]{0,1:T(8,128)S(1)} %add_convert_fusion.1), kind=kLoop, calls=%fused_computation.62 | loop fusion | flops 165888 | bytes 222592 | tf_op jit(solution)/shard_map/concatenate | solution.py:29
  77.3 84.7 %all-gather.3.cloned.1.call-done = bf16[8192,1024]{1,0:T(8,128)(2,1)} async-done(((bf16[512,1024]{1,0:T(8,128)(2,1)}), bf16[8192,1024]{1,0:T(8,128)(2,1)}) %all-gather.3.cloned.1.call-update) | async-done | bytes 16777232 | tf_op jit(solution)/shard_map/all_gather | solution.py:82
  162.0 10.1 %fusion.9 = bf16[36,8,8,128]{3,1,2,0:T(8,128)(2,1)S(1)} fusion(bf16[288,8192]{1,0:T(8,128)(2,1)} %bitcast.116, bf16[8192,1024]{1,0:T(8,128)(2,1)} %all-gather.3.cloned.1.call-done, f32[1024]{0:T(1024)S(1)} %convert_element_type.72), kind=kOutput, calls=%fused_computation.18 | convolution fusion | flops 4832428032 | bytes 22089728 | tf_op jit(solution)/shard_map/dot_general | solution.py:80
  172.1 0.1 copy.29
  172.2 1.0 copy.14
  173.1 0.7 gather_fusion
  173.8 1.2 copy.15
  175.0 0.1 fusion.21
  175.1 0.5 fusion.19
  175.6 5.4 %fusion.4 = (f32[2,144,8]{2,0,1:T(2,128)S(1)}, f32[144,2,8,256]{3,2,1,0:T(8,128)S(1)}) fusion(pred[144,256]{1,0:T(8,128)(4,1)S(1)} %iota_compare_fusion, bf16[2,144,1,256,128]{4,3,1,2,0:T(8,128)(2,1)} %bitcast.110, bf16[2,144,8,64]{3,2,0,1:T(8,128)(2,1)S(1)} %get-tuple-element.6, bf16[2,144,8,64]{3,2,0,1:T(8,128)(2,1)S(1)} %get-tuple-element.5), kind=kOutput, calls=%fused_computation.11 | convolution fusion | flops 153941760 | bytes 12432384 | tf_op jit(solution)/shard_map/srgqd,rgcd->srgqc/dot_general | solution.py:38
  181.0 2.9 %fusion.44 = (f32[2,144,8]{2,0,1:T(2,128)S(1)}, f32[2,144,1,8,2]{3,4,0,1,2:T(2,128)S(1)}) fusion(bf16[2,144,8,64]{3,2,0,1:T(8,128)(2,1)S(1)} %get-tuple-element.6, bf16[2,144,8,64]{3,2,0,1:T(8,128)(2,1)S(1)} %get-tuple-element.5, bf16[2,144,64]{2,0,1:T(2,128)(2,1)S(1)} %get-tuple-element.8, bf16[2,144,64]{2,0,1:T(2,128)(2,1)S(1)} %get-tuple-element.7, ...), kind=kOutput, calls=%fused_computation.74 | convolution fusion | flops 2518272 | bytes 691204 | tf_op jit(solution)/shard_map/srgqd,trgd->srgqt/dot_general | solution.py:42
  183.9 0.1 max.9
  184.0 1.3 fusion.3
  185.3 0.6 fusion.22
  185.9 0.1 add.80
  186.0 4.8 %fusion.5 = f32[144,128,2,8]{1,3,2,0:T(8,128)S(1)} fusion(bf16[2,144,1,256,128]{4,3,1,2,0:T(8,128)(2,1)} %bitcast.111, f32[144,2,8,256]{3,2,1,0:T(8,128)S(1)} %get-tuple-element.14, f32[2,144,8]{2,0,1:T(2,128)S(1)} %add.80, f32[2,144,8]{2,0,1:T(2,128)S(1)} %max.9, pred[144,256]{1,0:T(8,128)(4,1)S(1)} %iota_compare_fusion), kind=kOutput, calls=%fused_computation.13 | convolution fusion | flops 153944064 | bytes 13031424 | tf_op jit(solution)/shard_map/srgqc,rgcd->srgqd/dot_general | solution.py:61
  190.8 0.5 fusion.8
  191.3 0.1 reshape.253
  191.5 1.0 copy.22
  (6 shorter events, 0.0 us)
Async XLA Ops:
  6.5 61.8 %all-gather.5.cloned.1.call-start = ((), (), s32[]{:S(2)}) async-start(), calls=%async_computation.1 | async-start | bytes 4456448 | tf_op jit(solution)/shard_map/all_gather | solution.py:88
  7.5 9.6 %collective-permute-start.2 = (bf16[512,2,128]{2,0,1:T(8,128)(2,1)S(1)}, bf16[512,2,128]{2,0,1:T(8,128)(2,1)S(1)}, u32[]{:S(2)}, u32[]{:S(2)}) collective-permute-start(bf16[512,2,128]{2,0,1:T(8,128)(2,1)S(1)} %copy.17), channel_id=1, source_target_pairs={{0,4},{1,5},{2,6},{3,7},{4,0},{5,1},{6,2},{7,3},{8,12},{9,13},{10,... | collective-permute-start | bytes 786440 | tf_op jit(solution)/shard_map/ppermute | solution.py:16
  17.1 0.7 copy-start.1
  17.8 144.2 %all-gather.3.cloned.1.call-start = ((), (), s32[]{:S(2)}) async-start(), calls=%async_computation | async-start | bytes 17825792 | tf_op jit(solution)/shard_map/all_gather | solution.py:82
  17.9 35.7 %collective-permute-start = (bf16[512,1024]{1,0:T(8,128)(2,1)}, bf16[512,1024]{1,0:T(8,128)(2,1)S(1)}, u32[]{:S(2)}, u32[]{:S(2)}) collective-permute-start(bf16[512,1024]{1,0:T(8,128)(2,1)} %param.9), channel_id=1, source_target_pairs={{0,4},{1,5},{2,6},{3,7},{4,0},{5,1},{6,2},{7,3},{8,12},{9,13},{10,... | collective-permute-start | bytes 3145736 | tf_op jit(solution)/shard_map/ppermute | solution.py:16
  53.6 1.0 copy-start
  54.6 9.1 %collective-permute-start.1 = (bf16[1024]{0:T(1024)(128)(2,1)}, bf16[1024]{0:T(1024)(128)(2,1)S(1)}, u32[]{:S(2)}, u32[]{:S(2)}) collective-permute-start(bf16[1024]{0:T(1024)(128)(2,1)} %param.11), channel_id=1, source_target_pairs={{0,4},{1,5},{2,6},{3,7},{4,0},{5,1},{6,2},{7,3},{8,12},{9,13},{10,... | collective-permute-start | bytes 6152 | tf_op jit(solution)/shard_map/ppermute | solution.py:16
  58.2 5.4 %collective-permute-start.3 = (bf16[2,128]{1,0:T(2,128)(2,1)}, bf16[2,128]{1,0:T(2,128)(2,1)S(1)}, u32[]{:S(2)}, u32[]{:S(2)}) collective-permute-start(bf16[2,128]{1,0:T(2,128)(2,1)} %param.12), channel_id=1, source_target_pairs={{0,4},{1,5},{2,6},{3,7},{4,0},{5,1},{6,2},{7,3},{8,12},{9,13},{10,... | collective-permute-start | bytes 1544 | tf_op jit(solution)/shard_map/ppermute | solution.py:16
Sparse Core Ops, SparseCore 0:
  17.9 50.3 all-gather.4
  70.1 91.8 all-gather.2
where the time goes:
time: 199 us
  waiting for transfers between devices  128 us (64%)
  matrix products  28.6 us (14%)
  between operations  13.6 us (7%)
  other arithmetic  10.7 us (5%)
  starting transfers between devices  10.6 us (5%)
  local copies, waits for them, and re-layouts  7.82 us (4%)
    all_gather x1, waiting for transfers between devices, project(): lax.all_gather(w_query, 'fsdp', axis=0, tiled=True)  84.7 us
    ppermute x4, waiting for transfers between devices, passed_along(): lax.ppermute(value, axis, [(i, (i + by) % length) for i in range(length)])  38.4 us
    ppermute x4, starting transfers between devices, passed_along(): lax.ppermute(value, axis, [(i, (i + by) % length) for i in range(length)])  10.6 us
    dot_general x1, matrix products, project(): jnp.dot(flattened, lax.all_gather(w_query, 'fsdp', axis=0, tiled=True), p...  10.1 us
    dot_general x1, matrix products, attend(): jnp.einsum('srgqd,rgcd->srgqc', queries, cache[0], preferred_element_type...  5.38 us
    dot_general x1, matrix products, project(): jnp.einsum('rd,dkc->krc', flattened, lax.all_gather(w_keyval, 'fsdp', axi...  5.01 us
    dot_general x1, matrix products, attend(): jnp.einsum('srgqc,rgcd->srgqd', cached_weights, cache[1], preferred_eleme...  4.75 us
    all_gather x1, waiting for transfers between devices, project(): lax.all_gather(w_keyval, 'fsdp', axis=0, tiled=True)  4.65 us
  transfers between devices with their start and end apart: 6, of which 4 were waited for; matrix products, arithmetic and copies ran while one was open for 7% of the time, Pallas kernels for 0%

commit v1 on v0

--- a/solution.py
+++ b/solution.py
@@ -5,15 +5,56 @@
 
 HQ = 64
 HK = 8
-
+HD = 128
 
 rope_base = 1000000.0
 neg_large = -1e30
 
+AXES = ("fsdp", "tp")
+N_Z = 4
+N_TP = 8
 
-def passed_along(value, axis, by):
-    length = lax.axis_size(axis)
-    return lax.ppermute(value, axis, [(i, (i + by) % length) for i in range(length)])
+
+def place_of(index):
+    f, t = divmod(index, N_TP)
+    z, rest = divmod(f, 4)
+    y_lo, core = divmod(rest, 2)
+    y_hi, x = divmod(t, 4)
+    return z, y_hi * 2 + y_lo, x, core
+
+
+def index_of(z, y, x, core):
+    z, y, x, core = z % 4, y % 4, x % 4, core % 2
+    return (z * 4 + (y % 2) * 2 + core) * N_TP + (y // 2) * 4 + x
+
+
+def moved(value, to):
+    pairs = [(i, index_of(*to(*place_of(i)))) for i in range(128)]
+    return lax.ppermute(value, AXES, pairs)
+
+
+def z_by(step):
+    return lambda z, y, x, core: (z + step, y, x, core)
+
+
+def other_core(z, y, x, core):
+    return z, y, x, 1 - core
+
+
+def inner_y(z, y, x, core):
+    return z, y ^ 1, x, core
+
+
+def cross_y_core(z, y, x, core):
+    return z, 3 - y, x, 1 - core
+
+
+def cross_y(z, y, x, core):
+    return z, 3 - y, x, core
+
+
+def far_y(z, y, x, core):
+    return z, y + 2, x, core
 
 
 def rotate(vectors, position):
@@ -67,49 +108,70 @@
     return result.astype(jnp.bfloat16)
 
 
-def reverse_groups(tensor, dim_index, group_count):
-    old_shape = tensor.shape
-    width_each = old_shape[dim_index] // group_count
-    split_view = tensor.reshape(
-        old_shape[:dim_index] + (group_count, width_each) + old_shape[dim_index + 1 :]
-    )
-    return jnp.flip(split_view, axis=dim_index).reshape(old_shape)
+def gathered_over_z(block):
+    return [block, moved(block, z_by(1)), moved(block, z_by(-1)), moved(block, z_by(2))]
 
 
-def project(flattened, w_query, w_keyval, b_query, b_keyval):
-    query_sum = jnp.dot(
-        flattened,
-        lax.all_gather(w_query, "fsdp", axis=0, tiled=True),
-        preferred_element_type=jnp.float32,
-    )
-    keyval_sum = jnp.einsum(
-        "rd,dkc->krc",
-        flattened,
-        lax.all_gather(w_keyval, "fsdp", axis=0, tiled=True),
-        preferred_element_type=jnp.float32,
-    )
-    query_sum, keyval_sum = (query_sum, keyval_sum)
-    queries = (query_sum + b_query.astype(jnp.float32)).astype(jnp.bfloat16)
-    key_value = (keyval_sum + b_keyval.astype(jnp.float32)[:, None, :]).astype(jnp.bfloat16)
-    return (queries, key_value)
+def row_sets(tokens):
+    f = lax.axis_index("fsdp")
+    z, y_lo, core = f // 4, (f // 2) % 2, f % 2
+    flat = tokens.reshape(-1, tokens.shape[-1])
+    share = flat.shape[1] // 16
+
+    def slab(dy, dc):
+        parts = []
+        for dz in (0, -1, 1, 2):
+            block = ((z + dz) % 4) * 4 + (y_lo ^ dy) * 2 + (core ^ dc)
+            parts.append(lax.dynamic_slice_in_dim(flat, block * share, share, 1))
+        return jnp.concatenate(parts, axis=1)
+
+    return {
+        (0, 0): slab(0, 0),
+        (0, 1): moved(slab(0, 1), other_core),
+        (1, 0): moved(slab(1, 0), inner_y),
+        (1, 1): moved(slab(1, 1), cross_y_core),
+    }
+
+
+def returned(rows, blocks, bias):
+    weights = jnp.concatenate(blocks, axis=0)
+    sums = {
+        key: jnp.dot(value, weights, preferred_element_type=jnp.float32)
+        for key, value in rows.items()
+    }
+    partner = moved(
+        jnp.stack([sums[0, 1].astype(jnp.bfloat16), sums[1, 1].astype(jnp.bfloat16)]), other_core
+    ).astype(jnp.float32)
+    same = sums[0, 0] + partner[0] + bias.astype(jnp.float32)
+    other = sums[1, 0] + partner[1]
+    same = moved(same.astype(jnp.bfloat16), far_y)
+    other = moved(other.astype(jnp.bfloat16), cross_y)
+    return (same.astype(jnp.float32) + other.astype(jnp.float32)).astype(jnp.bfloat16)
 
 
 def body(tokens, w_query, w_keyval, b_query, b_keyval, rotary_perm, cache, lengths):
     step_count, row_count, model_width = tokens.shape
     per_group = HQ // HK
     head_size = rotary_perm.shape[0]
-    group_count = cache.shape[2]
-    half_way = lax.axis_size("tp") // 2
-    flattened = tokens.reshape(step_count * row_count, model_width)
-    moved = passed_along((w_query, w_keyval, b_query, b_keyval), "tp", half_way)
-    queries, key_value = project(flattened, moved[0], moved[1], moved[2], moved[3])
-    queries = reverse_groups(queries, 1, group_count)
-    key_value = reverse_groups(key_value, 2, group_count)
-    queries = queries.reshape(step_count, row_count, group_count, per_group, head_size)
+
+    early = 3 * head_size
+    first = jnp.concatenate([w_keyval[:, 0], w_keyval[:, 1], w_query[:, :early]], axis=1)
+    second = w_query[:, early:]
+    first_bias = jnp.concatenate([b_keyval[0], b_keyval[1], b_query[:early]])
+    rows = row_sets(tokens)
+    first_blocks = gathered_over_z(first)
+    second, first_blocks = lax.optimization_barrier((second, first_blocks))
+    second_blocks = gathered_over_z(second)
+    first_sums = returned(rows, first_blocks, first_bias)
+    second_sums = returned(rows, second_blocks, b_query[early:])
+
+    queries = jnp.concatenate([first_sums[:, 2 * head_size :], second_sums], axis=1)
+    queries = queries.reshape(step_count, row_count, 1, per_group, head_size)
     queries = jnp.take(queries, rotary_perm, axis=4)
-    key_value = key_value.reshape(2, step_count, row_count, group_count, head_size)
-    key_part = jnp.take(key_value[0], rotary_perm, axis=3)
-    value_part = key_value[1]
+    key_part = first_sums[:, :head_size].reshape(step_count, row_count, 1, head_size)
+    key_part = jnp.take(key_part, rotary_perm, axis=3)
+    value_part = first_sums[:, head_size : 2 * head_size]
+    value_part = value_part.reshape(step_count, row_count, 1, head_size)
     positions = (lengths[None, :] + jnp.arange(step_count, dtype=jnp.int32)[:, None]).astype(
         jnp.float32
     )
@@ -118,7 +180,7 @@
     )
     key_rot = rotate(key_part.astype(jnp.float32), positions[:, :, None, None]).astype(jnp.bfloat16)
     result = attend(query_rot, key_rot, value_part, cache, lengths)
-    return result.reshape(step_count, row_count, group_count * per_group * head_size)
+    return result.reshape(step_count, row_count, per_group * head_size)
 
 
 def solution(mesh):

time: 199 us -> 129 us (0.65)
  waiting for transfers between devices: 128 us -> 62 us
  starting transfers between devices: 10.6 us -> 24.9 us
  between operations: 13.6 us -> 0.55 us
  matrix products: 28.6 us -> 22.5 us
  local copies, waits for them, and re-layouts: 7.82 us -> 10.2 us
    all_gather x2 -> x0, waiting for transfers between devices: 89.3 us -> none  [the longest x1 84.7 us: project(): lax.all_gather(w_query, 'fsdp', axis=0, tiled=True)]
    ppermute x4 -> x15, waiting for transfers between devices: 38.4 us -> 62 us  [moved(): return lax.ppermute(value, AXES, pairs)]
    ppermute x4 -> x15, starting transfers between devices: 10.6 us -> 24.9 us  [moved(): return lax.ppermute(value, AXES, pairs)]
    dot_general x2 -> x8, matrix products: 15.1 us -> 8.93 us  [returned(): jnp.dot(value, weights, preferred_element_type=jnp.float32)]
    dynamic_slice x0 -> x1, local copies, waits for them, and re-layouts: none -> 2.65 us  [slab(): parts.append(lax.dynamic_slice_in_dim(flat, block * share, share, 1))]
    unnamed x6 -> x17, local copies, waits for them, and re-layouts: 2.76 us -> 0.64 us
  transfers between devices with their start and end apart: 6 -> 15, of which waited for: 4 -> 8; matrix products, arithmetic and copies ran while one was open for 7% -> 15% of each run, Pallas kernels for 0% -> 0%
where the time goes in v1:
time: 129 us
  waiting for transfers between devices  62 us (48%)
  starting transfers between devices  24.9 us (19%)
  matrix products  22.5 us (17%)
  local copies, waits for them, and re-layouts  10.2 us (8%)
  other arithmetic  9.18 us (7%)
    ppermute x15, waiting for transfers between devices, moved(): return lax.ppermute(value, AXES, pairs)  62 us
    ppermute x15, starting transfers between devices, moved(): return lax.ppermute(value, AXES, pairs)  24.9 us
    dot_general x8, matrix products, returned(): jnp.dot(value, weights, preferred_element_type=jnp.float32)  8.93 us
    dot_general x1, matrix products, attend(): jnp.einsum('srgqd,rgcd->srgqc', queries, cache[0], preferred_element_type...  5.37 us
    dot_general x1, matrix products, attend(): jnp.einsum('srgqc,rgcd->srgqd', cached_weights, cache[1], preferred_eleme...  4.76 us
    concatenate x2, other arithmetic, rotate(): jnp.concatenate([first_half * cos_part - second * sin_part, second * cos_...  3.2 us
    dot_general x1, matrix products, attend(): jnp.einsum('srgqd,trgd->srgqt', queries, key_new, preferred_element_type=...  2.89 us
    dynamic_slice x1, local copies, waits for them, and re-layouts, slab(): parts.append(lax.dynamic_slice_in_dim(flat, block * share, share, 1))  2.65 us
  transfers between devices with their start and end apart: 15, of which 8 were waited for; matrix products, arithmetic and copies ran while one was open for 15% of the time, Pallas kernels for 0%

profile of v1, /device:TPU:1, one launch (start us, length us, event | category | flops | bytes accessed | tf_op | source)
XLA Modules:
  0.0 129.3 jit_solution(15864665851776209634)
XLA Ops:
  0.0 1.5 %fusion.52 = (bf16[512,1,128]{2,1,0:T(2,128)(2,1)S(1)}, bf16[512,1,128]{2,1,0:T(2,128)(2,1)S(1)}) fusion(bf16[512,2,128]{2,1,0:T(2,128)(2,1)} %param.10), kind=kLoop, calls=%fused_computation.132 | loop fusion | bytes 524288 | tf_op jit(solution)/shard_map/slice | solution.py:158
  1.7 4.5 %collective-permute-start.2 = (bf16[512,640]{1,0:T(8,128)(2,1)S(1)}, bf16[512,640]{1,0:T(8,128)(2,1)S(1)}, u32[]{:S(2)}, u32[]{:S(2)}) collective-permute-start(bf16[512,640]{1,0:T(8,128)(2,1)S(1)} %pad_maximum_fusion.6), channel_id=1, source_target_pairs={{0,64},{1,65},{2,66},{3,67},{4,68},{5,69},{6,70},{7,71},{8,72},{9,... | collective-permute-start | bytes 1966088 | tf_op jit(solution)/shard_map/ppermute | solution.py:33
  6.2 0.4 collective-permute-start.1
  6.6 1.0 collective-permute-start
  7.7 2.6 %constant_dynamic-slice_fusion.15 = (bf16[288,512]{1,0:T(8,128)(2,1)S(1)}, bf16[288,512]{1,0:T(8,128)(2,1)S(1)}, bf16[288,512]{1,0:T(8,128)(2,1)S(1)}, bf16[288,...) fusion(bf16[288,8192]{1,0:T(8,128)(2,1)} %bitcast.150, ...), kind=kLoop, calls=%fused_computation.116 | loop fusion | bytes 9437248 | tf_op jit(solution)/shard_map/dynamic_slice | solution.py:125
  10.3 0.1 pad_maximum_fusion.1
  10.5 1.6 %collective-permute-start.3 = (bf16[288,2048]{1,0:T(8,128)(2,1)S(1)}, bf16[288,2048]{1,0:T(8,128)(2,1)S(1)}, u32[]{:S(2)}, u32[]{:S(2)}) collective-permute-start(bf16[288,2048]{1,0:T(8,128)(2,1)S(1)} %pad_maximum_fusion.1), channel_id=1, source_target_pairs={{0,8},{1,9},{2,10},{3,11},{4,12},{5,13},{6,14},{7,15},{8,0},{9,1},... | collective-permute-start | bytes 3538952 | tf_op jit(solution)/shard_map/ppermute | solution.py:33
  12.1 0.1 pad_maximum_fusion.2
  12.2 2.7 %collective-permute-start.4 = (bf16[288,2048]{1,0:T(8,128)(2,1)S(1)}, bf16[288,2048]{1,0:T(8,128)(2,1)S(1)}, u32[]{:S(2)}, u32[]{:S(2)}) collective-permute-start(bf16[288,2048]{1,0:T(8,128)(2,1)S(1)} %pad_maximum_fusion.2), channel_id=1, source_target_pairs={{0,28},{1,29},{2,30},{3,31},{4,24},{5,25},{6,26},{7,27},{8,20},{9,... | collective-permute-start | bytes 3538952 | tf_op jit(solution)/shard_map/ppermute | solution.py:33
  15.3 2.4 %multiply_cosine_fusion.1 = (f32[2,144,64]{2,0,1:T(2,128)S(1)}, f32[2,144,64]{2,0,1:T(2,128)S(1)}) fusion(f32[64]{0:T(128)S(1)} %multiply_power_fusion, f32[2,144]{0,1:T(8,128)S(1)} %add_convert_fusion.3), kind=kLoop, calls=%fused_computation.68 | loop fusion | flops 18432 | bytes 148864 | tf_op jit(solution)/shard_map/cos | solution.py:66
  17.8 0.1 pad_maximum_fusion.3
  18.0 2.7 %collective-permute-done.2 = bf16[512,640]{1,0:T(8,128)(2,1)S(1)} collective-permute-done((bf16[512,640]{1,0:T(8,128)(2,1)S(1)}, bf16[512,640]{1,0:T(8,128)(2,1)S(1)}, u32[]{:S(2)}, u32[]{:S(2)}) %collective-permute-start.2) | collective-permute-done | bytes 655392 | tf_op jit(solution)/shard_map/ppermute | solution.py:33
  20.7 1.3 %collective-permute-start.7 = (bf16[288,2048]{1,0:T(8,128)(2,1)S(1)}, bf16[288,2048]{1,0:T(8,128)(2,1)S(1)}, u32[]{:S(2)}, u32[]{:S(2)}) collective-permute-start(bf16[288,2048]{1,0:T(8,128)(2,1)S(1)} %pad_maximum_fusion.3), channel_id=1, source_target_pairs={{0,16},{1,17},{2,18},{3,19},{4,20},{5,21},{6,22},{7,23},{8,24},{9,... | collective-permute-start | bytes 3538952 | tf_op jit(solution)/shard_map/ppermute | solution.py:33
  22.0 13.2 %collective-permute-done.1 = bf16[512,640]{1,0:T(8,128)(2,1)S(1)} collective-permute-done((bf16[512,640]{1,0:T(8,128)(2,1)S(1)}, bf16[512,640]{1,0:T(8,128)(2,1)S(1)}, u32[]{:S(2)}, u32[]{:S(2)}) %collective-permute-start.1) | collective-permute-done | bytes 655392 | tf_op jit(solution)/shard_map/ppermute | solution.py:33
  35.2 0.2 collective-permute-done
  35.4 3.0 %collective-permute-start.11 = (bf16[512,640]{1,0:T(8,128)(2,1)S(1)}, bf16[512,640]{1,0:T(8,128)(2,1)S(1)}, u32[]{:S(2)}, u32[]{:S(2)}) collective-permute-start(bf16[512,640]{1,0:T(8,128)(2,1)S(1)} %slice.63), channel_id=1, source_target_pairs={{0,64},{1,65},{2,66},{3,67},{4,68},{5,69},{6,70},{7,71},{8,72},{9,... | collective-permute-start | bytes 1966088 | tf_op jit(solution)/shard_map/ppermute | solution.py:33
  38.4 0.4 collective-permute-start.10
  39.0 0.1 constant_dynamic-update-slice_fusion.2
  39.1 0.1 constant_dynamic-update-slice_fusion.1
  39.2 0.1 constant_dynamic-update-slice_fusion
  39.3 1.1 collective-permute-start.9
  40.4 1.1 fusion.14
  41.6 1.1 fusion.15
  42.8 1.3 %collective-permute-start.5 = (bf16[2,288,640]{2,1,0:T(8,128)(2,1)S(1)}, bf16[2,288,640]{2,1,0:T(8,128)(2,1)S(1)}, u32[]{:S(2)}, u32[]{:S(2)}) collective-permute-start(bf16[2,288,640]{2,1,0:T(8,128)(2,1)S(1)} %pad_maximum_fusion.4), channel_id=1, source_target_pairs={{0,8},{1,9},{2,10},{3,11},{4,12},{5,13},{6,14},{7,15},{8,0},{9,1},... | collective-permute-start | bytes 2211848 | tf_op jit(solution)/shard_map/ppermute | solution.py:33
  44.1 23.5 %collective-permute-done.9 = bf16[512,640]{1,0:T(8,128)(2,1)S(1)} collective-permute-done((bf16[512,640]{1,0:T(8,128)(2,1)S(1)}, bf16[512,640]{1,0:T(8,128)(2,1)S(1)}, u32[]{:S(2)}, u32[]{:S(2)}) %collective-permute-start.9) | collective-permute-done | bytes 655392 | tf_op jit(solution)/shard_map/ppermute | solution.py:33
  67.6 0.1 constant_dynamic-update-slice_fusion.6
  67.7 0.1 constant_dynamic-update-slice_fusion.5
  67.9 0.1 constant_dynamic-update-slice_fusion.4
  68.0 1.1 fusion.16
  69.1 1.1 fusion.17
  70.3 1.2 collective-permute-start.12
  71.5 0.1 convert_element_type.117
  71.6 1.1 fusion.13
  72.7 3.2 %collective-permute-start.6 = (bf16[288,640]{1,0:T(8,128)(2,1)S(1)}, bf16[288,640]{1,0:T(8,128)(2,1)S(1)}, u32[]{:S(2)}, u32[]{:S(2)}) collective-permute-start(bf16[288,640]{1,0:T(8,128)(2,1)S(1)} %fusion.13), channel_id=1, source_target_pairs={{0,4},{1,5},{2,6},{3,7},{4,0},{5,1},{6,2},{7,3},{8,12},{9,13},{10,... | collective-permute-start | bytes 1105928 | tf_op jit(solution)/shard_map/ppermute | solution.py:33
  75.9 1.1 fusion.10
  77.0 0.9 collective-permute-start.8
  77.9 0.1 convert_element_type.126
  78.0 1.1 fusion.12
  79.1 1.5 %collective-permute-start.13 = (bf16[288,640]{1,0:T(8,128)(2,1)S(1)}, bf16[288,640]{1,0:T(8,128)(2,1)S(1)}, u32[]{:S(2)}, u32[]{:S(2)}) collective-permute-start(bf16[288,640]{1,0:T(8,128)(2,1)S(1)} %fusion.12), channel_id=1, source_target_pairs={{0,4},{1,5},{2,6},{3,7},{4,0},{5,1},{6,2},{7,3},{8,12},{9,13},{10,... | collective-permute-start | bytes 1105928 | tf_op jit(solution)/shard_map/ppermute | solution.py:33
  80.6 1.1 fusion.11
  81.7 0.7 collective-permute-start.14
  82.4 2.3 %collective-permute-done.6 = bf16[288,640]{1,0:T(8,128)(2,1)S(1)} collective-permute-done((bf16[288,640]{1,0:T(8,128)(2,1)S(1)}, bf16[288,640]{1,0:T(8,128)(2,1)S(1)}, u32[]{:S(2)}, u32[]{:S(2)}) %collective-permute-start.6) | collective-permute-done | bytes 368672 | tf_op jit(solution)/shard_map/ppermute | solution.py:33
  84.7 16.1 %collective-permute-done.8 = bf16[288,640]{1,0:T(8,128)(2,1)S(1)} collective-permute-done((bf16[288,640]{1,0:T(8,128)(2,1)S(1)}, bf16[288,640]{1,0:T(8,128)(2,1)S(1)}, u32[]{:S(2)}, u32[]{:S(2)}) %collective-permute-start.8) | collective-permute-done | bytes 368672 | tf_op jit(solution)/shard_map/ppermute | solution.py:33
  100.8 0.1 add_convert_fusion.2
  101.0 0.1 copy.18
  101.1 0.9 gather_fusion.1
  102.0 0.1 copy.19
  102.2 2.7 %fusion.43 = (bf16[2,144,64]{2,0,1:T(2,128)(2,1)S(1)}, bf16[2,144,64]{2,0,1:T(2,128)(2,1)S(1)}) fusion(f32[2,144,1,128]{3,0,1,2:T(2,128)S(1)} %fusion.39, f32[64]{0:T(128)S(1)} %multiply_power_fusion, f32[2,144]{0,1:T(8,128)S(1)} %add_convert_fusion.3), kind=kLoop, calls=%fused_computation.90 | loop fusion | flops 165888 | bytes 222592 | tf_op jit(solution)/shard_map/concatenate | solution.py:70
  104.9 3.8 %collective-permute-done.14 = bf16[288,640]{1,0:T(8,128)(2,1)S(1)} collective-permute-done((bf16[288,640]{1,0:T(8,128)(2,1)S(1)}, bf16[288,640]{1,0:T(8,128)(2,1)S(1)}, u32[]{:S(2)}, u32[]{:S(2)}) %collective-permute-start.14) | collective-permute-done | bytes 368672 | tf_op jit(solution)/shard_map/ppermute | solution.py:33
  108.7 0.1 add_convert_fusion.1
  108.8 0.1 maximum_bitcast_fusion
  108.9 0.1 copy.31
  109.0 1.0 copy.15
  110.0 0.7 gather_fusion
  110.7 1.2 copy.16
  112.0 0.5 fusion.25
  112.5 5.4 %fusion.4 = (f32[2,144,8]{2,0,1:T(2,128)S(1)}, f32[144,2,8,256]{3,2,1,0:T(8,128)S(1)}) fusion(pred[144,256]{1,0:T(8,128)(4,1)S(1)} %iota_compare_fusion, bf16[2,144,1,256,128]{4,3,1,2,0:T(8,128)(2,1)} %bitcast.148, bf16[2,144,8,64]{3,2,0,1:T(8,128)(2,1)S(1)} %get-tuple-element.32, bf16[2,144,8,64]{3,2,0,1:T(8,128)(2,1)S(1)} %get-tuple-element.31), kind=kOutput, calls=%fused_computation.11 | convolution fusion | flops 153941760 | bytes 12432384 | tf_op jit(solution)/shard_map/srgqd,rgcd->srgqc/dot_general | solution.py:79
  117.9 2.9 %fusion.53 = (f32[2,144,8]{2,0,1:T(2,128)S(1)}, f32[2,144,1,8,2]{3,4,0,1,2:T(2,128)S(1)}) fusion(bf16[2,144,8,64]{3,2,0,1:T(8,128)(2,1)S(1)} %get-tuple-element.32, bf16[2,144,8,64]{3,2,0,1:T(8,128)(2,1)S(1)} %get-tuple-element.31, bf16[2,144,64]{2,0,1:T(2,128)(2,1)S(1)} %get-tuple-element.38, bf16[2,144,64]{2,0,1:T(2,128)(2,1)S(1)} %get-tuple-element.37, ...), kind=kOutput, calls=%fused_computation.133 | convolution fusion | flops 2518272 | bytes 691204 | tf_op jit(solution)/shard_map/srgqd,trgd->srgqt/dot_general | solution.py:83
  120.9 0.6 fusion.28
  121.4 1.3 %fusion.3 = f32[2,144,8]{2,0,1:T(2,128)S(1)} fusion(f32[144,2,8,256]{3,2,1,0:T(8,128)S(1)} %get-tuple-element.44, f32[2,144,8]{2,0,1:T(2,128)S(1)} %max.9, pred[144,256]{1,0:T(8,128)(4,1)S(1)} %iota_compare_fusion), kind=kLoop, calls=%fused_computation.10 | loop fusion | flops 2356992 | bytes 2414592 | tf_op jit(solution)/shard_map/reduce_sum | solution.py:97
  122.9 4.8 %fusion.5 = f32[144,128,2,8]{1,3,2,0:T(8,128)S(1)} fusion(bf16[2,144,1,256,128]{4,3,1,2,0:T(8,128)(2,1)} %bitcast.149, f32[144,2,8,256]{3,2,1,0:T(8,128)S(1)} %get-tuple-element.44, f32[2,144,8]{2,0,1:T(2,128)S(1)} %add.331, f32[2,144,8]{2,0,1:T(2,128)S(1)} %max.9, pred[144,256]{1,0:T(8,128)(4,1)S(1)} %iota_compare_fusion), kind=kOutput, calls=%fused_computation.13 | convolution fusion | flops 153944064 | bytes 13031424 | tf_op jit(solution)/shard_map/srgqc,rgcd->srgqd/dot_general | solution.py:102
  127.6 0.5 fusion.7
  128.2 0.1 reshape.275
  128.3 1.0 copy.22
  (44 shorter events, 1.2 us)
Async XLA Ops:
  0.0 1.6 %slice-start = ((bf16[512,1024]{1,0:T(8,128)(2,1)}), bf16[512,384]{1,0:T(8,128)(2,1)S(1)}, s32[]{:S(2)}) async-start(bf16[512,1024]{1,0:T(8,128)(2,1)} %param.9), calls=%async_computation | async-start | bytes 786432 | tf_op jit(solution)/shard_map/slice | solution.py:158
  1.7 19.0 %collective-permute-start.2 = (bf16[512,640]{1,0:T(8,128)(2,1)S(1)}, bf16[512,640]{1,0:T(8,128)(2,1)S(1)}, u32[]{:S(2)}, u32[]{:S(2)}) collective-permute-start(bf16[512,640]{1,0:T(8,128)(2,1)S(1)} %pad_maximum_fusion.6), channel_id=1, source_target_pairs={{0,64},{1,65},{2,66},{3,67},{4,68},{5,69},{6,70},{7,71},{8,72},{9,... | collective-permute-start | bytes 1966088 | tf_op jit(solution)/shard_map/ppermute | solution.py:33
  6.2 29.0 %collective-permute-start.1 = (bf16[512,640]{1,0:T(8,128)(2,1)S(1)}, bf16[512,640]{1,0:T(8,128)(2,1)S(1)}, u32[]{:S(2)}, u32[]{:S(2)}) collective-permute-start(bf16[512,640]{1,0:T(8,128)(2,1)S(1)} %pad_maximum_fusion.6), channel_id=1, source_target_pairs={{0,96},{1,97},{2,98},{3,99},{4,100},{5,101},{6,102},{7,103},{8,104... | collective-permute-start | bytes 1966088 | tf_op jit(solution)/shard_map/ppermute | solution.py:33
  6.6 28.8 %collective-permute-start = (bf16[512,640]{1,0:T(8,128)(2,1)S(1)}, bf16[512,640]{1,0:T(8,128)(2,1)S(1)}, u32[]{:S(2)}, u32[]{:S(2)}) collective-permute-start(bf16[512,640]{1,0:T(8,128)(2,1)S(1)} %pad_maximum_fusion.6), channel_id=1, source_target_pairs={{0,32},{1,33},{2,34},{3,35},{4,36},{5,37},{6,38},{7,39},{8,40},{9,... | collective-permute-start | bytes 1966088 | tf_op jit(solution)/shard_map/ppermute | solution.py:33
  10.3 4.7 %copy-start.1 = (bf16[1024]{0:T(1024)(128)(2,1)S(1)}, bf16[1024]{0:T(1024)(128)(2,1)}, u32[]{:S(2)}) copy-start(bf16[1024]{0:T(1024)(128)(2,1)} %param.11) | copy-start | bytes 6148
  10.3 4.7 %copy-start.2 = (s32[144]{0:T(256)S(1)}, s32[144]{0:T(256)}, u32[]{:S(2)}) copy-start(s32[144]{0:T(256)} %param.15) | copy-start | bytes 1732
  10.3 4.9 %copy-start = (bf16[512,1024]{1,0:T(8,128)(2,1)S(1)}, bf16[512,1024]{1,0:T(8,128)(2,1)}, u32[]{:S(2)}) copy-start(bf16[512,1024]{1,0:T(8,128)(2,1)} %param.9) | copy-start | bytes 3145732
  10.5 4.8 %copy-start.4 = (s32[128]{0:T(128)S(1)}, s32[128]{0:T(128)}, u32[]{:S(2)}) copy-start(s32[128]{0:T(128)} %param.13) | copy-start | bytes 1540
  10.5 4.8 %copy-start.3 = (bf16[2,128]{1,0:T(2,128)(2,1)S(1)}, bf16[2,128]{1,0:T(2,128)(2,1)}, u32[]{:S(2)}) copy-start(bf16[2,128]{1,0:T(2,128)(2,1)} %param.12) | copy-start | bytes 1540
  10.5 28.8 %collective-permute-start.3 = (bf16[288,2048]{1,0:T(8,128)(2,1)S(1)}, bf16[288,2048]{1,0:T(8,128)(2,1)S(1)}, u32[]{:S(2)}, u32[]{:S(2)}) collective-permute-start(bf16[288,2048]{1,0:T(8,128)(2,1)S(1)} %pad_maximum_fusion.1), channel_id=1, source_target_pairs={{0,8},{1,9},{2,10},{3,11},{4,12},{5,13},{6,14},{7,15},{8,0},{9,1},... | collective-permute-start | bytes 3538952 | tf_op jit(solution)/shard_map/ppermute | solution.py:33
  12.2 29.3 %collective-permute-start.4 = (bf16[288,2048]{1,0:T(8,128)(2,1)S(1)}, bf16[288,2048]{1,0:T(8,128)(2,1)S(1)}, u32[]{:S(2)}, u32[]{:S(2)}) collective-permute-start(bf16[288,2048]{1,0:T(8,128)(2,1)S(1)} %pad_maximum_fusion.2), channel_id=1, source_target_pairs={{0,28},{1,29},{2,30},{3,31},{4,24},{5,25},{6,26},{7,27},{8,20},{9,... | collective-permute-start | bytes 3538952 | tf_op jit(solution)/shard_map/ppermute | solution.py:33
  20.7 55.2 %collective-permute-start.7 = (bf16[288,2048]{1,0:T(8,128)(2,1)S(1)}, bf16[288,2048]{1,0:T(8,128)(2,1)S(1)}, u32[]{:S(2)}, u32[]{:S(2)}) collective-permute-start(bf16[288,2048]{1,0:T(8,128)(2,1)S(1)} %pad_maximum_fusion.3), channel_id=1, source_target_pairs={{0,16},{1,17},{2,18},{3,19},{4,20},{5,21},{6,22},{7,23},{8,24},{9,... | collective-permute-start | bytes 3538952 | tf_op jit(solution)/shard_map/ppermute | solution.py:33
  35.4 32.4 %collective-permute-start.11 = (bf16[512,640]{1,0:T(8,128)(2,1)S(1)}, bf16[512,640]{1,0:T(8,128)(2,1)S(1)}, u32[]{:S(2)}, u32[]{:S(2)}) collective-permute-start(bf16[512,640]{1,0:T(8,128)(2,1)S(1)} %slice.63), channel_id=1, source_target_pairs={{0,64},{1,65},{2,66},{3,67},{4,68},{5,69},{6,70},{7,71},{8,72},{9,... | collective-permute-start | bytes 1966088 | tf_op jit(solution)/shard_map/ppermute | solution.py:33
  38.4 29.3 %collective-permute-start.10 = (bf16[512,640]{1,0:T(8,128)(2,1)S(1)}, bf16[512,640]{1,0:T(8,128)(2,1)S(1)}, u32[]{:S(2)}, u32[]{:S(2)}) collective-permute-start(bf16[512,640]{1,0:T(8,128)(2,1)S(1)} %slice.63), channel_id=1, source_target_pairs={{0,96},{1,97},{2,98},{3,99},{4,100},{5,101},{6,102},{7,103},{8,104... | collective-permute-start | bytes 1966088 | tf_op jit(solution)/shard_map/ppermute | solution.py:33
  39.3 28.3 %collective-permute-start.9 = (bf16[512,640]{1,0:T(8,128)(2,1)S(1)}, bf16[512,640]{1,0:T(8,128)(2,1)S(1)}, u32[]{:S(2)}, u32[]{:S(2)}) collective-permute-start(bf16[512,640]{1,0:T(8,128)(2,1)S(1)} %slice.63), channel_id=1, source_target_pairs={{0,32},{1,33},{2,34},{3,35},{4,36},{5,37},{6,38},{7,39},{8,40},{9,... | collective-permute-start | bytes 1966088 | tf_op jit(solution)/shard_map/ppermute | solution.py:33
  42.8 28.7 %collective-permute-start.5 = (bf16[2,288,640]{2,1,0:T(8,128)(2,1)S(1)}, bf16[2,288,640]{2,1,0:T(8,128)(2,1)S(1)}, u32[]{:S(2)}, u32[]{:S(2)}) collective-permute-start(bf16[2,288,640]{2,1,0:T(8,128)(2,1)S(1)} %pad_maximum_fusion.4), channel_id=1, source_target_pairs={{0,8},{1,9},{2,10},{3,11},{4,12},{5,13},{6,14},{7,15},{8,0},{9,1},... | collective-permute-start | bytes 2211848 | tf_op jit(solution)/shard_map/ppermute | solution.py:33
  70.3 7.6 %collective-permute-start.12 = (bf16[2,288,640]{2,1,0:T(8,128)(2,1)S(1)}, bf16[2,288,640]{2,1,0:T(8,128)(2,1)S(1)}, u32[]{:S(2)}, u32[]{:S(2)}) collective-permute-start(bf16[2,288,640]{2,1,0:T(8,128)(2,1)S(1)} %pad_maximum_fusion.5), channel_id=1, source_target_pairs={{0,8},{1,9},{2,10},{3,11},{4,12},{5,13},{6,14},{7,15},{8,0},{9,1},... | collective-permute-start | bytes 2211848 | tf_op jit(solution)/shard_map/ppermute | solution.py:33
  72.7 12.0 %collective-permute-start.6 = (bf16[288,640]{1,0:T(8,128)(2,1)S(1)}, bf16[288,640]{1,0:T(8,128)(2,1)S(1)}, u32[]{:S(2)}, u32[]{:S(2)}) collective-permute-start(bf16[288,640]{1,0:T(8,128)(2,1)S(1)} %fusion.13), channel_id=1, source_target_pairs={{0,4},{1,5},{2,6},{3,7},{4,0},{5,1},{6,2},{7,3},{8,12},{9,13},{10,... | collective-permute-start | bytes 1105928 | tf_op jit(solution)/shard_map/ppermute | solution.py:33
  77.0 23.8 %collective-permute-start.8 = (bf16[288,640]{1,0:T(8,128)(2,1)S(1)}, bf16[288,640]{1,0:T(8,128)(2,1)S(1)}, u32[]{:S(2)}, u32[]{:S(2)}) collective-permute-start(bf16[288,640]{1,0:T(8,128)(2,1)S(1)} %fusion.10), channel_id=1, source_target_pairs={{0,20},{1,21},{2,22},{3,23},{4,16},{5,17},{6,18},{7,19},{8,28},{9,... | collective-permute-start | bytes 1105928 | tf_op jit(solution)/shard_map/ppermute | solution.py:33
  79.1 25.8 %collective-permute-start.13 = (bf16[288,640]{1,0:T(8,128)(2,1)S(1)}, bf16[288,640]{1,0:T(8,128)(2,1)S(1)}, u32[]{:S(2)}, u32[]{:S(2)}) collective-permute-start(bf16[288,640]{1,0:T(8,128)(2,1)S(1)} %fusion.12), channel_id=1, source_target_pairs={{0,4},{1,5},{2,6},{3,7},{4,0},{5,1},{6,2},{7,3},{8,12},{9,13},{10,... | collective-permute-start | bytes 1105928 | tf_op jit(solution)/shard_map/ppermute | solution.py:33
  81.7 27.0 %collective-permute-start.14 = (bf16[288,640]{1,0:T(8,128)(2,1)S(1)}, bf16[288,640]{1,0:T(8,128)(2,1)S(1)}, u32[]{:S(2)}, u32[]{:S(2)}) collective-permute-start(bf16[288,640]{1,0:T(8,128)(2,1)S(1)} %fusion.11), channel_id=1, source_target_pairs={{0,20},{1,21},{2,22},{3,23},{4,16},{5,17},{6,18},{7,19},{8,28},{9,... | collective-permute-start | bytes 1105928 | tf_op jit(solution)/shard_map/ppermute | solution.py:33

commit v2 on v1

--- a/solution.py
+++ b/solution.py
@@ -108,8 +108,13 @@
     return result.astype(jnp.bfloat16)
 
 
-def gathered_over_z(block):
-    return [block, moved(block, z_by(1)), moved(block, z_by(-1)), moved(block, z_by(2))]
+def near_over_z(block):
+    return moved(block, z_by(1)), moved(block, z_by(-1))
+
+
+def far_over_z(lower, upper):
+    half = lower.shape[0] // 2
+    return moved(lower[:half], z_by(1)), moved(upper[half:], z_by(-1))
 
 
 def row_sets(tokens):
@@ -133,20 +138,12 @@
     }
 
 
-def returned(rows, blocks, bias):
+def core_sums(rows, blocks, dy):
     weights = jnp.concatenate(blocks, axis=0)
-    sums = {
-        key: jnp.dot(value, weights, preferred_element_type=jnp.float32)
-        for key, value in rows.items()
-    }
-    partner = moved(
-        jnp.stack([sums[0, 1].astype(jnp.bfloat16), sums[1, 1].astype(jnp.bfloat16)]), other_core
-    ).astype(jnp.float32)
-    same = sums[0, 0] + partner[0] + bias.astype(jnp.float32)
-    other = sums[1, 0] + partner[1]
-    same = moved(same.astype(jnp.bfloat16), far_y)
-    other = moved(other.astype(jnp.bfloat16), cross_y)
-    return (same.astype(jnp.float32) + other.astype(jnp.float32)).astype(jnp.bfloat16)
+    theirs = jnp.dot(rows[dy, 1], weights, preferred_element_type=jnp.float32)
+    theirs = moved(theirs.astype(jnp.bfloat16), other_core)
+    ours = jnp.dot(rows[dy, 0], weights, preferred_element_type=jnp.float32)
+    return ours + theirs.astype(jnp.float32)
 
 
 def body(tokens, w_query, w_keyval, b_query, b_keyval, rotary_perm, cache, lengths):
@@ -159,11 +156,27 @@
     second = w_query[:, early:]
     first_bias = jnp.concatenate([b_keyval[0], b_keyval[1], b_query[:early]])
     rows = row_sets(tokens)
-    first_blocks = gathered_over_z(first)
-    second, first_blocks = lax.optimization_barrier((second, first_blocks))
-    second_blocks = gathered_over_z(second)
-    first_sums = returned(rows, first_blocks, first_bias)
-    second_sums = returned(rows, second_blocks, b_query[early:])
+    depth = first.shape[0]
+    pad = jnp.broadcast_to(b_query[None, early:], (16, b_query.shape[0] - early))
+    shifted = moved(jnp.concatenate([second, pad], axis=0), far_y)
+    first_near = near_over_z(first)
+    shifted, first_near = lax.optimization_barrier((shifted, first_near))
+    second, second_bias = shifted[:depth], shifted[depth]
+    below, above = first_near
+    up = moved(jnp.concatenate([below[: depth // 2], second], axis=0), z_by(1))
+    down = moved(jnp.concatenate([above[depth // 2 :], second], axis=0), z_by(-1))
+    up, down = lax.optimization_barrier((up, down))
+    first_blocks = [first, below, above, up[: depth // 2], down[: depth // 2]]
+    below, above = up[depth // 2 :], down[depth // 2 :]
+    second_blocks = [second, below, above, *far_over_z(below, above)]
+
+    other = moved(core_sums(rows, first_blocks, 1).astype(jnp.bfloat16), cross_y)
+    same = core_sums(rows, first_blocks, 0) + first_bias.astype(jnp.float32)
+    same = moved(same.astype(jnp.bfloat16), far_y)
+    first_sums = same.astype(jnp.float32) + other.astype(jnp.float32)
+    other = moved(core_sums(rows, second_blocks, 1).astype(jnp.bfloat16), inner_y)
+    same = core_sums(rows, second_blocks, 0) + second_bias.astype(jnp.float32)
+    second_sums = same + other.astype(jnp.float32)
 
     queries = jnp.concatenate([first_sums[:, 2 * head_size :], second_sums], axis=1)
     queries = queries.reshape(step_count, row_count, 1, per_group, head_size)
@@ -171,14 +184,14 @@
     key_part = first_sums[:, :head_size].reshape(step_count, row_count, 1, head_size)
     key_part = jnp.take(key_part, rotary_perm, axis=3)
     value_part = first_sums[:, head_size : 2 * head_size]
-    value_part = value_part.reshape(step_count, row_count, 1, head_size)
+    value_part = value_part.reshape(step_count, row_count, 1, head_size).astype(jnp.bfloat16)
     positions = (lengths[None, :] + jnp.arange(step_count, dtype=jnp.int32)[:, None]).astype(
         jnp.float32
     )
-    query_rot = rotate(queries.astype(jnp.float32), positions[:, :, None, None, None]).astype(
+    query_rot = rotate(queries, positions[:, :, None, None, None]).astype(
         jnp.bfloat16
     )
-    key_rot = rotate(key_part.astype(jnp.float32), positions[:, :, None, None]).astype(jnp.bfloat16)
+    key_rot = rotate(key_part, positions[:, :, None, None]).astype(jnp.bfloat16)
     result = attend(query_rot, key_rot, value_part, cache, lengths)
     return result.reshape(step_count, row_count, per_group * head_size)
 

time: 129 us -> 116 us (0.90)
  waiting for transfers between devices: 62 us -> 35.9 us
  starting transfers between devices: 24.9 us -> 28.6 us
  local copies, waits for them, and re-layouts: 10.2 us -> 13.7 us
  matrix products: 22.5 us -> 25.9 us
  other arithmetic: 9.18 us -> 11.1 us
    ppermute x15 -> x17, waiting for transfers between devices: 62 us -> 35.9 us  [moved(): return lax.ppermute(value, AXES, pairs)]
    ppermute x15 -> x17, starting transfers between devices: 24.9 us -> 28.6 us  [moved(): return lax.ppermute(value, AXES, pairs)]
    dot_general x8, matrix products: 8.93 us -> 12.3 us  [the longest x4 7.08 us: core_sums(): ours = jnp.dot(rows[dy, 0], weights, preferred_element_type=jnp.float32)]
    gather x2, local copies, waits for them, and re-layouts: 1.84 us -> 4.27 us  [body(): queries = jnp.take(queries, rotary_perm, axis=4)]
  transfers between devices with their start and end apart: 15 -> 17, of which waited for: 8 -> 5; matrix products, arithmetic and copies ran while one was open for 15% -> 19% of each run, Pallas kernels for 0% -> 0%
where the time goes in v2:
time: 116 us
  waiting for transfers between devices  35.9 us (31%)
  starting transfers between devices  28.6 us (25%)
  matrix products  25.9 us (22%)
  local copies, waits for them, and re-layouts  13.7 us (12%)
  other arithmetic  11.1 us (10%)
    ppermute x17, waiting for transfers between devices, moved(): return lax.ppermute(value, AXES, pairs)  35.9 us
    ppermute x17, starting transfers between devices, moved(): return lax.ppermute(value, AXES, pairs)  28.6 us
    dot_general x4, matrix products, core_sums(): ours = jnp.dot(rows[dy, 0], weights, preferred_element_type=jnp.float32)  7.08 us
    dot_general x1, matrix products, attend(): jnp.einsum('srgqd,rgcd->srgqc', queries, cache[0], preferred_element_type...  5.4 us
    dot_general x4, matrix products, core_sums(): theirs = jnp.dot(rows[dy, 1], weights, preferred_element_type=jnp.float32)  5.22 us
    dot_general x1, matrix products, attend(): jnp.einsum('srgqc,rgcd->srgqd', cached_weights, cache[1], preferred_eleme...  4.78 us
    gather x2, local copies, waits for them, and re-layouts, body(): queries = jnp.take(queries, rotary_perm, axis=4)  4.27 us
    concatenate x2, other arithmetic, rotate(): jnp.concatenate([first_half * cos_part - second * sin_part, second * cos_...  3.84 us
  transfers between devices with their start and end apart: 17, of which 5 were waited for; matrix products, arithmetic and copies ran while one was open for 19% of the time, Pallas kernels for 0%

profile of v2, /device:TPU:1, one launch (start us, length us, event | category | flops | bytes accessed | tf_op | source)
XLA Modules:
  0.0 116.0 jit_solution(4276988125217265470)
XLA Ops:
  0.0 1.6 %fusion.45 = (bf16[512,1,128]{2,1,0:T(2,128)(2,1)S(1)}, bf16[512,1,128]{2,1,0:T(2,128)(2,1)S(1)}) fusion(bf16[512,2,128]{2,1,0:T(2,128)(2,1)} %param.10), kind=kLoop, calls=%fused_computation.124 | loop fusion | bytes 524288 | tf_op jit(solution)/shard_map/slice | solution.py:155
  1.6 1.0 constant_dynamic-update-slice_fusion.2
  2.6 2.5 %collective-permute-start.1 = (bf16[512,640]{1,0:T(8,128)(2,1)S(1)}, bf16[512,640]{1,0:T(8,128)(2,1)S(1)}, u32[]{:S(2)}, u32[]{:S(2)}) collective-permute-start(bf16[512,640]{1,0:T(8,128)(2,1)S(1)} %get-tuple-element.40), channel_id=1, source_target_pairs={{0,32},{1,33},{2,34},{3,35},{4,36},{5,37},{6,38},{7,39},{8,40},{9,... | collective-permute-start | bytes 1966088 | tf_op jit(solution)/shard_map/ppermute | solution.py:33
  5.1 2.1 %collective-permute-start.2 = (bf16[512,640]{1,0:T(8,128)(2,1)S(1)}, bf16[512,640]{1,0:T(8,128)(2,1)S(1)}, u32[]{:S(2)}, u32[]{:S(2)}) collective-permute-start(bf16[512,640]{1,0:T(8,128)(2,1)S(1)} %get-tuple-element.40), channel_id=1, source_target_pairs={{0,96},{1,97},{2,98},{3,99},{4,100},{5,101},{6,102},{7,103},{8,104... | collective-permute-start | bytes 1966088 | tf_op jit(solution)/shard_map/ppermute | solution.py:33
  7.3 3.0 %collective-permute-start = (bf16[528,640]{1,0:T(8,128)(2,1)S(1)}, bf16[528,640]{1,0:T(8,128)(2,1)S(1)}, u32[]{:S(2)}, u32[]{:S(2)}) collective-permute-start(bf16[528,640]{1,0:T(8,128)(2,1)S(1)} %pad_maximum_fusion.6), channel_id=1, source_target_pairs={{0,4},{1,5},{2,6},{3,7},{4,0},{5,1},{6,2},{7,3},{8,12},{9,13},{10,... | collective-permute-start | bytes 2027528 | tf_op jit(solution)/shard_map/ppermute | solution.py:33
  10.3 2.6 %constant_dynamic-slice_fusion.15 = (bf16[288,512]{1,0:T(8,128)(2,1)S(1)}, bf16[288,512]{1,0:T(8,128)(2,1)S(1)}, bf16[288,512]{1,0:T(8,128)(2,1)S(1)}, bf16[288,...) fusion(bf16[288,8192]{1,0:T(8,128)(2,1)} %bitcast.125, ...), kind=kLoop, calls=%fused_computation.108 | loop fusion | bytes 9437248 | tf_op jit(solution)/shard_map/dynamic_slice | solution.py:130
  13.0 0.1 pad_maximum_fusion.1
  13.2 1.3 %collective-permute-start.5 = (bf16[288,2048]{1,0:T(8,128)(2,1)S(1)}, bf16[288,2048]{1,0:T(8,128)(2,1)S(1)}, u32[]{:S(2)}, u32[]{:S(2)}) collective-permute-start(bf16[288,2048]{1,0:T(8,128)(2,1)S(1)} %pad_maximum_fusion.1), channel_id=1, source_target_pairs={{0,8},{1,9},{2,10},{3,11},{4,12},{5,13},{6,14},{7,15},{8,0},{9,1},... | collective-permute-start | bytes 3538952 | tf_op jit(solution)/shard_map/ppermute | solution.py:33
  14.5 0.1 pad_maximum_fusion.2
  14.6 0.5 collective-permute-start.8
  15.2 0.1 iota_compare_fusion
  15.3 0.1 pad_maximum_fusion.3
  15.4 6.2 %collective-permute-done.1 = bf16[512,640]{1,0:T(8,128)(2,1)S(1)} collective-permute-done((bf16[512,640]{1,0:T(8,128)(2,1)S(1)}, bf16[512,640]{1,0:T(8,128)(2,1)S(1)}, u32[]{:S(2)}, u32[]{:S(2)}) %collective-permute-start.1) | collective-permute-done | bytes 655392 | tf_op jit(solution)/shard_map/ppermute | solution.py:33
  21.7 3.8 %collective-permute-start.9 = (bf16[288,2048]{1,0:T(8,128)(2,1)S(1)}, bf16[288,2048]{1,0:T(8,128)(2,1)S(1)}, u32[]{:S(2)}, u32[]{:S(2)}) collective-permute-start(bf16[288,2048]{1,0:T(8,128)(2,1)S(1)} %pad_maximum_fusion.3), channel_id=1, source_target_pairs={{0,28},{1,29},{2,30},{3,31},{4,24},{5,25},{6,26},{7,27},{8,20},{9,... | collective-permute-start | bytes 3538952 | tf_op jit(solution)/shard_map/ppermute | solution.py:33
  25.6 0.1 fusion.44
  25.7 0.2 pad_maximum_fusion.4
  25.9 1.5 %collective-permute-start.4 = (bf16[768,640]{1,0:T(8,128)(2,1)S(1)}, bf16[768,640]{1,0:T(8,128)(2,1)S(1)}, u32[]{:S(2)}, u32[]{:S(2)}) collective-permute-start(bf16[768,640]{1,0:T(8,128)(2,1)S(1)} %get-tuple-element.41), channel_id=1, source_target_pairs={{0,96},{1,97},{2,98},{3,99},{4,100},{5,101},{6,102},{7,103},{8,104... | collective-permute-start | bytes 2949128 | tf_op jit(solution)/shard_map/ppermute | solution.py:33
  27.4 0.1 add_convert_fusion.2
  27.5 3.1 %multiply_cosine_fusion.1 = (f32[2,144,64]{2,0,1:T(2,128)S(1)}, f32[2,144,64]{2,0,1:T(2,128)}) fusion(f32[64]{0:T(128)S(1)} %multiply_power_fusion, f32[2,144]{0,1:T(8,128)S(1)} %add_convert_fusion.2), kind=kLoop, calls=%fused_computation.62 | loop fusion | flops 18432 | bytes 148864 | tf_op jit(solution)/shard_map/cos | solution.py:66
  30.6 0.1 constant_dynamic-update-slice_fusion.1
  30.7 0.1 constant_dynamic-update-slice_fusion
  30.8 16.0 %collective-permute-done.4 = bf16[768,640]{1,0:T(8,128)(2,1)S(1)} collective-permute-done((bf16[768,640]{1,0:T(8,128)(2,1)S(1)}, bf16[768,640]{1,0:T(8,128)(2,1)S(1)}, u32[]{:S(2)}, u32[]{:S(2)}) %collective-permute-start.4) | collective-permute-done | bytes 983072 | tf_op jit(solution)/shard_map/ppermute | solution.py:33
  46.8 2.1 %collective-permute-done.3 = bf16[768,640]{1,0:T(8,128)(2,1)S(1)} collective-permute-done((bf16[768,640]{1,0:T(8,128)(2,1)S(1)}, bf16[768,640]{1,0:T(8,128)(2,1)S(1)}, u32[]{:S(2)}, u32[]{:S(2)}) %collective-permute-start.3) | collective-permute-done | bytes 983072 | tf_op jit(solution)/shard_map/ppermute | solution.py:33
  49.0 0.4 collective-permute-start.13
  49.4 1.2 %collective-permute-start.12 = (bf16[256,640]{1,0:T(8,128)(2,1)S(1)}, bf16[256,640]{1,0:T(8,128)(2,1)S(1)}, u32[]{:S(2)}, u32[]{:S(2)}) collective-permute-start(bf16[256,640]{1,0:T(8,128)(2,1)S(1)} %get-tuple-element.36), channel_id=1, source_target_pairs={{0,32},{1,33},{2,34},{3,35},{4,36},{5,37},{6,38},{7,39},{8,40},{9,... | collective-permute-start | bytes 983048 | tf_op jit(solution)/shard_map/ppermute | solution.py:33
  50.6 1.1 convolution_convert_fusion.3
  51.7 4.6 %collective-permute-start.6 = (bf16[288,640]{1,0:T(8,128)(2,1)S(1)}, bf16[288,640]{1,0:T(8,128)(2,1)S(1)}, u32[]{:S(2)}, u32[]{:S(2)}) collective-permute-start(bf16[288,640]{1,0:T(8,128)(2,1)S(1)} %convolution_convert_fusion.3), channel_id=1, source_target_pairs={{0,8},{1,9},{2,10},{3,11},{4,12},{5,13},{6,14},{7,15},{8,0},{9,1},... | collective-permute-start | bytes 1105928 | tf_op jit(solution)/shard_map/ppermute | solution.py:33
  56.3 0.1 slice_dynamic-update-slice_fusion.1
  56.4 1.1 convolution_convert_fusion.2
  57.5 0.1 collective-permute-start.10
  57.6 0.1 slice_dynamic-update-slice_fusion
  57.8 1.1 convolution_convert_fusion
  58.9 4.0 %collective-permute-start.15 = (bf16[288,640]{1,0:T(8,128)(2,1)S(1)}, bf16[288,640]{1,0:T(8,128)(2,1)S(1)}, u32[]{:S(2)}, u32[]{:S(2)}) collective-permute-start(bf16[288,640]{1,0:T(8,128)(2,1)S(1)} %convolution_convert_fusion), channel_id=1, source_target_pairs={{0,8},{1,9},{2,10},{3,11},{4,12},{5,13},{6,14},{7,15},{8,0},{9,1},... | collective-permute-start | bytes 1105928 | tf_op jit(solution)/shard_map/ppermute | solution.py:33
  62.9 1.1 add_convert_fusion.1
  64.1 2.2 %collective-permute-start.7 = (bf16[288,640]{1,0:T(8,128)(2,1)S(1)}, bf16[288,640]{1,0:T(8,128)(2,1)S(1)}, u32[]{:S(2)}, u32[]{:S(2)}) collective-permute-start(bf16[288,640]{1,0:T(8,128)(2,1)S(1)} %add_convert_fusion.1), channel_id=1, source_target_pairs={{0,4},{1,5},{2,6},{3,7},{4,0},{5,1},{6,2},{7,3},{8,12},{9,13},{10,... | collective-permute-start | bytes 1105928 | tf_op jit(solution)/shard_map/ppermute | solution.py:33
  66.3 1.1 fusion.10
  67.4 0.9 collective-permute-start.11
  68.2 1.9 %convolution_convert_fusion.1 = bf16[288,640]{1,0:T(8,128)(2,1)} fusion(bf16[288,2048]{1,0:T(8,128)(2,1)S(1)} %collective-permute-done.5, bf16[2048,640]{1,0:T(8,128)(2,1)S(1)} %constant_dynamic-update-slice_fusion.3), kind=kOutput, calls=%fused_computation.24 | convolution fusion | flops 755159040 | bytes 4169728 | tf_op jit(solution)/shard_map/dot_general | solution.py:143
  70.1 0.6 collective-permute-start.14
  70.7 1.9 %fusion.11 = bf16[288,640]{1,0:T(8,128)(2,1)} fusion(bf16[288,2048]{1,0:T(8,128)(2,1)S(1)} %collective-permute-done.8, bf16[2048,640]{1,0:T(8,128)(2,1)S(1)} %constant_dynamic-update-slice_fusion.3, bf16[288,640]{1,0:T(8,128)(2,1)S(1)} %collective-permute-done.15), kind=kOutput, calls=%fused_computation.22 | convolution fusion | flops 755527680 | bytes 4538368 | tf_op jit(solution)/shard_map/dot_general | solution.py:145
  72.6 0.1 collective-permute-start.16
  72.7 3.4 %collective-permute-done.7 = bf16[288,640]{1,0:T(8,128)(2,1)S(1)} collective-permute-done((bf16[288,640]{1,0:T(8,128)(2,1)S(1)}, bf16[288,640]{1,0:T(8,128)(2,1)S(1)}, u32[]{:S(2)}, u32[]{:S(2)}) %collective-permute-start.7) | collective-permute-done | bytes 368672 | tf_op jit(solution)/shard_map/ppermute | solution.py:33
  76.0 8.2 %collective-permute-done.11 = bf16[288,640]{1,0:T(8,128)(2,1)S(1)} collective-permute-done((bf16[288,640]{1,0:T(8,128)(2,1)S(1)}, bf16[288,640]{1,0:T(8,128)(2,1)S(1)}, u32[]{:S(2)}, u32[]{:S(2)}) %collective-permute-start.11) | collective-permute-done | bytes 368672 | tf_op jit(solution)/shard_map/ppermute | solution.py:33
  84.3 0.1 convert_add_fusion
  84.3 0.6 slice.163
  85.0 0.1 copy.18
  85.2 0.9 gather_fusion.1
  86.1 0.2 copy.19
  86.3 3.3 %fusion.36 = (bf16[2,144,64]{2,0,1:T(2,128)(2,1)}, bf16[2,144,64]{2,0,1:T(2,128)(2,1)}) fusion(f32[2,144,1,128]{3,0,1,2:T(2,128)S(1)} %bitcast_select_fusion.2, f32[64]{0:T(128)S(1)} %multiply_power_fusion, f32[2,144]{0,1:T(8,128)S(1)} %add_convert_fusion.2), kind=kLoop, calls=%fused_computation.84 | loop fusion | flops 165888 | bytes 222592 | tf_op jit(solution)/shard_map/concatenate | solution.py:70
  89.6 3.0 %fusion.9 = f32[288,640]{1,0:T(8,128)S(1)} fusion(bf16[2048,640]{1,0:T(8,128)(2,1)} %copy-done.10, bf16[288,640]{1,0:T(8,128)(2,1)} %collective-permute-done.16, bf16[288,640]{1,0:T(8,128)(2,1)} %collective-permute-done.14, f32[640]{0:T(1024)S(1)} %convert_reduce_fusion, bf16[288,512]{1,0:T(8,128)(2,1)S(1)} %copy-done.4, ...), kind=kOutput, calls=%fused_computation.20 | convolution fusion | flops 760614912 | bytes 5278208 | tf_op jit(solution)/shard_map/dot_general | solution.py:145
  92.6 0.1 maximum_bitcast_fusion
  92.8 0.2 copy.31
  93.0 1.1 copy.15
  94.2 2.0 %gather_fusion = f32[128,2,144,8]{2,3,1,0:T(8,128)} fusion(f32[2,144,8,128]{1,2,3,0:T(8,128)S(1)} %copy.15, s32[1024]{0:T(1024)S(1)} %pad_clamp_fusion), kind=kCustom, calls=%fused_computation | custom fusion | bytes 2359808 | tf_op jit(solution)/shard_map/jit(_take)/gather | solution.py:183
  96.2 2.2 %copy.16 = f32[128,2,144,8]{0,3,1,2:T(8,128)S(1)} copy(f32[128,2,144,8]{2,3,1,0:T(8,128)} %gather_fusion) | data formatting | bytes 2359296 | tf_op jit(solution)/shard_map/jit(_take)/gather | solution.py:183
  98.5 0.5 fusion.19
  99.1 5.4 %fusion.4 = (f32[2,144,8]{2,0,1:T(2,128)S(1)}, f32[144,2,8,256]{3,2,1,0:T(8,128)S(1)}) fusion(pred[144,256]{1,0:T(8,128)(4,1)S(1)} %iota_compare_fusion, bf16[2,144,1,256,128]{4,3,1,2,0:T(8,128)(2,1)} %bitcast.123, bf16[2,144,8,64]{3,2,0,1:T(8,128)(2,1)S(1)} %get-tuple-element.32, bf16[2,144,8,64]{3,2,0,1:T(8,128)(2,1)S(1)} %get-tuple-element.31), kind=kOutput, calls=%fused_computation.11 | convolution fusion | flops 153941760 | bytes 12432384 | tf_op jit(solution)/shard_map/srgqd,rgcd->srgqc/dot_general | solution.py:79
  104.5 2.9 %fusion.46 = (f32[2,144,8]{2,0,1:T(2,128)S(1)}, f32[2,144,1,8,2]{3,4,0,1,2:T(2,128)S(1)}) fusion(bf16[2,144,8,64]{3,2,0,1:T(8,128)(2,1)S(1)} %get-tuple-element.32, bf16[2,144,8,64]{3,2,0,1:T(8,128)(2,1)S(1)} %get-tuple-element.31, bf16[2,144,64]{2,0,1:T(2,128)(2,1)S(1)} %copy-done.12, bf16[2,144,64]{2,0,1:T(2,128)(2,1)S(1)} %copy-done.11, ...), kind=kOutput, calls=%fused_computation.125 | convolution fusion | flops 2518272 | bytes 691204 | tf_op jit(solution)/shard_map/srgqd,trgd->srgqt/dot_general | solution.py:83
  107.5 0.6 fusion.22
  108.1 1.3 %fusion.3 = f32[2,144,8]{2,0,1:T(2,128)S(1)} fusion(f32[144,2,8,256]{3,2,1,0:T(8,128)S(1)} %get-tuple-element.52, f32[2,144,8]{2,0,1:T(2,128)S(1)} %max.9, pred[144,256]{1,0:T(8,128)(4,1)S(1)} %iota_compare_fusion), kind=kLoop, calls=%fused_computation.10 | loop fusion | flops 2356992 | bytes 2414592 | tf_op jit(solution)/shard_map/reduce_sum | solution.py:97
  109.5 4.8 %fusion.5 = f32[144,128,2,8]{1,3,2,0:T(8,128)S(1)} fusion(bf16[2,144,1,256,128]{4,3,1,2,0:T(8,128)(2,1)} %bitcast.124, f32[144,2,8,256]{3,2,1,0:T(8,128)S(1)} %get-tuple-element.52, f32[2,144,8]{2,0,1:T(2,128)S(1)} %add.338, f32[2,144,8]{2,0,1:T(2,128)S(1)} %max.9, pred[144,256]{1,0:T(8,128)(4,1)S(1)} %iota_compare_fusion), kind=kOutput, calls=%fused_computation.13 | convolution fusion | flops 153944064 | bytes 13031424 | tf_op jit(solution)/shard_map/srgqc,rgcd->srgqd/dot_general | solution.py:102
  114.3 0.5 fusion.7
  114.9 0.1 reshape.268
  115.0 1.0 copy.22
  (78 shorter events, 0.9 us)
Async XLA Ops:
  0.0 1.6 %slice-start = ((bf16[512,1024]{1,0:T(8,128)(2,1)}), bf16[512,384]{1,0:T(8,128)(2,1)S(1)}, s32[]{:S(2)}) async-start(bf16[512,1024]{1,0:T(8,128)(2,1)} %param.9), calls=%async_computation | async-start | bytes 786432 | tf_op jit(solution)/shard_map/slice | solution.py:155
  0.0 7.2 %copy-start.14 = (bf16[1024]{0:T(1024)(128)(2,1)S(1)}, bf16[1024]{0:T(1024)(128)(2,1)}, u32[]{:S(2)}) copy-start(bf16[1024]{0:T(1024)(128)(2,1)} %param.11) | copy-start | bytes 6148
  0.0 7.2 %slice-start.1 = ((bf16[512,1024]{1,0:T(8,128)(2,1)}), bf16[512,640]{1,0:T(8,128)(2,1)S(1)}, s32[]{:S(2)}) async-start(bf16[512,1024]{1,0:T(8,128)(2,1)} %param.9), calls=%async_computation.1 | async-start | bytes 1310720 | tf_op jit(solution)/shard_map/slice | solution.py:156
  2.6 19.0 %collective-permute-start.1 = (bf16[512,640]{1,0:T(8,128)(2,1)S(1)}, bf16[512,640]{1,0:T(8,128)(2,1)S(1)}, u32[]{:S(2)}, u32[]{:S(2)}) collective-permute-start(bf16[512,640]{1,0:T(8,128)(2,1)S(1)} %get-tuple-element.40), channel_id=1, source_target_pairs={{0,32},{1,33},{2,34},{3,35},{4,36},{5,37},{6,38},{7,39},{8,40},{9,... | collective-permute-start | bytes 1966088 | tf_op jit(solution)/shard_map/ppermute | solution.py:33
  5.1 20.4 %collective-permute-start.2 = (bf16[512,640]{1,0:T(8,128)(2,1)S(1)}, bf16[512,640]{1,0:T(8,128)(2,1)S(1)}, u32[]{:S(2)}, u32[]{:S(2)}) collective-permute-start(bf16[512,640]{1,0:T(8,128)(2,1)S(1)} %get-tuple-element.40), channel_id=1, source_target_pairs={{0,96},{1,97},{2,98},{3,99},{4,100},{5,101},{6,102},{7,103},{8,104... | collective-permute-start | bytes 1966088 | tf_op jit(solution)/shard_map/ppermute | solution.py:33
  7.3 18.2 %collective-permute-start = (bf16[528,640]{1,0:T(8,128)(2,1)S(1)}, bf16[528,640]{1,0:T(8,128)(2,1)S(1)}, u32[]{:S(2)}, u32[]{:S(2)}) collective-permute-start(bf16[528,640]{1,0:T(8,128)(2,1)S(1)} %pad_maximum_fusion.6), channel_id=1, source_target_pairs={{0,4},{1,5},{2,6},{3,7},{4,0},{5,1},{6,2},{7,3},{8,12},{9,13},{10,... | collective-permute-start | bytes 2027528 | tf_op jit(solution)/shard_map/ppermute | solution.py:33
  12.9 50.0 %copy-start.1 = (bf16[288,512]{1,0:T(8,128)(2,1)}, bf16[288,512]{1,0:T(8,128)(2,1)S(1)}, u32[]{:S(2)}) copy-start(bf16[288,512]{1,0:T(8,128)(2,1)S(1)} %get-tuple-element.15) | copy-start | bytes 884740
  13.0 50.0 %copy-start.3 = (bf16[288,512]{1,0:T(8,128)(2,1)}, bf16[288,512]{1,0:T(8,128)(2,1)S(1)}, u32[]{:S(2)}) copy-start(bf16[288,512]{1,0:T(8,128)(2,1)S(1)} %get-tuple-element.28) | copy-start | bytes 884740
  13.0 50.0 %copy-start.5 = (bf16[288,512]{1,0:T(8,128)(2,1)}, bf16[288,512]{1,0:T(8,128)(2,1)S(1)}, u32[]{:S(2)}) copy-start(bf16[288,512]{1,0:T(8,128)(2,1)S(1)} %get-tuple-element.29) | copy-start | bytes 884740
  13.0 50.0 %copy-start.7 = (bf16[288,512]{1,0:T(8,128)(2,1)}, bf16[288,512]{1,0:T(8,128)(2,1)S(1)}, u32[]{:S(2)}) copy-start(bf16[288,512]{1,0:T(8,128)(2,1)S(1)} %get-tuple-element.30) | copy-start | bytes 884740
  13.0 2.1 %copy-start.17 = (s32[128]{0:T(128)S(1)}, s32[128]{0:T(128)}, u32[]{:S(2)}) copy-start(s32[128]{0:T(128)} %param.13) | copy-start | bytes 1540
  13.0 2.1 %copy-start.16 = (bf16[2,128]{1,0:T(2,128)(2,1)S(1)}, bf16[2,128]{1,0:T(2,128)(2,1)}, u32[]{:S(2)}) copy-start(bf16[2,128]{1,0:T(2,128)(2,1)} %param.12) | copy-start | bytes 1540
  13.0 2.2 %copy-start.15 = (s32[144]{0:T(256)S(1)}, s32[144]{0:T(256)}, u32[]{:S(2)}) copy-start(s32[144]{0:T(256)} %param.15) | copy-start | bytes 1732
  13.2 37.4 %collective-permute-start.5 = (bf16[288,2048]{1,0:T(8,128)(2,1)S(1)}, bf16[288,2048]{1,0:T(8,128)(2,1)S(1)}, u32[]{:S(2)}, u32[]{:S(2)}) collective-permute-start(bf16[288,2048]{1,0:T(8,128)(2,1)S(1)} %pad_maximum_fusion.1), channel_id=1, source_target_pairs={{0,8},{1,9},{2,10},{3,11},{4,12},{5,13},{6,14},{7,15},{8,0},{9,1},... | collective-permute-start | bytes 3538952 | tf_op jit(solution)/shard_map/ppermute | solution.py:33
  14.6 51.6 %collective-permute-start.8 = (bf16[288,2048]{1,0:T(8,128)(2,1)S(1)}, bf16[288,2048]{1,0:T(8,128)(2,1)S(1)}, u32[]{:S(2)}, u32[]{:S(2)}) collective-permute-start(bf16[288,2048]{1,0:T(8,128)(2,1)S(1)} %pad_maximum_fusion.2), channel_id=1, source_target_pairs={{0,16},{1,17},{2,18},{3,19},{4,20},{5,21},{6,22},{7,23},{8,24},{9,... | collective-permute-start | bytes 3538952 | tf_op jit(solution)/shard_map/ppermute | solution.py:33
  21.7 34.7 %collective-permute-start.9 = (bf16[288,2048]{1,0:T(8,128)(2,1)S(1)}, bf16[288,2048]{1,0:T(8,128)(2,1)S(1)}, u32[]{:S(2)}, u32[]{:S(2)}) collective-permute-start(bf16[288,2048]{1,0:T(8,128)(2,1)S(1)} %pad_maximum_fusion.3), channel_id=1, source_target_pairs={{0,28},{1,29},{2,30},{3,31},{4,24},{5,25},{6,26},{7,27},{8,20},{9,... | collective-permute-start | bytes 3538952 | tf_op jit(solution)/shard_map/ppermute | solution.py:33
  25.6 5.0 %copy-start.9 = (bf16[2048,640]{1,0:T(8,128)(2,1)S(1)}, bf16[2048,640]{1,0:T(8,128)(2,1)}, u32[]{:S(2)}) copy-start(bf16[2048,640]{1,0:T(8,128)(2,1)} %get-tuple-element.39) | copy-start | bytes 7864324
  25.9 20.9 %collective-permute-start.4 = (bf16[768,640]{1,0:T(8,128)(2,1)S(1)}, bf16[768,640]{1,0:T(8,128)(2,1)S(1)}, u32[]{:S(2)}, u32[]{:S(2)}) collective-permute-start(bf16[768,640]{1,0:T(8,128)(2,1)S(1)} %get-tuple-element.41), channel_id=1, source_target_pairs={{0,96},{1,97},{2,98},{3,99},{4,100},{5,101},{6,102},{7,103},{8,104... | collective-permute-start | bytes 2949128 | tf_op jit(solution)/shard_map/ppermute | solution.py:33
  27.4 21.5 %collective-permute-start.3 = (bf16[768,640]{1,0:T(8,128)(2,1)S(1)}, bf16[768,640]{1,0:T(8,128)(2,1)S(1)}, u32[]{:S(2)}, u32[]{:S(2)}) collective-permute-start(bf16[768,640]{1,0:T(8,128)(2,1)S(1)} %get-tuple-element.42), channel_id=1, source_target_pairs={{0,32},{1,33},{2,34},{3,35},{4,36},{5,37},{6,38},{7,39},{8,40},{9,... | collective-permute-start | bytes 2949128 | tf_op jit(solution)/shard_map/ppermute | solution.py:33
  49.0 8.7 %collective-permute-start.13 = (bf16[256,640]{1,0:T(8,128)(2,1)S(1)}, bf16[256,640]{1,0:T(8,128)(2,1)S(1)}, u32[]{:S(2)}, u32[]{:S(2)}) collective-permute-start(bf16[256,640]{1,0:T(8,128)(2,1)S(1)} %get-tuple-element.34), channel_id=1, source_target_pairs={{0,96},{1,97},{2,98},{3,99},{4,100},{5,101},{6,102},{7,103},{8,104... | collective-permute-start | bytes 983048 | tf_op jit(solution)/shard_map/ppermute | solution.py:33
  49.4 8.3 %collective-permute-start.12 = (bf16[256,640]{1,0:T(8,128)(2,1)S(1)}, bf16[256,640]{1,0:T(8,128)(2,1)S(1)}, u32[]{:S(2)}, u32[]{:S(2)}) collective-permute-start(bf16[256,640]{1,0:T(8,128)(2,1)S(1)} %get-tuple-element.36), channel_id=1, source_target_pairs={{0,32},{1,33},{2,34},{3,35},{4,36},{5,37},{6,38},{7,39},{8,40},{9,... | collective-permute-start | bytes 983048 | tf_op jit(solution)/shard_map/ppermute | solution.py:33
  51.7 11.2 %collective-permute-start.6 = (bf16[288,640]{1,0:T(8,128)(2,1)S(1)}, bf16[288,640]{1,0:T(8,128)(2,1)S(1)}, u32[]{:S(2)}, u32[]{:S(2)}) collective-permute-start(bf16[288,640]{1,0:T(8,128)(2,1)S(1)} %convolution_convert_fusion.3), channel_id=1, source_target_pairs={{0,8},{1,9},{2,10},{3,11},{4,12},{5,13},{6,14},{7,15},{8,0},{9,1},... | collective-permute-start | bytes 1105928 | tf_op jit(solution)/shard_map/ppermute | solution.py:33
  57.5 8.8 %collective-permute-start.10 = (bf16[288,640]{1,0:T(8,128)(2,1)S(1)}, bf16[288,640]{1,0:T(8,128)(2,1)S(1)}, u32[]{:S(2)}, u32[]{:S(2)}) collective-permute-start(bf16[288,640]{1,0:T(8,128)(2,1)S(1)} %convolution_convert_fusion.2), channel_id=1, source_target_pairs={{0,8},{1,9},{2,10},{3,11},{4,12},{5,13},{6,14},{7,15},{8,0},{9,1},... | collective-permute-start | bytes 1105928 | tf_op jit(solution)/shard_map/ppermute | solution.py:33
  57.8 12.9 %copy-start.10 = (bf16[2048,640]{1,0:T(8,128)(2,1)}, bf16[2048,640]{1,0:T(8,128)(2,1)S(1)}, u32[]{:S(2)}) copy-start(bf16[2048,640]{1,0:T(8,128)(2,1)S(1)} %constant_dynamic-update-slice_fusion.3) | copy-start | bytes 7864324
  58.9 11.7 %collective-permute-start.15 = (bf16[288,640]{1,0:T(8,128)(2,1)S(1)}, bf16[288,640]{1,0:T(8,128)(2,1)S(1)}, u32[]{:S(2)}, u32[]{:S(2)}) collective-permute-start(bf16[288,640]{1,0:T(8,128)(2,1)S(1)} %convolution_convert_fusion), channel_id=1, source_target_pairs={{0,8},{1,9},{2,10},{3,11},{4,12},{5,13},{6,14},{7,15},{8,0},{9,1},... | collective-permute-start | bytes 1105928 | tf_op jit(solution)/shard_map/ppermute | solution.py:33
  64.1 12.0 %collective-permute-start.7 = (bf16[288,640]{1,0:T(8,128)(2,1)S(1)}, bf16[288,640]{1,0:T(8,128)(2,1)S(1)}, u32[]{:S(2)}, u32[]{:S(2)}) collective-permute-start(bf16[288,640]{1,0:T(8,128)(2,1)S(1)} %add_convert_fusion.1), channel_id=1, source_target_pairs={{0,4},{1,5},{2,6},{3,7},{4,0},{5,1},{6,2},{7,3},{8,12},{9,13},{10,... | collective-permute-start | bytes 1105928 | tf_op jit(solution)/shard_map/ppermute | solution.py:33
  67.4 16.9 %collective-permute-start.11 = (bf16[288,640]{1,0:T(8,128)(2,1)S(1)}, bf16[288,640]{1,0:T(8,128)(2,1)S(1)}, u32[]{:S(2)}, u32[]{:S(2)}) collective-permute-start(bf16[288,640]{1,0:T(8,128)(2,1)S(1)} %fusion.10), channel_id=1, source_target_pairs={{0,20},{1,21},{2,22},{3,23},{4,16},{5,17},{6,18},{7,19},{8,28},{9,... | collective-permute-start | bytes 1105928 | tf_op jit(solution)/shard_map/ppermute | solution.py:33
  70.1 19.5 %collective-permute-start.14 = (bf16[288,640]{1,0:T(8,128)(2,1)}, bf16[288,640]{1,0:T(8,128)(2,1)}, u32[]{:S(2)}, u32[]{:S(2)}) collective-permute-start(bf16[288,640]{1,0:T(8,128)(2,1)} %convolution_convert_fusion.1), channel_id=1, source_target_pairs={{0,8},{1,9},{2,10},{3,11},{4,12},{5,13},{6,14},{7,15},{8,0},{9,1},... | collective-permute-start | bytes 1105928 | tf_op jit(solution)/shard_map/ppermute | solution.py:33
  72.5 17.0 %copy-start.2 = (bf16[288,512]{1,0:T(8,128)(2,1)S(1)}, bf16[288,512]{1,0:T(8,128)(2,1)}, u32[]{:S(2)}) copy-start(bf16[288,512]{1,0:T(8,128)(2,1)} %copy-done.1) | copy-start | bytes 884740
  72.6 17.1 %copy-start.4 = (bf16[288,512]{1,0:T(8,128)(2,1)S(1)}, bf16[288,512]{1,0:T(8,128)(2,1)}, u32[]{:S(2)}) copy-start(bf16[288,512]{1,0:T(8,128)(2,1)} %copy-done.3) | copy-start | bytes 884740
  72.6 17.1 %copy-start.6 = (bf16[288,512]{1,0:T(8,128)(2,1)S(1)}, bf16[288,512]{1,0:T(8,128)(2,1)}, u32[]{:S(2)}) copy-start(bf16[288,512]{1,0:T(8,128)(2,1)} %copy-done.5) | copy-start | bytes 884740
  72.6 17.1 %copy-start.8 = (bf16[288,512]{1,0:T(8,128)(2,1)S(1)}, bf16[288,512]{1,0:T(8,128)(2,1)}, u32[]{:S(2)}) copy-start(bf16[288,512]{1,0:T(8,128)(2,1)} %copy-done.7) | copy-start | bytes 884740
  72.6 17.0 %collective-permute-start.16 = (bf16[288,640]{1,0:T(8,128)(2,1)}, bf16[288,640]{1,0:T(8,128)(2,1)}, u32[]{:S(2)}, u32[]{:S(2)}) collective-permute-start(bf16[288,640]{1,0:T(8,128)(2,1)} %fusion.11), channel_id=1, source_target_pairs={{0,16},{1,17},{2,18},{3,19},{4,20},{5,21},{6,22},{7,23},{8,24},{9,... | collective-permute-start | bytes 1105928 | tf_op jit(solution)/shard_map/ppermute | solution.py:33
  96.2 2.3 %copy-start = (f32[2,144,64]{2,0,1:T(2,128)S(1)}, f32[2,144,64]{2,0,1:T(2,128)}, u32[]{:S(2)}) copy-start(f32[2,144,64]{2,0,1:T(2,128)} %get-tuple-element.48) | copy-start | bytes 221188
  99.1 5.4 %copy-start.11 = (bf16[2,144,64]{2,0,1:T(2,128)(2,1)S(1)}, bf16[2,144,64]{2,0,1:T(2,128)(2,1)}, u32[]{:S(2)}) copy-start(bf16[2,144,64]{2,0,1:T(2,128)(2,1)} %get-tuple-element.45) | copy-start | bytes 110596
  99.1 5.4 %copy-start.12 = (bf16[2,144,64]{2,0,1:T(2,128)(2,1)S(1)}, bf16[2,144,64]{2,0,1:T(2,128)(2,1)}, u32[]{:S(2)}) copy-start(bf16[2,144,64]{2,0,1:T(2,128)(2,1)} %get-tuple-element.46) | copy-start | bytes 110596
  109.5 4.8 %copy-start.13 = (bf16[288,128]{1,0:T(8,128)(2,1)S(1)}, bf16[288,128]{1,0:T(8,128)(2,1)}, u32[]{:S(2)}) copy-start(bf16[288,128]{1,0:T(8,128)(2,1)} %slice.163) | copy-start | bytes 221188

commit v3 on v1

v3 whole, which is shorter than its diff:
```python
import functools

import jax
import jax.numpy as jnp
from jax import lax
from jax.experimental import pallas as pl
from jax.experimental.pallas import tpu as pltpu
from jax.sharding import PartitionSpec as P

rope_base = 1000000.0
neg_large = -1e30
EARLY = 6
TILE = 256
ALL_Z = (0, -1, 1, 2)
BLOCK = 48

AXES = ("fsdp", "tp")
N_Z = 4
N_TP = 8


def place_of(index):
    f, t = divmod(index, N_TP)
    z, rest = divmod(f, 4)
    y_lo, core = divmod(rest, 2)
    y_hi, x = divmod(t, 4)
    return z, y_hi * 2 + y_lo, x, core


def index_of(z, y, x, core):
    z, y, x, core = z % 4, y % 4, x % 4, core % 2
    return (z * 4 + (y % 2) * 2 + core) * N_TP + (y // 2) * 4 + x


def moved(value, to):
    pairs = [(i, index_of(*to(*place_of(i)))) for i in range(128)]
    return lax.ppermute(value, AXES, pairs)


def z_by(step):
    return lambda z, y, x, core: (z + step, y, x, core)


def other_core(z, y, x, core):
    return z, y, x, 1 - core


def inner_y(z, y, x, core):
    return z, y ^ 1, x, core


def inner_y_core(z, y, x, core):
    return z, y ^ 1, x, 1 - core


def cross_y_core(z, y, x, core):
    return z, 3 - y, x, 1 - core


def cross_y(z, y, x, core):
    return z, 3 - y, x, core


def far_y(z, y, x, core):
    return z, y + 2, x, core


def turned(values, turn, cos_part, sin_part):
    high = values.astype(jnp.bfloat16)
    low = (values - high.astype(jnp.float32)).astype(jnp.bfloat16)
    both = jnp.dot(
        jnp.concatenate([high, low], axis=1), turn, preferred_element_type=jnp.float32
    )
    head_size = values.shape[1]
    rotated = both[:, :head_size] * cos_part + both[:, head_size:] * sin_part
    return rotated.astype(jnp.bfloat16).astype(jnp.float32)


def attention_kernel(
    same1,
    other1,
    same2,
    other2,
    last2,
    waves,
    turn,
    lengths,
    cache,
    out,
    held,
    held_q,
    held_s,
    held_o,
    done,
):
    n_parts = cache.shape[1] // BLOCK
    copies = [
        pltpu.make_async_copy(
            cache.at[k, pl.ds(i * BLOCK, BLOCK)],
            held.at[k, pl.ds(i * BLOCK, BLOCK)],
            done.at[k, i],
        )
        for i in range(cache.shape[1] // BLOCK)
        for k in range(2)
    ]
    for copy in copies:
        copy.start()
    for part in range(n_parts):
        attend_block(
            part * BLOCK,
            copies[part * len(copies) // n_parts : (part + 1) * len(copies) // n_parts],
            *(ref.at[:, pl.ds(part * BLOCK, BLOCK)] for ref in (same1, other1, same2, other2, last2, waves)),
            turn,
            lengths.at[pl.ds(part * BLOCK, BLOCK)],
            held,
            out.at[:, pl.ds(part * BLOCK, BLOCK)],
            held_q,
            held_s,
            held_o,
        )


def attend_block(
    first_row,
    copies,
    same1,
    other1,
    same2,
    other2,
    last2,
    waves,
    turn,
    lengths,
    cache,
    out,
    held_q,
    held_s,
    held_o,
):
    steps, rows, head_size = 2, same1.shape[1], turn.shape[1] // 2
    slots = cache.shape[3]
    per_group = out.shape[2] // head_size
    group = steps * per_group
    early = same1.shape[2] // head_size
    table = waves[...].reshape(steps * rows, 2 * head_size)
    cos_part, sin_part = table[:, :head_size], table[:, head_size:]

    def head(parts, index):
        columns = pl.ds(index * head_size, head_size)
        total = sum(part[:, :, columns].astype(jnp.float32) for part in parts)
        return total.reshape(steps * rows, head_size)

    parts1, parts2 = (same1, other1), (same2, other2, last2)
    keys = turned(head(parts2, 0), turn[...], cos_part, sin_part)
    values = head(parts2, 1).astype(jnp.bfloat16).astype(jnp.float32)
    for h in range(per_group):
        raw = head(parts1, h) if h < early else head(parts2, h - early + 2)
        query = turned(raw, turn[...], cos_part, sin_part)
        for s in range(steps):
            held_q[pl.ds(s * per_group + h, rows, stride=group), :] = query[
                s * rows : (s + 1) * rows
            ]

    queries = held_q[...]
    narrow = queries.astype(jnp.bfloat16)
    scale = head_size ** (-0.5)
    for copy in copies[::2]:
        copy.wait()
    for r in range(rows):
        held_s[r * group : (r + 1) * group, :] = lax.dot_general(
            narrow[r * group : (r + 1) * group],
            cache[0, first_row + r, 0],
            (((1,), (1,)), ((), ())),
            preferred_element_type=jnp.float32,
        )
    old = held_s[...].reshape(rows, group, slots) * scale
    visible = lax.broadcasted_iota(jnp.int32, (rows, slots), 1) < lengths[...]
    old = jnp.where(visible[:, None, :], old, neg_large)
    cube = queries.reshape(rows, group, head_size)
    new0 = jnp.sum(cube * keys[:rows][:, None, :], axis=2, keepdims=True) * scale
    new1 = jnp.sum(cube * keys[rows:][:, None, :], axis=2, keepdims=True) * scale
    later = lax.broadcasted_iota(jnp.int32, (rows, group, 1), 1) >= per_group
    new1 = jnp.where(later, new1, neg_large)
    top = jnp.maximum(jnp.max(old, axis=2, keepdims=True), jnp.maximum(new0, new1))
    old, new0, new1 = jnp.exp(old - top), jnp.exp(new0 - top), jnp.exp(new1 - top)
    share = 1.0 / (jnp.sum(old, axis=2, keepdims=True) + new0 + new1)
    weights = (old * share).astype(jnp.bfloat16).reshape(rows * group, slots)
    new0 = (new0 * share).astype(jnp.bfloat16).astype(jnp.float32)
    new1 = (new1 * share).astype(jnp.bfloat16).astype(jnp.float32)
    fresh = new0 * values[:rows][:, None, :] + new1 * values[rows:][:, None, :]
    for copy in copies[1::2]:
        copy.wait()
    for r in range(rows):
        total = fresh[r] + jnp.dot(
            weights[r * group : (r + 1) * group],
            cache[1, first_row + r, 0],
            preferred_element_type=jnp.float32,
        )
        held_o[pl.ds(r, group, stride=rows), :] = total
    for s in range(steps):
        for h in range(per_group):
            part = held_o[pl.ds((s * per_group + h) * rows, rows), :]
            out[s, :, h * head_size : (h + 1) * head_size] = part.astype(out.dtype)


def attention(same1, other1, same2, other2, last2, waves, turn, lengths, cache):
    steps, rows, slots, head_size = 2, cache.shape[1], cache.shape[3], cache.shape[4]
    width = same1.shape[1] + same2.shape[1] - 2 * head_size
    group = steps * width // head_size
    split = lambda a: a.reshape(steps, rows, a.shape[-1])
    here = pl.BlockSpec(memory_space=pltpu.VMEM)
    return pl.pallas_call(
        attention_kernel,
        out_shape=jax.ShapeDtypeStruct((steps, rows, width), jnp.bfloat16),
        in_specs=[here] * 8 + [pl.BlockSpec(memory_space=pl.ANY)],
        out_specs=here,
        scratch_shapes=[
            pltpu.VMEM(cache.shape, cache.dtype),
            pltpu.VMEM((BLOCK * group, head_size), jnp.float32),
            pltpu.VMEM((BLOCK * group, slots), jnp.float32),
            pltpu.VMEM((BLOCK * group, head_size), jnp.float32),
            pltpu.SemaphoreType.DMA((2, rows // BLOCK)),
        ],
        compiler_params=pltpu.CompilerParams(vmem_limit_bytes=28 * 2**20),
        cost_estimate=pl.CostEstimate(
            flops=4 * rows * group * slots * head_size,
            bytes_accessed=2 * cache.size,
            transcendentals=rows * group * slots,
        ),
    )(
        *(split(a) for a in (same1, other1, same2, other2, last2, waves)),
        turn,
        lengths,
        pltpu.with_memory_space_constraint(cache, pltpu.HBM),
    )


def turning(rotary_perm):
    head_size = rotary_perm.shape[0]
    chosen = jnp.arange(head_size, dtype=jnp.int32)[:, None] == rotary_perm[None, :]
    chosen = chosen.astype(jnp.bfloat16)
    half = head_size // 2
    partner = jnp.concatenate([-chosen[:, half:], chosen[:, :half]], axis=1)
    once = jnp.concatenate([chosen, partner], axis=1)
    return jnp.concatenate([once, once], axis=0)


def wave_table(lengths, steps, head_size):
    pair_index = jnp.arange(head_size // 2, dtype=jnp.float32)
    inverse = rope_base ** (-2.0 * pair_index / head_size)
    places = lengths[None, :] + jnp.arange(steps, dtype=jnp.int32)[:, None]
    angles = places.astype(jnp.float32)[:, :, None] * inverse
    cos_part, sin_part = jnp.cos(angles), jnp.sin(angles)
    table = jnp.concatenate([cos_part, cos_part, sin_part, sin_part], axis=2)
    return table.reshape(-1, 2 * head_size)


def near_over_z(block):
    return moved(block, z_by(1)), moved(block, z_by(-1))


def slabs(tokens):
    f = lax.axis_index("fsdp")
    z, y_lo, core = f // 4, (f // 2) % 2, f % 2
    flat = tokens.reshape(-1, tokens.shape[-1])
    share = flat.shape[1] // 16

    def slab(dy, dc, steps):
        parts = []
        for dz in steps:
            block = ((z + dz) % 4) * 4 + (y_lo ^ dy) * 2 + (core ^ dc)
            parts.append(lax.dynamic_slice_in_dim(flat, block * share, share, 1))
        return jnp.concatenate(parts, axis=1)

    return slab


def product_kernel(n_rows, n_weights, tiles, *refs):
    row_refs, weight_refs = refs[:n_rows], refs[n_rows : n_rows + n_weights]
    out = refs[-1]
    for tile, spans in enumerate(tiles):
        columns = pl.ds(tile * TILE, TILE)
        total, at, which = None, 0, 0
        for source, row, column, depth in spans:
            if at == row_refs[which].shape[1]:
                at, which = 0, which + 1
            part = jnp.dot(
                row_refs[which][:, at : at + depth],
                weight_refs[source][row : row + depth, column : column + TILE],
                preferred_element_type=jnp.float32,
            )
            total = part if total is None else total + part
            at += depth
        for extra in refs[n_rows + n_weights : -1]:
            total = total + extra[:, columns].astype(jnp.float32)
        out[:, columns] = total.astype(out.dtype)


def product(rows, weights, tiles, dtype, *extras):
    operands = [*rows, *weights, *extras]
    here = pl.BlockSpec(memory_space=pltpu.VMEM)
    return pl.pallas_call(
        functools.partial(product_kernel, len(rows), len(weights), tiles),
        out_shape=pltpu.VMEM((rows[0].shape[0], len(tiles) * TILE), dtype),
        in_specs=[here] * len(operands),
        out_specs=here,
        compiler_params=pltpu.CompilerParams(vmem_limit_bytes=4 * 2**20),
        cost_estimate=pl.CostEstimate(flops=1, bytes_accessed=1, transcendentals=0),
    )(*(pltpu.with_memory_space_constraint(a, pltpu.VMEM) for a in operands))


def packed(half, whole):
    width, rest = whole.shape[1], half.shape[1] - whole.shape[1]
    depth = half.shape[0] * rest // width
    pieces = [half[i * depth : (i + 1) * depth, width:] for i in range(width // rest)]
    return jnp.concatenate([whole, half[:, :width], jnp.concatenate(pieces, axis=1)], axis=0)


def body(tokens, w_query, w_keyval, b_query, b_keyval, rotary_perm, cache, lengths):
    head_size = rotary_perm.shape[0]
    tables = (
        wave_table(lengths, tokens.shape[0], head_size),
        turning(rotary_perm),
        lengths.reshape(-1, 1),
    )
    early = EARLY * head_size
    depth = w_query.shape[0]
    half = depth // 2
    first, first_bias = w_query[:, :early], b_query[None, :early]
    second = jnp.concatenate([w_keyval[:, 0], w_keyval[:, 1], w_query[:, early:]], axis=1)
    second_bias = jnp.concatenate([b_keyval[0], b_keyval[1], b_query[early:]])
    second_bias = jnp.broadcast_to(second_bias[None], (16, second_bias.shape[0]))
    slab = slabs(tokens)

    below, above = moved(first, z_by(1)), moved(first, z_by(-1))
    shifted = moved(jnp.concatenate([second, second_bias], axis=0), far_y)
    shifted, below, above, out01, out10, out11 = lax.optimization_barrier(
        (shifted, below, above, slab(0, 1, ALL_Z), slab(1, 0, ALL_Z), slab(1, 1, ALL_Z))
    )
    up = moved(packed(below[:half], shifted[:depth]), z_by(1))
    down = moved(packed(above[half:], shifted[:depth]), z_by(-1))
    rows01 = moved(out01, other_core)
    rows10 = moved(out10, inner_y)
    rows11 = moved(out11, cross_y_core)
    up, down, rows00, tables = lax.optimization_barrier(
        (up, down, slab(0, 0, ALL_Z), tables)
    )
    far_up = moved(up[:half], z_by(1))
    far_down = moved(down[half:depth], z_by(-1))

    width, rest = second.shape[1], early - second.shape[1]
    tiles = []
    for column in range(0, early, TILE):
        spans = [(i, 0, column, depth) for i in range(3)]
        for i in (3, 4):
            if column < width:
                spans.append((i, depth, column, half))
            else:
                count = width // rest
                for j in range(count):
                    spans.append((i, depth + half, column - width + j * rest, half // count))
        tiles.append(tuple(spans))
    weights = first, below, above, up, down
    theirs0 = product([rows01], weights, tiles, jnp.bfloat16)
    theirs0, rows10, rows11 = lax.optimization_barrier((theirs0, rows10, rows11))
    theirs0 = moved(theirs0, other_core)
    theirs1 = moved(product([rows11], weights, tiles, jnp.bfloat16), other_core)
    same = product([rows00], weights, tiles, jnp.bfloat16, theirs0, first_bias)
    other = product([rows10], weights, tiles, jnp.bfloat16, theirs1)
    first_parts = moved(same, far_y), moved(other, cross_y)
    far_up, far_down, _, _ = lax.optimization_barrier((far_up, far_down, same, other))

    tiles = []
    for column in range(0, width, TILE):
        spans = [(i, 0, column, depth) for i in range(3)]
        tiles.append((*spans, (3, 0, column, half), (4, 0, column, half)))
    weights = shifted, up, down, far_up, far_down
    inner = moved(product([rows10], weights, tiles, jnp.bfloat16), inner_y)
    crossed = moved(product([rows11], weights, tiles, jnp.bfloat16), inner_y_core)
    theirs = moved(product([rows01], weights, tiles, jnp.bfloat16), other_core)
    own = product([rows00], weights, tiles, jnp.float32, theirs, shifted[depth : depth + 1])
    return attention(*first_parts, own, inner, crossed, *tables, cache)


def solution(mesh):
    placed = (
        P(None, "fsdp", None),
        P("fsdp", "tp"),
        P("fsdp", None, "tp"),
        P("tp"),
        P(None, "tp"),
        P(),
        P(None, "fsdp", "tp", None, None),
        P("fsdp"),
    )
    return jax.shard_map(
        body, mesh=mesh, in_specs=placed, out_specs=P(None, "fsdp", "tp"), check_vma=False
    )
```

time: 129 us -> 99.9 us (0.77)
  waiting for transfers between devices: 62 us -> 36 us
  matrix products: 22.5 us -> 0 us
  Pallas kernels: 0 us -> 22.4 us
  other arithmetic: 9.18 us -> 5.25 us
  starting transfers between devices: 24.9 us -> 23.2 us
  local copies, waits for them, and re-layouts: 10.2 us -> 11.5 us
    ppermute x15 -> x17, waiting for transfers between devices: 62 us -> 36 us  [moved(): return lax.ppermute(value, AXES, pairs)]
    dot_general x12 -> x0, matrix products: 22.5 us -> none  [the longest x8 8.93 us: returned(): jnp.dot(value, weights, preferred_element_type=jnp.float32)]
    pallas_call x0 -> x9, Pallas kernels: none -> 22.4 us  [the longest x8 12.7 us: product(): pl.pallas_call(functools.partial(product_kernel, len(rows), len(weights),...]
    gather x4 -> x0, local copies, waits for them, and re-layouts: 2.85 us -> none  [the longest x2 1.84 us: body(): queries = jnp.take(queries, rotary_perm, axis=4)]
    unnamed x17 -> x62, local copies, waits for them, and re-layouts: 0.64 us -> 2.95 us
    reshape x4 -> x0, local copies, waits for them, and re-layouts: 2.2 us -> none  [the longest x2 1.09 us: body(): return result.reshape(step_count, row_count, per_group * head_size)]
    reduce_sum x2 -> x0, other arithmetic: 1.9 us -> none  [the longest x1 1.33 us: attend(): jnp.sum(cached_exp, axis=-1, keepdims=True)]
    dynamic_slice x1, local copies, waits for them, and re-layouts: 2.65 us -> 4.54 us  [slab(): parts.append(lax.dynamic_slice_in_dim(flat, block * share, share, 1))]
  transfers between devices with their start and end apart: 15 -> 17, of which waited for: 8 -> 7; matrix products, arithmetic and copies ran while one was open for 15% -> 13% of each run, Pallas kernels for 0% -> 12%
where the time goes in v3:
time: 99.9 us; the launch traced here: 99.1 us
  waiting for transfers between devices  36 us (36%)
  starting transfers between devices  23.2 us (23%)
  Pallas kernels  22.4 us (22%)
  local copies, waits for them, and re-layouts  11.5 us (12%)
  other arithmetic  5.25 us (5%)
    ppermute x17, waiting for transfers between devices, moved(): return lax.ppermute(value, AXES, pairs)  36 us
    ppermute x17, starting transfers between devices, moved(): return lax.ppermute(value, AXES, pairs)  23.2 us
    pallas_call x8, Pallas kernels, product(): pl.pallas_call(functools.partial(product_kernel, len(rows), len(weights),...  12.7 us
    pallas_call x1, Pallas kernels, attention(): pl.pallas_call(attention_kernel, out_shape=jax.ShapeDtypeStruct((steps, r...  9.68 us
    dynamic_slice x1, local copies, waits for them, and re-layouts, slab(): parts.append(lax.dynamic_slice_in_dim(flat, block * share, share, 1))  4.54 us
    unnamed x62, local copies, waits for them, and re-layouts  2.95 us
  transfers between devices with their start and end apart: 17, of which 7 were waited for; matrix products, arithmetic and copies ran while one was open for 13% of the time, Pallas kernels for 12%

profile of v3, /device:TPU:1, one launch (start us, length us, event | category | flops | bytes accessed | tf_op | source)
XLA Modules:
  0.0 99.1 jit_solution(4695723751415602535)
XLA Ops:
  0.0 1.2 %slice.75.refs_1_ = bf16[512,768]{1,0:T(8,128)(2,1)S(1)} slice(bf16[512,1024]{1,0:T(8,128)(2,1)} %param.9), slice={[0:512], [0:768]} | slice | bytes 1572864 | tf_op jit(solution)/shard_map/slice | solution.py:329
  1.3 0.0 copy-start.30
  1.3 2.5 %collective-permute-start.1 = (bf16[512,768]{1,0:T(8,128)(2,1)S(1)}, bf16[512,768]{1,0:T(8,128)(2,1)S(1)}, u32[]{:S(2)}, u32[]{:S(2)}) collective-permute-start(bf16[512,768]{1,0:T(8,128)(2,1)S(1)} %slice.75.refs_1_), channel_id=1, source_target_pairs={{0,32},{1,33},{2,34},{3,35},{4,36},{5,37},{6,38},{7,39},{8,40},{9,... | collective-permute-start | bytes 2359304 | tf_op jit(solution)/shard_map/ppermute | solution.py:37
  3.8 2.2 %collective-permute-start.2 = (bf16[512,768]{1,0:T(8,128)(2,1)S(1)}, bf16[512,768]{1,0:T(8,128)(2,1)S(1)}, u32[]{:S(2)}, u32[]{:S(2)}) collective-permute-start(bf16[512,768]{1,0:T(8,128)(2,1)S(1)} %slice.75.refs_1_), channel_id=1, source_target_pairs={{0,96},{1,97},{2,98},{3,99},{4,100},{5,101},{6,102},{7,103},{8,104... | collective-permute-start | bytes 2359304 | tf_op jit(solution)/shard_map/ppermute | solution.py:37
  6.0 0.4 fusion.5
  6.5 0.8 pad_maximum_fusion.6
  7.4 2.9 %collective-permute-start = (bf16[528,512]{1,0:T(8,128)(2,1)}, bf16[528,512]{1,0:T(8,128)(2,1)S(1)}, u32[]{:S(2)}, u32[]{:S(2)}) collective-permute-start(bf16[528,512]{1,0:T(8,128)(2,1)} %pad_maximum_fusion.6), channel_id=1, source_target_pairs={{0,4},{1,5},{2,6},{3,7},{4,0},{5,1},{6,2},{7,3},{8,12},{9,13},{10,... | collective-permute-start | bytes 1622024 | tf_op jit(solution)/shard_map/ppermute | solution.py:37
  10.4 0.0 copy-start.27
  10.4 4.5 %constant_dynamic-slice_fusion.3 = (bf16[288,512]{1,0:T(8,128)(2,1)}, bf16[288,512]{1,0:T(8,128)(2,1)}, bf16[288,512]{1,0:T(8,128)(2,1)}, bf16[288,512]{1,0:T(8,...) fusion(bf16[288,8192]{1,0:T(8,128)(2,1)} %bitcast.19, ...), kind=kLoop, calls=%fused_computation.21 | loop fusion | bytes 9437248 | tf_op jit(solution)/shard_map/dynamic_slice | solution.py:272
  14.9 0.1 slice_negate_fusion
  15.0 0.7 maximum_maximum_fusion.turn
  15.8 0.1 add.250
  15.9 0.1 add.252
  16.0 1.5 %pad_maximum_fusion.2 = bf16[288,2048]{1,0:T(8,128)(2,1)S(1)} fusion(bf16[288,512]{1,0:T(8,128)(2,1)} %get-tuple-element.43, bf16[288,512]{1,0:T(8,128)(2,1)} %get-tuple-element.44, bf16[288,512]{1,0:T(8,128)(2,1)} %get-tuple-element.45, bf16[288,512]{1,0:T(8,128)(2,1)} %get-tuple-element.46), kind=kLoop, calls=%fused_computation.2 | loop fusion | flops 4718592 | bytes 2359296 | tf_op jit(solution)/shard_map/concatenate | solution.py:273
  17.5 0.0 copy-done.22
  17.6 0.1 copy-done.23
  17.6 0.1 copy-done.24
  17.7 0.1 copy-done.25
  17.8 0.3 pad_maximum_fusion
  18.1 3.8 %collective-permute-done.refs_1_ = bf16[528,512]{1,0:T(8,128)(2,1)S(1)} collective-permute-done((bf16[528,512]{1,0:T(8,128)(2,1)}, bf16[528,512]{1,0:T(8,128)(2,1)S(1)}, u32[]{:S(2)}, u32[]{:S(2)}) %collective-permute-start) | collective-permute-done | bytes 540704 | tf_op jit(solution)/shard_map/ppermute | solution.py:37
  21.9 1.3 %collective-permute-done.1.refs_2_ = bf16[512,768]{1,0:T(8,128)(2,1)S(1)} collective-permute-done((bf16[512,768]{1,0:T(8,128)(2,1)S(1)}, bf16[512,768]{1,0:T(8,128)(2,1)S(1)}, u32[]{:S(2)}, u32[]{:S(2)}) %collective-permute-start.1) | collective-permute-done | bytes 786464 | tf_op jit(solution)/shard_map/ppermute | solution.py:37
  23.2 0.0 collective-permute-done.2.refs_3_
  23.2 1.3 %collective-permute-start.5 = (bf16[288,2048]{1,0:T(8,128)(2,1)S(1)}, bf16[288,2048]{1,0:T(8,128)(2,1)S(1)}, u32[]{:S(2)}, u32[]{:S(2)}) collective-permute-start(bf16[288,2048]{1,0:T(8,128)(2,1)S(1)} %get-tuple-element.28), channel_id=1, source_target_pairs={{0,8},{1,9},{2,10},{3,11},{4,12},{5,13},{6,14},{7,15},{8,0},{9,1},... | collective-permute-start | bytes 3538952 | tf_op jit(solution)/shard_map/ppermute | solution.py:37
  24.5 1.3 %collective-permute-start.6 = (bf16[288,2048]{1,0:T(8,128)(2,1)S(1)}, bf16[288,2048]{1,0:T(8,128)(2,1)S(1)}, u32[]{:S(2)}, u32[]{:S(2)}) collective-permute-start(bf16[288,2048]{1,0:T(8,128)(2,1)S(1)} %get-tuple-element.29), channel_id=1, source_target_pairs={{0,16},{1,17},{2,18},{3,19},{4,20},{5,21},{6,22},{7,23},{8,24},{9,... | collective-permute-start | bytes 3538952 | tf_op jit(solution)/shard_map/ppermute | solution.py:37
  25.8 2.1 %collective-permute-start.7 = (bf16[288,2048]{1,0:T(8,128)(2,1)S(1)}, bf16[288,2048]{1,0:T(8,128)(2,1)S(1)}, u32[]{:S(2)}, u32[]{:S(2)}) collective-permute-start(bf16[288,2048]{1,0:T(8,128)(2,1)S(1)} %pad_maximum_fusion.2), channel_id=1, source_target_pairs={{0,28},{1,29},{2,30},{3,31},{4,24},{5,25},{6,26},{7,27},{8,20},{9,... | collective-permute-start | bytes 3538952 | tf_op jit(solution)/shard_map/ppermute | solution.py:37
  28.1 0.1 fusion.1
  28.3 1.0 %collective-permute-start.3 = (bf16[896,512]{1,0:T(8,128)(2,1)S(1)}, bf16[896,512]{1,0:T(8,128)(2,1)S(1)}, u32[]{:S(2)}, u32[]{:S(2)}) collective-permute-start(bf16[896,512]{1,0:T(8,128)(2,1)S(1)} %get-tuple-element.60), channel_id=1, source_target_pairs={{0,32},{1,33},{2,34},{3,35},{4,36},{5,37},{6,38},{7,39},{8,40},{9,... | collective-permute-start | bytes 2752520 | tf_op jit(solution)/shard_map/ppermute | solution.py:37
  29.3 1.9 %collective-permute-start.4 = (bf16[896,512]{1,0:T(8,128)(2,1)S(1)}, bf16[896,512]{1,0:T(8,128)(2,1)S(1)}, u32[]{:S(2)}, u32[]{:S(2)}) collective-permute-start(bf16[896,512]{1,0:T(8,128)(2,1)S(1)} %get-tuple-element.59), channel_id=1, source_target_pairs={{0,96},{1,97},{2,98},{3,99},{4,100},{5,101},{6,102},{7,103},{8,104... | collective-permute-start | bytes 2752520 | tf_op jit(solution)/shard_map/ppermute | solution.py:37
  31.2 0.6 multiply_cosine_fusion
  31.8 0.9 pad_maximum_fusion.7
  32.8 0.1 pad_maximum_fusion.3.refs_0_
  32.9 18.6 %collective-permute-done.3.refs_4_.refs_2_ = bf16[896,512]{1,0:T(8,128)(2,1)S(1)} collective-permute-done((bf16[896,512]{1,0:T(8,128)(2,1)S(1)}, bf16[896,512]{1,0:T(8,128)(2,1)S(1)}, u32[]{:S(2)}, u32[]{:S(2)}) %collective-permute-start.3) | collective-permute-done | bytes 917536 | tf_op jit(solution)/shard_map/ppermute | solution.py:37
  51.6 1.2 %shard_map.82 = bf16[288,768]{1,0:T(8,128)(2,1)S(1)} custom-call(bf16[288,2048]{1,0:T(8,128)(2,1)S(1)} %collective-permute-done.5.refs_0_, bf16[512,768]{1,0:T(8,128)(2,1)S(1)} %slice.75.refs_1_, bf16[512,768]{1,0:T(8,128)(2,1)S(1)} %collective-permute-done.1.refs_2_, bf16[512,768]{1,0:T(8,128)(2,1)S(1)} %copy-done.1, ...), custom_call_target="tpu_custom_call" | custom-call | flops 1 | bytes 1 | tf_op jit(solution)/shard_map/pallas_call | solution.py:302
  52.8 0.0 collective-permute-done.6.refs_0_
  52.8 2.2 %collective-permute-done.7.refs_0_ = bf16[288,2048]{1,0:T(8,128)(2,1)S(1)} collective-permute-done((bf16[288,2048]{1,0:T(8,128)(2,1)S(1)}, bf16[288,2048]{1,0:T(8,128)(2,1)S(1)}, u32[]{:S(2)}, u32[]{:S(2)}) %collective-permute-start.7) | collective-permute-done | bytes 1179680 | tf_op jit(solution)/shard_map/ppermute | solution.py:37
  55.0 1.2 %shard_map.84 = bf16[288,768]{1,0:T(8,128)(2,1)S(1)} custom-call(bf16[288,2048]{1,0:T(8,128)(2,1)S(1)} %collective-permute-done.7.refs_0_, bf16[512,768]{1,0:T(8,128)(2,1)S(1)} %slice.75.refs_1_, bf16[512,768]{1,0:T(8,128)(2,1)S(1)} %collective-permute-done.1.refs_2_, bf16[512,768]{1,0:T(8,128)(2,1)S(1)} %copy-done.1, ...), custom_call_target="tpu_custom_call" | custom-call | flops 1 | bytes 1 | tf_op jit(solution)/shard_map/pallas_call | solution.py:302
  56.2 0.4 collective-permute-start.10
  56.6 0.2 collective-permute-start.8
  56.8 1.0 %collective-permute-start.12 = (bf16[256,512]{1,0:T(8,128)(2,1)S(1)}, bf16[256,512]{1,0:T(8,128)(2,1)S(1)}, u32[]{:S(2)}, u32[]{:S(2)}) collective-permute-start(bf16[256,512]{1,0:T(8,128)(2,1)S(1)} %slice.86), channel_id=1, source_target_pairs={{0,32},{1,33},{2,34},{3,35},{4,36},{5,37},{6,38},{7,39},{8,40},{9,... | collective-permute-start | bytes 786440 | tf_op jit(solution)/shard_map/ppermute | solution.py:37
  57.9 1.9 %collective-permute-start.13 = (bf16[256,512]{1,0:T(8,128)(2,1)S(1)}, bf16[256,512]{1,0:T(8,128)(2,1)S(1)}, u32[]{:S(2)}, u32[]{:S(2)}) collective-permute-start(bf16[256,512]{1,0:T(8,128)(2,1)S(1)} %slice.87), channel_id=1, source_target_pairs={{0,96},{1,97},{2,98},{3,99},{4,100},{5,101},{6,102},{7,103},{8,104... | collective-permute-start | bytes 786440 | tf_op jit(solution)/shard_map/ppermute | solution.py:37
  59.7 0.0 collective-permute-done.10.refs_6_
  59.7 2.0 %shard_map.85 = bf16[288,768]{1,0:T(8,128)(2,1)} custom-call(bf16[288,2048]{1,0:T(8,128)(2,1)S(1)} %collective-permute-done.6.refs_0_, bf16[512,768]{1,0:T(8,128)(2,1)S(1)} %slice.75.refs_1_, bf16[512,768]{1,0:T(8,128)(2,1)S(1)} %collective-permute-done.1.refs_2_, bf16[512,768]{1,0:T(8,128)(2,1)S(1)} %copy-done.1, ...), custom_call_target="tpu_custom_call" | custom-call | flops 1 | bytes 1 | tf_op jit(solution)/shard_map/pallas_call | solution.py:302
  61.7 1.9 %collective-permute-start.11 = (bf16[288,768]{1,0:T(8,128)(2,1)}, bf16[288,768]{1,0:T(8,128)(2,1)}, u32[]{:S(2)}, u32[]{:S(2)}) collective-permute-start(bf16[288,768]{1,0:T(8,128)(2,1)} %shard_map.85), channel_id=1, source_target_pairs={{0,20},{1,21},{2,22},{3,23},{4,16},{5,17},{6,18},{7,19},{8,28},{9,... | collective-permute-start | bytes 1327112 | tf_op jit(solution)/shard_map/ppermute | solution.py:37
  63.6 2.0 %shard_map.83 = bf16[288,768]{1,0:T(8,128)(2,1)} custom-call(bf16[288,2048]{1,0:T(8,128)(2,1)S(1)} %pad_maximum_fusion.3.refs_0_, bf16[512,768]{1,0:T(8,128)(2,1)S(1)} %slice.75.refs_1_, bf16[512,768]{1,0:T(8,128)(2,1)S(1)} %collective-permute-done.1.refs_2_, bf16[512,768]{1,0:T(8,128)(2,1)S(1)} %copy-done.1, ...), custom_call_target="tpu_custom_call" | custom-call | flops 1 | bytes 1 | tf_op jit(solution)/shard_map/pallas_call | solution.py:302
  65.6 0.2 collective-permute-done.12.refs_4_
  65.8 0.0 collective-permute-done.13.refs_5_
  65.8 1.5 %shard_map.86 = bf16[288,512]{1,0:T(8,128)(2,1)} custom-call(bf16[288,2048]{1,0:T(8,128)(2,1)S(1)} %collective-permute-done.5.refs_0_, bf16[528,512]{1,0:T(8,128)(2,1)S(1)} %copy-done.3, bf16[896,512]{1,0:T(8,128)(2,1)S(1)} %collective-permute-done.3.refs_4_.refs_2_, bf16[896,512]{1,0:T(8,128)(2,1)S(1)} %collective-permute-done.4.refs_5_.refs_3_, ...), custom_call_target="tpu_custom_call" | custom-call | flops 1 | bytes 1 | tf_op jit(solution)/shard_map/pallas_call | solution.py:302
  67.3 1.1 %collective-permute-start.14 = (bf16[288,512]{1,0:T(8,128)(2,1)}, bf16[288,512]{1,0:T(8,128)(2,1)}, u32[]{:S(2)}, u32[]{:S(2)}) collective-permute-start(bf16[288,512]{1,0:T(8,128)(2,1)} %shard_map.86), channel_id=1, source_target_pairs={{0,8},{1,9},{2,10},{3,11},{4,12},{5,13},{6,14},{7,15},{8,0},{9,1},... | collective-permute-start | bytes 884744 | tf_op jit(solution)/shard_map/ppermute | solution.py:37
  68.4 1.5 %shard_map.89 = bf16[288,512]{1,0:T(8,128)(2,1)} custom-call(bf16[288,2048]{1,0:T(8,128)(2,1)S(1)} %collective-permute-done.7.refs_0_, bf16[528,512]{1,0:T(8,128)(2,1)S(1)} %copy-done.3, bf16[896,512]{1,0:T(8,128)(2,1)S(1)} %collective-permute-done.3.refs_4_.refs_2_, bf16[896,512]{1,0:T(8,128)(2,1)S(1)} %collective-permute-done.4.refs_5_.refs_3_, ...), custom_call_target="tpu_custom_call" | custom-call | flops 1 | bytes 1 | tf_op jit(solution)/shard_map/pallas_call | solution.py:302
  69.9 1.3 %collective-permute-start.16 = (bf16[288,512]{1,0:T(8,128)(2,1)}, bf16[288,512]{1,0:T(8,128)(2,1)}, u32[]{:S(2)}, u32[]{:S(2)}) collective-permute-start(bf16[288,512]{1,0:T(8,128)(2,1)} %shard_map.89), channel_id=1, source_target_pairs={{0,24},{1,25},{2,26},{3,27},{4,28},{5,29},{6,30},{7,31},{8,16},{9,... | collective-permute-start | bytes 884744 | tf_op jit(solution)/shard_map/ppermute | solution.py:37
  71.3 1.5 %shard_map.88 = bf16[288,512]{1,0:T(8,128)(2,1)} custom-call(bf16[288,2048]{1,0:T(8,128)(2,1)S(1)} %collective-permute-done.6.refs_0_, bf16[528,512]{1,0:T(8,128)(2,1)S(1)} %copy-done.3, bf16[896,512]{1,0:T(8,128)(2,1)S(1)} %collective-permute-done.3.refs_4_.refs_2_, bf16[896,512]{1,0:T(8,128)(2,1)S(1)} %collective-permute-done.4.refs_5_.refs_3_, ...), custom_call_target="tpu_custom_call" | custom-call | flops 1 | bytes 1 | tf_op jit(solution)/shard_map/pallas_call | solution.py:302
  72.8 0.1 collective-permute-start.15
  72.9 0.6 slice.88.refs_7_
  73.5 1.4 %copy.13.lengths = s32[144,1]{1,0:T(8,128)} copy(s32[144,1]{0,1:T(1,128)} %bitcast.20) | data formatting | bytes 1152 | tf_op jit(solution)/shard_map/optimization_barrier | solution.py:345
  74.9 0.0 collective-permute-done.14.refs_6_
  74.9 0.9 copy-done.8
  75.9 0.9 copy-done.10
  76.8 0.7 copy-done.14
  77.5 1.8 %shard_map.87 = f32[288,512]{1,0:T(8,128)S(1)} custom-call(bf16[288,2048]{1,0:T(8,128)(2,1)S(1)} %copy-done.6, bf16[528,512]{1,0:T(8,128)(2,1)S(1)} %copy-done.4, bf16[896,512]{1,0:T(8,128)(2,1)S(1)} %collective-permute-done.3.refs_4_.refs_2_, bf16[896,512]{1,0:T(8,128)(2,1)S(1)} %collective-permute-done.4.refs_5_.refs_3_, bf16[256,512]{1,0:T(8,128)(2,1)S(1)} %copy-done.8, ...), custom_call_target="tpu_custom_call" | custom-call | flops 1 | bytes 1 | tf_op jit(solution)/shard_map/pallas_call | solution.py:302
  79.3 6.3 %collective-permute-done.16 = bf16[288,512]{1,0:T(8,128)(2,1)} collective-permute-done((bf16[288,512]{1,0:T(8,128)(2,1)}, bf16[288,512]{1,0:T(8,128)(2,1)}, u32[]{:S(2)}, u32[]{:S(2)}) %collective-permute-start.16) | collective-permute-done | bytes 294944 | tf_op jit(solution)/shard_map/ppermute | solution.py:37
  85.6 3.5 %collective-permute-done.15 = bf16[288,512]{1,0:T(8,128)(2,1)} collective-permute-done((bf16[288,512]{1,0:T(8,128)(2,1)}, bf16[288,512]{1,0:T(8,128)(2,1)}, u32[]{:S(2)}, u32[]{:S(2)}) %collective-permute-start.15) | collective-permute-done | bytes 294944 | tf_op jit(solution)/shard_map/ppermute | solution.py:37
  89.2 0.0 collective-permute-done.11
  89.2 0.0 collective-permute-done.9
  89.2 9.7 %shard_map.90 = bf16[2,144,1024]{2,1,0:T(8,128)(2,1)} custom-call(bf16[2,144,768]{2,1,0:T(8,128)(2,1)} %bitcast.6.same1, bf16[2,144,768]{2,1,0:T(8,128)(2,1)} %bitcast.7.other1, f32[2,144,512]{2,1,0:T(8,128)S(1)} %bitcast.17, bf16[2,144,512]{2,1,0:T(8,128)(2,1)} %bitcast.9.other2, bf16[2,144,512]{2,1,0:T(8,128)(2,1)} %bitcast.10.last2, ...), custom_call_target="tpu_custom_call" | custom-call | flops 301989888 | bytes 18874368 | tf_op jit(solution)/shard_map/pallas_call | solution.py:212
  (77 shorter events, 0.4 us)
Async XLA Ops:
  0.0 6.5 %slice-start = ((bf16[512,1024]{1,0:T(8,128)(2,1)}), bf16[512,256]{1,0:T(8,128)(2,1)S(1)}, s32[]{:S(2)}) async-start(bf16[512,1024]{1,0:T(8,128)(2,1)} %param.9), calls=%async_computation | async-start | bytes 524288 | tf_op jit(solution)/shard_map/slice | solution.py:330
  0.0 6.0 %copy-start.26 = (bf16[512,2,128]{2,1,0:T(2,128)(2,1)S(1)}, bf16[512,2,128]{2,1,0:T(2,128)(2,1)}, u32[]{:S(2)}) copy-start(bf16[512,2,128]{2,1,0:T(2,128)(2,1)} %param.10) | copy-start | bytes 786436
  0.0 6.4 %copy-start.29 = (bf16[2,128]{1,0:T(2,128)(2,1)S(1)}, bf16[2,128]{1,0:T(2,128)(2,1)}, u32[]{:S(2)}) copy-start(bf16[2,128]{1,0:T(2,128)(2,1)} %param.12) | copy-start | bytes 1540
  0.0 6.4 %copy-start.28 = (bf16[1024]{0:T(1024)(128)(2,1)S(1)}, bf16[1024]{0:T(1024)(128)(2,1)}, u32[]{:S(2)}) copy-start(bf16[1024]{0:T(1024)(128)(2,1)} %param.11) | copy-start | bytes 6148
  1.3 9.0 %copy-start.30 = (s32[128]{0:T(128)S(1)}, s32[128]{0:T(128)}, u32[]{:S(2)}) copy-start(s32[128]{0:T(128)} %param.13) | copy-start | bytes 1540
  1.3 21.9 %collective-permute-start.1 = (bf16[512,768]{1,0:T(8,128)(2,1)S(1)}, bf16[512,768]{1,0:T(8,128)(2,1)S(1)}, u32[]{:S(2)}, u32[]{:S(2)}) collective-permute-start(bf16[512,768]{1,0:T(8,128)(2,1)S(1)} %slice.75.refs_1_), channel_id=1, source_target_pairs={{0,32},{1,33},{2,34},{3,35},{4,36},{5,37},{6,38},{7,39},{8,40},{9,... | collective-permute-start | bytes 2359304 | tf_op jit(solution)/shard_map/ppermute | solution.py:37
  3.8 19.4 %collective-permute-start.2 = (bf16[512,768]{1,0:T(8,128)(2,1)S(1)}, bf16[512,768]{1,0:T(8,128)(2,1)S(1)}, u32[]{:S(2)}, u32[]{:S(2)}) collective-permute-start(bf16[512,768]{1,0:T(8,128)(2,1)S(1)} %slice.75.refs_1_), channel_id=1, source_target_pairs={{0,96},{1,97},{2,98},{3,99},{4,100},{5,101},{6,102},{7,103},{8,104... | collective-permute-start | bytes 2359304 | tf_op jit(solution)/shard_map/ppermute | solution.py:37
  7.4 14.5 %collective-permute-start = (bf16[528,512]{1,0:T(8,128)(2,1)}, bf16[528,512]{1,0:T(8,128)(2,1)S(1)}, u32[]{:S(2)}, u32[]{:S(2)}) collective-permute-start(bf16[528,512]{1,0:T(8,128)(2,1)} %pad_maximum_fusion.6), channel_id=1, source_target_pairs={{0,4},{1,5},{2,6},{3,7},{4,0},{5,1},{6,2},{7,3},{8,12},{9,13},{10,... | collective-permute-start | bytes 1622024 | tf_op jit(solution)/shard_map/ppermute | solution.py:37
  10.4 5.4 %copy-start.27 = (s32[144]{0:T(256)S(1)}, s32[144]{0:T(256)}, u32[]{:S(2)}) copy-start(s32[144]{0:T(256)} %param.15) | copy-start | bytes 1732
  16.0 1.5 %copy-start.19 = (bf16[288,512]{1,0:T(8,128)(2,1)S(1)}, bf16[288,512]{1,0:T(8,128)(2,1)}, u32[]{:S(2)}) copy-start(bf16[288,512]{1,0:T(8,128)(2,1)} %get-tuple-element.48) | copy-start | bytes 884740
  16.0 1.6 %copy-start.20 = (bf16[288,512]{1,0:T(8,128)(2,1)S(1)}, bf16[288,512]{1,0:T(8,128)(2,1)}, u32[]{:S(2)}) copy-start(bf16[288,512]{1,0:T(8,128)(2,1)} %get-tuple-element.49) | copy-start | bytes 884740
  16.0 1.6 %copy-start.21 = (bf16[288,512]{1,0:T(8,128)(2,1)S(1)}, bf16[288,512]{1,0:T(8,128)(2,1)}, u32[]{:S(2)}) copy-start(bf16[288,512]{1,0:T(8,128)(2,1)} %get-tuple-element.50) | copy-start | bytes 884740
  16.0 1.6 %copy-start.22 = (bf16[288,512]{1,0:T(8,128)(2,1)S(1)}, bf16[288,512]{1,0:T(8,128)(2,1)}, u32[]{:S(2)}) copy-start(bf16[288,512]{1,0:T(8,128)(2,1)} %get-tuple-element.51) | copy-start | bytes 884740
  16.0 1.7 %copy-start.23 = (bf16[288,512]{1,0:T(8,128)(2,1)S(1)}, bf16[288,512]{1,0:T(8,128)(2,1)}, u32[]{:S(2)}) copy-start(bf16[288,512]{1,0:T(8,128)(2,1)} %get-tuple-element.52) | copy-start | bytes 884740
  16.0 1.7 %copy-start.24 = (bf16[288,512]{1,0:T(8,128)(2,1)S(1)}, bf16[288,512]{1,0:T(8,128)(2,1)}, u32[]{:S(2)}) copy-start(bf16[288,512]{1,0:T(8,128)(2,1)} %get-tuple-element.53) | copy-start | bytes 884740
  16.0 1.8 %copy-start.25 = (bf16[288,512]{1,0:T(8,128)(2,1)S(1)}, bf16[288,512]{1,0:T(8,128)(2,1)}, u32[]{:S(2)}) copy-start(bf16[288,512]{1,0:T(8,128)(2,1)} %get-tuple-element.54) | copy-start | bytes 884740
  21.9 6.4 %copy-start.2 = (bf16[528,512]{1,0:T(8,128)(2,1)}, bf16[528,512]{1,0:T(8,128)(2,1)S(1)}, u32[]{:S(2)}) copy-start(bf16[528,512]{1,0:T(8,128)(2,1)S(1)} %collective-permute-done.refs_1_) | copy-start | bytes 1622020
  23.2 5.1 %copy-start = (bf16[512,768]{1,0:T(8,128)(2,1)}, bf16[512,768]{1,0:T(8,128)(2,1)S(1)}, u32[]{:S(2)}) copy-start(bf16[512,768]{1,0:T(8,128)(2,1)S(1)} %collective-permute-done.2.refs_3_) | copy-start | bytes 2359300
  23.2 28.3 %collective-permute-start.5 = (bf16[288,2048]{1,0:T(8,128)(2,1)S(1)}, bf16[288,2048]{1,0:T(8,128)(2,1)S(1)}, u32[]{:S(2)}, u32[]{:S(2)}) collective-permute-start(bf16[288,2048]{1,0:T(8,128)(2,1)S(1)} %get-tuple-element.28), channel_id=1, source_target_pairs={{0,8},{1,9},{2,10},{3,11},{4,12},{5,13},{6,14},{7,15},{8,0},{9,1},... | collective-permute-start | bytes 3538952 | tf_op jit(solution)/shard_map/ppermute | solution.py:37
  24.5 28.2 %collective-permute-start.6 = (bf16[288,2048]{1,0:T(8,128)(2,1)S(1)}, bf16[288,2048]{1,0:T(8,128)(2,1)S(1)}, u32[]{:S(2)}, u32[]{:S(2)}) collective-permute-start(bf16[288,2048]{1,0:T(8,128)(2,1)S(1)} %get-tuple-element.29), channel_id=1, source_target_pairs={{0,16},{1,17},{2,18},{3,19},{4,20},{5,21},{6,22},{7,23},{8,24},{9,... | collective-permute-start | bytes 3538952 | tf_op jit(solution)/shard_map/ppermute | solution.py:37
  25.8 29.1 %collective-permute-start.7 = (bf16[288,2048]{1,0:T(8,128)(2,1)S(1)}, bf16[288,2048]{1,0:T(8,128)(2,1)S(1)}, u32[]{:S(2)}, u32[]{:S(2)}) collective-permute-start(bf16[288,2048]{1,0:T(8,128)(2,1)S(1)} %pad_maximum_fusion.2), channel_id=1, source_target_pairs={{0,28},{1,29},{2,30},{3,31},{4,24},{5,25},{6,26},{7,27},{8,20},{9,... | collective-permute-start | bytes 3538952 | tf_op jit(solution)/shard_map/ppermute | solution.py:37
  28.1 4.7 %copy-start.15 = (bf16[288,512]{1,0:T(8,128)(2,1)S(1)}, bf16[288,512]{1,0:T(8,128)(2,1)}, u32[]{:S(2)}) copy-start(bf16[288,512]{1,0:T(8,128)(2,1)} %get-tuple-element.39) | copy-start | bytes 884740
  28.1 4.6 %copy-start.16 = (bf16[288,512]{1,0:T(8,128)(2,1)S(1)}, bf16[288,512]{1,0:T(8,128)(2,1)}, u32[]{:S(2)}) copy-start(bf16[288,512]{1,0:T(8,128)(2,1)} %get-tuple-element.40) | copy-start | bytes 884740
  28.1 4.6 %copy-start.17 = (bf16[288,512]{1,0:T(8,128)(2,1)S(1)}, bf16[288,512]{1,0:T(8,128)(2,1)}, u32[]{:S(2)}) copy-start(bf16[288,512]{1,0:T(8,128)(2,1)} %get-tuple-element.41) | copy-start | bytes 884740
  28.1 4.6 %copy-start.18 = (bf16[288,512]{1,0:T(8,128)(2,1)S(1)}, bf16[288,512]{1,0:T(8,128)(2,1)}, u32[]{:S(2)}) copy-start(bf16[288,512]{1,0:T(8,128)(2,1)} %get-tuple-element.42) | copy-start | bytes 884740
  28.3 23.3 %copy-start.1 = (bf16[512,768]{1,0:T(8,128)(2,1)S(1)}, bf16[512,768]{1,0:T(8,128)(2,1)}, u32[]{:S(2)}) copy-start(bf16[512,768]{1,0:T(8,128)(2,1)} %copy-done) | copy-start | bytes 2359300
  28.3 23.2 %collective-permute-start.3 = (bf16[896,512]{1,0:T(8,128)(2,1)S(1)}, bf16[896,512]{1,0:T(8,128)(2,1)S(1)}, u32[]{:S(2)}, u32[]{:S(2)}) collective-permute-start(bf16[896,512]{1,0:T(8,128)(2,1)S(1)} %get-tuple-element.60), channel_id=1, source_target_pairs={{0,32},{1,33},{2,34},{3,35},{4,36},{5,37},{6,38},{7,39},{8,40},{9,... | collective-permute-start | bytes 2752520 | tf_op jit(solution)/shard_map/ppermute | solution.py:37
  29.3 22.2 %collective-permute-start.4 = (bf16[896,512]{1,0:T(8,128)(2,1)S(1)}, bf16[896,512]{1,0:T(8,128)(2,1)S(1)}, u32[]{:S(2)}, u32[]{:S(2)}) collective-permute-start(bf16[896,512]{1,0:T(8,128)(2,1)S(1)} %get-tuple-element.59), channel_id=1, source_target_pairs={{0,96},{1,97},{2,98},{3,99},{4,100},{5,101},{6,102},{7,103},{8,104... | collective-permute-start | bytes 2752520 | tf_op jit(solution)/shard_map/ppermute | solution.py:37
  32.9 30.7 %copy-start.5 = (bf16[288,2048]{1,0:T(8,128)(2,1)}, bf16[288,2048]{1,0:T(8,128)(2,1)S(1)}, u32[]{:S(2)}) copy-start(bf16[288,2048]{1,0:T(8,128)(2,1)S(1)} %pad_maximum_fusion.3.refs_0_) | copy-start | bytes 3538948
  56.2 3.5 %collective-permute-start.10 = (bf16[288,768]{1,0:T(8,128)(2,1)S(1)}, bf16[288,768]{1,0:T(8,128)(2,1)S(1)}, u32[]{:S(2)}, u32[]{:S(2)}) collective-permute-start(bf16[288,768]{1,0:T(8,128)(2,1)S(1)} %shard_map.84), channel_id=1, source_target_pairs={{0,8},{1,9},{2,10},{3,11},{4,12},{5,13},{6,14},{7,15},{8,0},{9,1},... | collective-permute-start | bytes 1327112 | tf_op jit(solution)/shard_map/ppermute | solution.py:37
  56.6 7.0 %collective-permute-start.8 = (bf16[288,768]{1,0:T(8,128)(2,1)S(1)}, bf16[288,768]{1,0:T(8,128)(2,1)S(1)}, u32[]{:S(2)}, u32[]{:S(2)}) collective-permute-start(bf16[288,768]{1,0:T(8,128)(2,1)S(1)} %shard_map.82), channel_id=1, source_target_pairs={{0,8},{1,9},{2,10},{3,11},{4,12},{5,13},{6,14},{7,15},{8,0},{9,1},... | collective-permute-start | bytes 1327112 | tf_op jit(solution)/shard_map/ppermute | solution.py:37
  56.8 9.0 %collective-permute-start.12 = (bf16[256,512]{1,0:T(8,128)(2,1)S(1)}, bf16[256,512]{1,0:T(8,128)(2,1)S(1)}, u32[]{:S(2)}, u32[]{:S(2)}) collective-permute-start(bf16[256,512]{1,0:T(8,128)(2,1)S(1)} %slice.86), channel_id=1, source_target_pairs={{0,32},{1,33},{2,34},{3,35},{4,36},{5,37},{6,38},{7,39},{8,40},{9,... | collective-permute-start | bytes 786440 | tf_op jit(solution)/shard_map/ppermute | solution.py:37
  57.9 7.9 %collective-permute-start.13 = (bf16[256,512]{1,0:T(8,128)(2,1)S(1)}, bf16[256,512]{1,0:T(8,128)(2,1)S(1)}, u32[]{:S(2)}, u32[]{:S(2)}) collective-permute-start(bf16[256,512]{1,0:T(8,128)(2,1)S(1)} %slice.87), channel_id=1, source_target_pairs={{0,96},{1,97},{2,98},{3,99},{4,100},{5,101},{6,102},{7,103},{8,104... | collective-permute-start | bytes 786440 | tf_op jit(solution)/shard_map/ppermute | solution.py:37
  61.7 4.1 %copy-start.3 = (bf16[528,512]{1,0:T(8,128)(2,1)S(1)}, bf16[528,512]{1,0:T(8,128)(2,1)}, u32[]{:S(2)}) copy-start(bf16[528,512]{1,0:T(8,128)(2,1)} %copy-done.2) | copy-start | bytes 1622020
  61.7 27.4 %collective-permute-start.11 = (bf16[288,768]{1,0:T(8,128)(2,1)}, bf16[288,768]{1,0:T(8,128)(2,1)}, u32[]{:S(2)}, u32[]{:S(2)}) collective-permute-start(bf16[288,768]{1,0:T(8,128)(2,1)} %shard_map.85), channel_id=1, source_target_pairs={{0,20},{1,21},{2,22},{3,23},{4,16},{5,17},{6,18},{7,19},{8,28},{9,... | collective-permute-start | bytes 1327112 | tf_op jit(solution)/shard_map/ppermute | solution.py:37
  65.6 23.5 %collective-permute-start.9 = (bf16[288,768]{1,0:T(8,128)(2,1)}, bf16[288,768]{1,0:T(8,128)(2,1)}, u32[]{:S(2)}, u32[]{:S(2)}) collective-permute-start(bf16[288,768]{1,0:T(8,128)(2,1)} %shard_map.83), channel_id=1, source_target_pairs={{0,4},{1,5},{2,6},{3,7},{4,0},{5,1},{6,2},{7,3},{8,12},{9,13},{10,... | collective-permute-start | bytes 1327112 | tf_op jit(solution)/shard_map/ppermute | solution.py:37
  65.8 5.5 %copy-start.7 = (bf16[256,512]{1,0:T(8,128)(2,1)}, bf16[256,512]{1,0:T(8,128)(2,1)S(1)}, u32[]{:S(2)}) copy-start(bf16[256,512]{1,0:T(8,128)(2,1)S(1)} %collective-permute-done.12.refs_4_) | copy-start | bytes 786436
  65.8 5.4 %copy-start.9 = (bf16[256,512]{1,0:T(8,128)(2,1)}, bf16[256,512]{1,0:T(8,128)(2,1)S(1)}, u32[]{:S(2)}) copy-start(bf16[256,512]{1,0:T(8,128)(2,1)S(1)} %collective-permute-done.13.refs_5_) | copy-start | bytes 786436
  67.3 7.6 %collective-permute-start.14 = (bf16[288,512]{1,0:T(8,128)(2,1)}, bf16[288,512]{1,0:T(8,128)(2,1)}, u32[]{:S(2)}, u32[]{:S(2)}) collective-permute-start(bf16[288,512]{1,0:T(8,128)(2,1)} %shard_map.86), channel_id=1, source_target_pairs={{0,8},{1,9},{2,10},{3,11},{4,12},{5,13},{6,14},{7,15},{8,0},{9,1},... | collective-permute-start | bytes 884744 | tf_op jit(solution)/shard_map/ppermute | solution.py:37
  69.9 5.0 %copy-start.4 = (bf16[528,512]{1,0:T(8,128)(2,1)S(1)}, bf16[528,512]{1,0:T(8,128)(2,1)}, u32[]{:S(2)}) copy-start(bf16[528,512]{1,0:T(8,128)(2,1)} %copy-done.2) | copy-start | bytes 1622020
  69.9 5.0 %copy-start.6 = (bf16[288,2048]{1,0:T(8,128)(2,1)S(1)}, bf16[288,2048]{1,0:T(8,128)(2,1)}, u32[]{:S(2)}) copy-start(bf16[288,2048]{1,0:T(8,128)(2,1)} %copy-done.5) | copy-start | bytes 3538948
  69.9 15.7 %collective-permute-start.16 = (bf16[288,512]{1,0:T(8,128)(2,1)}, bf16[288,512]{1,0:T(8,128)(2,1)}, u32[]{:S(2)}, u32[]{:S(2)}) collective-permute-start(bf16[288,512]{1,0:T(8,128)(2,1)} %shard_map.89), channel_id=1, source_target_pairs={{0,24},{1,25},{2,26},{3,27},{4,28},{5,29},{6,30},{7,31},{8,16},{9,... | collective-permute-start | bytes 884744 | tf_op jit(solution)/shard_map/ppermute | solution.py:37
  72.8 16.4 %collective-permute-start.15 = (bf16[288,512]{1,0:T(8,128)(2,1)}, bf16[288,512]{1,0:T(8,128)(2,1)}, u32[]{:S(2)}, u32[]{:S(2)}) collective-permute-start(bf16[288,512]{1,0:T(8,128)(2,1)} %shard_map.88), channel_id=1, source_target_pairs={{0,16},{1,17},{2,18},{3,19},{4,20},{5,21},{6,22},{7,23},{8,24},{9,... | collective-permute-start | bytes 884744 | tf_op jit(solution)/shard_map/ppermute | solution.py:37
  74.9 1.0 copy-start.8
  75.9 0.9 copy-start.10
  76.8 0.7 copy-start.14
  77.5 11.7 %copy-start.11 = (f32[288,256]{1,0:T(8,128)S(1)}, f32[288,256]{1,0:T(8,128)}, u32[]{:S(2)}) copy-start(f32[288,256]{1,0:T(8,128)} %pad_maximum_fusion.7) | copy-start | bytes 884740
  77.5 11.7 %copy-start.12 = (bf16[256,256]{1,0:T(8,128)(2,1)S(1)}, bf16[256,256]{1,0:T(8,128)(2,1)}, u32[]{:S(2)}) copy-start(bf16[256,256]{1,0:T(8,128)(2,1)} %maximum_maximum_fusion.turn) | copy-start | bytes 393220
  77.5 11.7 %copy-start.13 = (s32[144,1]{1,0:T(8,128)S(1)}, s32[144,1]{1,0:T(8,128)}, u32[]{:S(2)}) copy-start(s32[144,1]{1,0:T(8,128)} %copy.13.lengths) | copy-start | bytes 1732

commit v4 on v3

--- a/solution.py
+++ b/solution.py
@@ -330,25 +330,27 @@
     second = jnp.concatenate([w_keyval[:, 0], w_keyval[:, 1], w_query[:, early:]], axis=1)
     second_bias = jnp.concatenate([b_keyval[0], b_keyval[1], b_query[early:]])
     second_bias = jnp.broadcast_to(second_bias[None], (16, second_bias.shape[0]))
+
+    second = jnp.concatenate([second, second_bias], axis=0)
+    second, tokens = lax.optimization_barrier((second, tokens))
     slab = slabs(tokens)
-
     below, above = moved(first, z_by(1)), moved(first, z_by(-1))
-    shifted = moved(jnp.concatenate([second, second_bias], axis=0), far_y)
-    shifted, below, above, out01, out10, out11 = lax.optimization_barrier(
-        (shifted, below, above, slab(0, 1, ALL_Z), slab(1, 0, ALL_Z), slab(1, 1, ALL_Z))
+    shifted = moved(second, far_y)
+    rows10 = moved(slab(1, 0, ALL_Z), inner_y)
+    rows11 = moved(slab(1, 1, ALL_Z), cross_y_core)
+    shifted, below, above, out01 = lax.optimization_barrier(
+        (shifted, below, above, slab(0, 1, ALL_Z))
     )
     up = moved(packed(below[:half], shifted[:depth]), z_by(1))
     down = moved(packed(above[half:], shifted[:depth]), z_by(-1))
     rows01 = moved(out01, other_core)
-    rows10 = moved(out10, inner_y)
-    rows11 = moved(out11, cross_y_core)
     up, down, rows00, tables = lax.optimization_barrier(
         (up, down, slab(0, 0, ALL_Z), tables)
     )
     far_up = moved(up[:half], z_by(1))
     far_down = moved(down[half:depth], z_by(-1))
 
-    width, rest = second.shape[1], early - second.shape[1]
+    width, rest = shifted.shape[1], early - shifted.shape[1]
     tiles = []
     for column in range(0, early, TILE):
         spans = [(i, 0, column, depth) for i in range(3)]
@@ -368,7 +370,6 @@
     same = product([rows00], weights, tiles, jnp.bfloat16, theirs0, first_bias)
     other = product([rows10], weights, tiles, jnp.bfloat16, theirs1)
     first_parts = moved(same, far_y), moved(other, cross_y)
-    far_up, far_down, _, _ = lax.optimization_barrier((far_up, far_down, same, other))
 
     tiles = []
     for column in range(0, width, TILE):

time: 99.9 us -> 96.9 us (0.970)
  waiting for transfers between devices: 36 us -> 25.6 us
  Pallas kernels: 22.4 us -> 27.5 us
  starting transfers between devices: 23.2 us -> 25.4 us
  other arithmetic: 5.25 us -> 7.07 us
  local copies, waits for them, and re-layouts: 11.5 us -> 10.3 us
    ppermute x17, waiting for transfers between devices: 36 us -> 25.6 us  [moved(): return lax.ppermute(value, AXES, pairs)]
    pallas_call x8, Pallas kernels: 12.7 us -> 17.8 us  [product(): pl.pallas_call(functools.partial(product_kernel, len(rows), len(weights),...]
    ppermute x17, starting transfers between devices: 23.2 us -> 25.4 us  [moved(): return lax.ppermute(value, AXES, pairs)]
    concatenate x3 -> x4, other arithmetic: 1.89 us -> 3.75 us  [slab(): return jnp.concatenate(parts, axis=1)]
    unnamed x62 -> x48, local copies, waits for them, and re-layouts: 2.95 us -> 2.65 us
  transfers between devices with their start and end apart: 17 -> 17, of which waited for: 7 -> 4; matrix products, arithmetic and copies ran while one was open for 13% -> 14% of each run, Pallas kernels for 12% -> 18%
where the time goes in v4:
time: 96.9 us; the launch traced here: 96.5 us
  Pallas kernels  27.5 us (28%)
  waiting for transfers between devices  25.6 us (26%)
  starting transfers between devices  25.4 us (26%)
  local copies, waits for them, and re-layouts  10.3 us (11%)
  other arithmetic  7.07 us (7%)
    ppermute x17, waiting for transfers between devices, moved(): return lax.ppermute(value, AXES, pairs)  25.6 us
    ppermute x17, starting transfers between devices, moved(): return lax.ppermute(value, AXES, pairs)  25.4 us
    pallas_call x8, Pallas kernels, product(): pl.pallas_call(functools.partial(product_kernel, len(rows), len(weights),...  17.8 us
    pallas_call x1, Pallas kernels, attention(): pl.pallas_call(attention_kernel, out_shape=jax.ShapeDtypeStruct((steps, r...  9.69 us
    concatenate x4, other arithmetic, slab(): return jnp.concatenate(parts, axis=1)  3.75 us
    dynamic_slice x1, local copies, waits for them, and re-layouts, slab(): parts.append(lax.dynamic_slice_in_dim(flat, block * share, share, 1))  3.68 us
    unnamed x48, local copies, waits for them, and re-layouts  2.65 us
  transfers between devices with their start and end apart: 17, of which 4 were waited for; matrix products, arithmetic and copies ran while one was open for 14% of the time, Pallas kernels for 18%

profile of v4, /device:TPU:1, one launch (start us, length us, event | category | flops | bytes accessed | tf_op | source)
XLA Modules:
  0.0 96.5 jit_solution(2142619193203487582)
XLA Ops:
  0.0 1.2 %slice.75.refs_1_ = bf16[512,768]{1,0:T(8,128)(2,1)S(1)} slice(bf16[512,1024]{1,0:T(8,128)(2,1)} %param.9), slice={[0:512], [0:768]} | slice | bytes 1572864 | tf_op jit(solution)/shard_map/slice | solution.py:329
  1.3 2.5 %collective-permute-start.1 = (bf16[512,768]{1,0:T(8,128)(2,1)S(1)}, bf16[512,768]{1,0:T(8,128)(2,1)S(1)}, u32[]{:S(2)}, u32[]{:S(2)}) collective-permute-start(bf16[512,768]{1,0:T(8,128)(2,1)S(1)} %slice.75.refs_1_), channel_id=1, source_target_pairs={{0,32},{1,33},{2,34},{3,35},{4,36},{5,37},{6,38},{7,39},{8,40},{9,... | collective-permute-start | bytes 2359304 | tf_op jit(solution)/shard_map/ppermute | solution.py:37
  3.8 2.2 %collective-permute-start.2 = (bf16[512,768]{1,0:T(8,128)(2,1)S(1)}, bf16[512,768]{1,0:T(8,128)(2,1)S(1)}, u32[]{:S(2)}, u32[]{:S(2)}) collective-permute-start(bf16[512,768]{1,0:T(8,128)(2,1)S(1)} %slice.75.refs_1_), channel_id=1, source_target_pairs={{0,96},{1,97},{2,98},{3,99},{4,100},{5,101},{6,102},{7,103},{8,104... | collective-permute-start | bytes 2359304 | tf_op jit(solution)/shard_map/ppermute | solution.py:37
  6.0 0.4 fusion.5
  6.5 0.8 pad_maximum_fusion.6
  7.3 2.9 %collective-permute-start = (bf16[528,512]{1,0:T(8,128)(2,1)}, bf16[528,512]{1,0:T(8,128)(2,1)S(1)}, u32[]{:S(2)}, u32[]{:S(2)}) collective-permute-start(bf16[528,512]{1,0:T(8,128)(2,1)} %pad_maximum_fusion.6), channel_id=1, source_target_pairs={{0,4},{1,5},{2,6},{3,7},{4,0},{5,1},{6,2},{7,3},{8,12},{9,13},{10,... | collective-permute-start | bytes 1622024 | tf_op jit(solution)/shard_map/ppermute | solution.py:37
  10.3 3.7 %constant_dynamic-slice_fusion.3 = (bf16[288,512]{1,0:T(8,128)(2,1)S(1)}, bf16[288,512]{1,0:T(8,128)(2,1)S(1)}, bf16[288,512]{1,0:T(8,128)(2,1)S(1)}, bf16[288,5...) fusion(bf16[288,8192]{1,0:T(8,128)(2,1)} %bitcast.19, ...), kind=kLoop, calls=%fused_computation.21 | loop fusion | bytes 9437248 | tf_op jit(solution)/shard_map/dynamic_slice | solution.py:272
  13.9 0.0 copy-start.23
  14.0 1.2 %pad_maximum_fusion.2 = bf16[288,2048]{1,0:T(8,128)(2,1)} fusion(bf16[288,512]{1,0:T(8,128)(2,1)S(1)} %get-tuple-element.39, bf16[288,512]{1,0:T(8,128)(2,1)S(1)} %get-tuple-element.40, bf16[288,512]{1,0:T(8,128)(2,1)S(1)} %get-tuple-element.41, bf16[288,512]{1,0:T(8,128)(2,1)S(1)} %get-tuple-element.42), kind=kLoop, calls=%fused_computation.2 | loop fusion | flops 4718592 | bytes 2359296 | tf_op jit(solution)/shard_map/concatenate | solution.py:273
  15.1 0.4 collective-permute-start.6
  15.5 1.2 %pad_maximum_fusion.3 = bf16[288,2048]{1,0:T(8,128)(2,1)} fusion(bf16[288,512]{1,0:T(8,128)(2,1)S(1)} %get-tuple-element.36, bf16[288,512]{1,0:T(8,128)(2,1)S(1)} %get-tuple-element.37, bf16[288,512]{1,0:T(8,128)(2,1)S(1)} %get-tuple-element.38, bf16[288,512]{1,0:T(8,128)(2,1)S(1)} %get-tuple-element.35), kind=kLoop, calls=%fused_computation.3 | loop fusion | flops 4718592 | bytes 2359296 | tf_op jit(solution)/shard_map/concatenate | solution.py:273
  16.7 1.5 %collective-permute-start.7 = (bf16[288,2048]{1,0:T(8,128)(2,1)}, bf16[288,2048]{1,0:T(8,128)(2,1)}, u32[]{:S(2)}, u32[]{:S(2)}) collective-permute-start(bf16[288,2048]{1,0:T(8,128)(2,1)} %pad_maximum_fusion.3), channel_id=1, source_target_pairs={{0,28},{1,29},{2,30},{3,31},{4,24},{5,25},{6,26},{7,27},{8,20},{9,... | collective-permute-start | bytes 3538952 | tf_op jit(solution)/shard_map/ppermute | solution.py:37
  18.2 0.1 add.230
  18.3 0.1 add.232
  18.4 0.1 slice_negate_fusion
  18.5 0.7 maximum_maximum_fusion.turn
  19.3 1.3 %pad_maximum_fusion = bf16[288,2048]{1,0:T(8,128)(2,1)S(1)} fusion(bf16[288,512]{1,0:T(8,128)(2,1)S(1)} %get-tuple-element.47, bf16[288,512]{1,0:T(8,128)(2,1)} %get-tuple-element.48, bf16[288,512]{1,0:T(8,128)(2,1)} %get-tuple-element.49, bf16[288,512]{1,0:T(8,128)(2,1)} %get-tuple-element.50), kind=kLoop, calls=%fused_computation | loop fusion | flops 4718592 | bytes 2359296 | tf_op jit(solution)/shard_map/concatenate | solution.py:273
  20.5 1.3 %collective-permute-done.refs_1_ = bf16[528,512]{1,0:T(8,128)(2,1)S(1)} collective-permute-done((bf16[528,512]{1,0:T(8,128)(2,1)}, bf16[528,512]{1,0:T(8,128)(2,1)S(1)}, u32[]{:S(2)}, u32[]{:S(2)}) %collective-permute-start) | collective-permute-done | bytes 540704 | tf_op jit(solution)/shard_map/ppermute | solution.py:37
  21.9 1.4 %collective-permute-done.1.refs_2_ = bf16[512,768]{1,0:T(8,128)(2,1)S(1)} collective-permute-done((bf16[512,768]{1,0:T(8,128)(2,1)S(1)}, bf16[512,768]{1,0:T(8,128)(2,1)S(1)}, u32[]{:S(2)}, u32[]{:S(2)}) %collective-permute-start.1) | collective-permute-done | bytes 786464 | tf_op jit(solution)/shard_map/ppermute | solution.py:37
  23.3 0.0 collective-permute-done.2.refs_3_
  23.3 2.0 %collective-permute-start.5 = (bf16[288,2048]{1,0:T(8,128)(2,1)S(1)}, bf16[288,2048]{1,0:T(8,128)(2,1)S(1)}, u32[]{:S(2)}, u32[]{:S(2)}) collective-permute-start(bf16[288,2048]{1,0:T(8,128)(2,1)S(1)} %pad_maximum_fusion), channel_id=1, source_target_pairs={{0,8},{1,9},{2,10},{3,11},{4,12},{5,13},{6,14},{7,15},{8,0},{9,1},... | collective-permute-start | bytes 3538952 | tf_op jit(solution)/shard_map/ppermute | solution.py:37
  25.5 0.1 fusion.1
  25.7 0.2 collective-permute-start.3
  25.9 2.5 %collective-permute-start.4 = (bf16[896,512]{1,0:T(8,128)(2,1)S(1)}, bf16[896,512]{1,0:T(8,128)(2,1)S(1)}, u32[]{:S(2)}, u32[]{:S(2)}) collective-permute-start(bf16[896,512]{1,0:T(8,128)(2,1)S(1)} %get-tuple-element.55), channel_id=1, source_target_pairs={{0,96},{1,97},{2,98},{3,99},{4,100},{5,101},{6,102},{7,103},{8,104... | collective-permute-start | bytes 2752520 | tf_op jit(solution)/shard_map/ppermute | solution.py:37
  28.4 0.6 multiply_cosine_fusion
  29.0 0.9 pad_maximum_fusion.7
  29.9 0.1 pad_maximum_fusion.1.refs_0_
  30.1 18.3 %collective-permute-done.3.refs_4_.refs_2_ = bf16[896,512]{1,0:T(8,128)(2,1)S(1)} collective-permute-done((bf16[896,512]{1,0:T(8,128)(2,1)S(1)}, bf16[896,512]{1,0:T(8,128)(2,1)S(1)}, u32[]{:S(2)}, u32[]{:S(2)}) %collective-permute-start.3) | collective-permute-done | bytes 917536 | tf_op jit(solution)/shard_map/ppermute | solution.py:37
  48.4 0.0 collective-permute-done.4.refs_5_.refs_3_
  48.4 0.0 collective-permute-done.5.refs_0_
  48.4 1.2 %shard_map.82 = bf16[288,768]{1,0:T(8,128)(2,1)S(1)} custom-call(bf16[288,2048]{1,0:T(8,128)(2,1)S(1)} %collective-permute-done.5.refs_0_, bf16[512,768]{1,0:T(8,128)(2,1)S(1)} %slice.75.refs_1_, bf16[512,768]{1,0:T(8,128)(2,1)S(1)} %collective-permute-done.1.refs_2_, bf16[512,768]{1,0:T(8,128)(2,1)S(1)} %copy-done.1, ...), custom_call_target="tpu_custom_call" | custom-call | flops 1 | bytes 1 | tf_op jit(solution)/shard_map/pallas_call | solution.py:302
  49.6 0.0 collective-permute-done.6.refs_0_
  49.6 0.0 collective-permute-done.7.refs_0_
  49.6 1.4 %collective-permute-start.8 = (bf16[288,768]{1,0:T(8,128)(2,1)S(1)}, bf16[288,768]{1,0:T(8,128)(2,1)S(1)}, u32[]{:S(2)}, u32[]{:S(2)}) collective-permute-start(bf16[288,768]{1,0:T(8,128)(2,1)S(1)} %shard_map.82), channel_id=1, source_target_pairs={{0,8},{1,9},{2,10},{3,11},{4,12},{5,13},{6,14},{7,15},{8,0},{9,1},... | collective-permute-start | bytes 1327112 | tf_op jit(solution)/shard_map/ppermute | solution.py:37
  51.0 2.4 %shard_map.84 = bf16[288,768]{1,0:T(8,128)(2,1)S(1)} custom-call(bf16[288,2048]{1,0:T(8,128)(2,1)} %collective-permute-done.7.refs_0_, bf16[512,768]{1,0:T(8,128)(2,1)S(1)} %slice.75.refs_1_, bf16[512,768]{1,0:T(8,128)(2,1)S(1)} %collective-permute-done.1.refs_2_, bf16[512,768]{1,0:T(8,128)(2,1)S(1)} %copy-done.1, ...), custom_call_target="tpu_custom_call" | custom-call | flops 1 | bytes 1 | tf_op jit(solution)/shard_map/pallas_call | solution.py:302
  53.5 0.1 collective-permute-start.10
  53.6 0.3 collective-permute-start.12
  54.0 2.5 %collective-permute-start.13 = (bf16[256,512]{1,0:T(8,128)(2,1)S(1)}, bf16[256,512]{1,0:T(8,128)(2,1)S(1)}, u32[]{:S(2)}, u32[]{:S(2)}) collective-permute-start(bf16[256,512]{1,0:T(8,128)(2,1)S(1)} %slice.87), channel_id=1, source_target_pairs={{0,96},{1,97},{2,98},{3,99},{4,100},{5,101},{6,102},{7,103},{8,104... | collective-permute-start | bytes 786440 | tf_op jit(solution)/shard_map/ppermute | solution.py:37
  56.4 0.0 collective-permute-done.8.refs_6_
  56.5 2.0 %shard_map.83 = bf16[288,768]{1,0:T(8,128)(2,1)} custom-call(bf16[288,2048]{1,0:T(8,128)(2,1)S(1)} %pad_maximum_fusion.1.refs_0_, bf16[512,768]{1,0:T(8,128)(2,1)S(1)} %slice.75.refs_1_, bf16[512,768]{1,0:T(8,128)(2,1)S(1)} %collective-permute-done.1.refs_2_, bf16[512,768]{1,0:T(8,128)(2,1)S(1)} %copy-done.1, ...), custom_call_target="tpu_custom_call" | custom-call | flops 1 | bytes 1 | tf_op jit(solution)/shard_map/pallas_call | solution.py:302
  58.4 3.0 %collective-permute-start.9 = (bf16[288,768]{1,0:T(8,128)(2,1)}, bf16[288,768]{1,0:T(8,128)(2,1)}, u32[]{:S(2)}, u32[]{:S(2)}) collective-permute-start(bf16[288,768]{1,0:T(8,128)(2,1)} %shard_map.83), channel_id=1, source_target_pairs={{0,4},{1,5},{2,6},{3,7},{4,0},{5,1},{6,2},{7,3},{8,12},{9,13},{10,... | collective-permute-start | bytes 1327112 | tf_op jit(solution)/shard_map/ppermute | solution.py:37
  61.4 0.0 collective-permute-done.10.refs_6_
  61.4 3.2 %shard_map.85 = bf16[288,768]{1,0:T(8,128)(2,1)} custom-call(bf16[288,2048]{1,0:T(8,128)(2,1)} %collective-permute-done.6.refs_0_, bf16[512,768]{1,0:T(8,128)(2,1)S(1)} %slice.75.refs_1_, bf16[512,768]{1,0:T(8,128)(2,1)S(1)} %collective-permute-done.1.refs_2_, bf16[512,768]{1,0:T(8,128)(2,1)S(1)} %copy-done.1, ...), custom_call_target="tpu_custom_call" | custom-call | flops 1 | bytes 1 | tf_op jit(solution)/shard_map/pallas_call | solution.py:302
  64.6 0.8 collective-permute-start.11
  65.4 0.0 collective-permute-done.12.refs_4_
  65.4 0.0 collective-permute-done.13.refs_5_
  65.5 1.5 %shard_map.86 = bf16[288,512]{1,0:T(8,128)(2,1)} custom-call(bf16[288,2048]{1,0:T(8,128)(2,1)S(1)} %collective-permute-done.5.refs_0_, bf16[528,512]{1,0:T(8,128)(2,1)S(1)} %copy-done.3, bf16[896,512]{1,0:T(8,128)(2,1)S(1)} %collective-permute-done.3.refs_4_.refs_2_, bf16[896,512]{1,0:T(8,128)(2,1)S(1)} %collective-permute-done.4.refs_5_.refs_3_, ...), custom_call_target="tpu_custom_call" | custom-call | flops 1 | bytes 1 | tf_op jit(solution)/shard_map/pallas_call | solution.py:302
  67.0 1.5 %collective-permute-start.14 = (bf16[288,512]{1,0:T(8,128)(2,1)}, bf16[288,512]{1,0:T(8,128)(2,1)}, u32[]{:S(2)}, u32[]{:S(2)}) collective-permute-start(bf16[288,512]{1,0:T(8,128)(2,1)} %shard_map.86), channel_id=1, source_target_pairs={{0,8},{1,9},{2,10},{3,11},{4,12},{5,13},{6,14},{7,15},{8,0},{9,1},... | collective-permute-start | bytes 884744 | tf_op jit(solution)/shard_map/ppermute | solution.py:37
  68.5 2.8 %shard_map.88 = bf16[288,512]{1,0:T(8,128)(2,1)} custom-call(bf16[288,2048]{1,0:T(8,128)(2,1)} %collective-permute-done.6.refs_0_, bf16[528,512]{1,0:T(8,128)(2,1)S(1)} %copy-done.3, bf16[896,512]{1,0:T(8,128)(2,1)S(1)} %collective-permute-done.3.refs_4_.refs_2_, bf16[896,512]{1,0:T(8,128)(2,1)S(1)} %collective-permute-done.4.refs_5_.refs_3_, ...), custom_call_target="tpu_custom_call" | custom-call | flops 1 | bytes 1 | tf_op jit(solution)/shard_map/pallas_call | solution.py:302
  71.3 0.0 collective-permute-start.15
  71.3 2.9 %shard_map.89 = bf16[288,512]{1,0:T(8,128)(2,1)} custom-call(bf16[288,2048]{1,0:T(8,128)(2,1)} %collective-permute-done.7.refs_0_, bf16[528,512]{1,0:T(8,128)(2,1)S(1)} %copy-done.3, bf16[896,512]{1,0:T(8,128)(2,1)S(1)} %collective-permute-done.3.refs_4_.refs_2_, bf16[896,512]{1,0:T(8,128)(2,1)S(1)} %collective-permute-done.4.refs_5_.refs_3_, ...), custom_call_target="tpu_custom_call" | custom-call | flops 1 | bytes 1 | tf_op jit(solution)/shard_map/pallas_call | solution.py:302
  74.2 1.5 %collective-permute-start.16 = (bf16[288,512]{1,0:T(8,128)(2,1)}, bf16[288,512]{1,0:T(8,128)(2,1)}, u32[]{:S(2)}, u32[]{:S(2)}) collective-permute-start(bf16[288,512]{1,0:T(8,128)(2,1)} %shard_map.89), channel_id=1, source_target_pairs={{0,24},{1,25},{2,26},{3,27},{4,28},{5,29},{6,30},{7,31},{8,16},{9,... | collective-permute-start | bytes 884744 | tf_op jit(solution)/shard_map/ppermute | solution.py:37
  75.7 0.6 slice.88.refs_7_
  76.3 1.4 %copy.13.lengths = s32[144,1]{1,0:T(8,128)} copy(s32[144,1]{0,1:T(1,128)} %bitcast.20) | data formatting | bytes 1152 | tf_op jit(solution)/shard_map/optimization_barrier | solution.py:347
  77.7 0.0 collective-permute-done.14.refs_6_
  77.7 0.9 copy-done.8
  78.6 0.9 copy-done.10
  79.6 0.7 copy-done.14
  80.3 1.8 %shard_map.87 = f32[288,512]{1,0:T(8,128)S(1)} custom-call(bf16[288,2048]{1,0:T(8,128)(2,1)S(1)} %copy-done.6, bf16[528,512]{1,0:T(8,128)(2,1)S(1)} %copy-done.4, bf16[896,512]{1,0:T(8,128)(2,1)S(1)} %collective-permute-done.3.refs_4_.refs_2_, bf16[896,512]{1,0:T(8,128)(2,1)S(1)} %collective-permute-done.4.refs_5_.refs_3_, bf16[256,512]{1,0:T(8,128)(2,1)S(1)} %copy-done.8, ...), custom_call_target="tpu_custom_call" | custom-call | flops 1 | bytes 1 | tf_op jit(solution)/shard_map/pallas_call | solution.py:302
  82.1 0.0 collective-permute-done.15
  82.1 4.5 %collective-permute-done.16 = bf16[288,512]{1,0:T(8,128)(2,1)} collective-permute-done((bf16[288,512]{1,0:T(8,128)(2,1)}, bf16[288,512]{1,0:T(8,128)(2,1)}, u32[]{:S(2)}, u32[]{:S(2)}) %collective-permute-start.16) | collective-permute-done | bytes 294944 | tf_op jit(solution)/shard_map/ppermute | solution.py:37
  86.6 0.0 collective-permute-done.9
  86.6 0.0 collective-permute-done.11
  86.7 9.7 %shard_map.90 = bf16[2,144,1024]{2,1,0:T(8,128)(2,1)} custom-call(bf16[2,144,768]{2,1,0:T(8,128)(2,1)} %bitcast.6.same1, bf16[2,144,768]{2,1,0:T(8,128)(2,1)} %bitcast.7.other1, f32[2,144,512]{2,1,0:T(8,128)S(1)} %bitcast.17, bf16[2,144,512]{2,1,0:T(8,128)(2,1)} %bitcast.9.other2, bf16[2,144,512]{2,1,0:T(8,128)(2,1)} %bitcast.10.last2, ...), custom_call_target="tpu_custom_call" | custom-call | flops 301989888 | bytes 18874368 | tf_op jit(solution)/shard_map/pallas_call | solution.py:212
  (64 shorter events, 0.3 us)
Async XLA Ops:
  0.0 6.5 %slice-start = ((bf16[512,1024]{1,0:T(8,128)(2,1)}), bf16[512,256]{1,0:T(8,128)(2,1)S(1)}, s32[]{:S(2)}) async-start(bf16[512,1024]{1,0:T(8,128)(2,1)} %param.9), calls=%async_computation | async-start | bytes 524288 | tf_op jit(solution)/shard_map/slice | solution.py:330
  0.0 6.0 %copy-start.21 = (bf16[1024]{0:T(1024)(128)(2,1)S(1)}, bf16[1024]{0:T(1024)(128)(2,1)}, u32[]{:S(2)}) copy-start(bf16[1024]{0:T(1024)(128)(2,1)} %param.11) | copy-start | bytes 6148
  0.0 6.0 %copy-start.22 = (bf16[2,128]{1,0:T(2,128)(2,1)S(1)}, bf16[2,128]{1,0:T(2,128)(2,1)}, u32[]{:S(2)}) copy-start(bf16[2,128]{1,0:T(2,128)(2,1)} %param.12) | copy-start | bytes 1540
  0.0 6.0 %copy-start.19 = (bf16[512,2,128]{2,1,0:T(2,128)(2,1)S(1)}, bf16[512,2,128]{2,1,0:T(2,128)(2,1)}, u32[]{:S(2)}) copy-start(bf16[512,2,128]{2,1,0:T(2,128)(2,1)} %param.10) | copy-start | bytes 786436
  1.3 22.0 %collective-permute-start.1 = (bf16[512,768]{1,0:T(8,128)(2,1)S(1)}, bf16[512,768]{1,0:T(8,128)(2,1)S(1)}, u32[]{:S(2)}, u32[]{:S(2)}) collective-permute-start(bf16[512,768]{1,0:T(8,128)(2,1)S(1)} %slice.75.refs_1_), channel_id=1, source_target_pairs={{0,32},{1,33},{2,34},{3,35},{4,36},{5,37},{6,38},{7,39},{8,40},{9,... | collective-permute-start | bytes 2359304 | tf_op jit(solution)/shard_map/ppermute | solution.py:37
  3.8 19.5 %collective-permute-start.2 = (bf16[512,768]{1,0:T(8,128)(2,1)S(1)}, bf16[512,768]{1,0:T(8,128)(2,1)S(1)}, u32[]{:S(2)}, u32[]{:S(2)}) collective-permute-start(bf16[512,768]{1,0:T(8,128)(2,1)S(1)} %slice.75.refs_1_), channel_id=1, source_target_pairs={{0,96},{1,97},{2,98},{3,99},{4,100},{5,101},{6,102},{7,103},{8,104... | collective-permute-start | bytes 2359304 | tf_op jit(solution)/shard_map/ppermute | solution.py:37
  7.3 14.5 %collective-permute-start = (bf16[528,512]{1,0:T(8,128)(2,1)}, bf16[528,512]{1,0:T(8,128)(2,1)S(1)}, u32[]{:S(2)}, u32[]{:S(2)}) collective-permute-start(bf16[528,512]{1,0:T(8,128)(2,1)} %pad_maximum_fusion.6), channel_id=1, source_target_pairs={{0,4},{1,5},{2,6},{3,7},{4,0},{5,1},{6,2},{7,3},{8,12},{9,13},{10,... | collective-permute-start | bytes 1622024 | tf_op jit(solution)/shard_map/ppermute | solution.py:37
  13.9 4.3 %copy-start.20 = (s32[144]{0:T(256)S(1)}, s32[144]{0:T(256)}, u32[]{:S(2)}) copy-start(s32[144]{0:T(256)} %param.15) | copy-start | bytes 1732
  13.9 4.5 %copy-start.23 = (s32[128]{0:T(128)S(1)}, s32[128]{0:T(128)}, u32[]{:S(2)}) copy-start(s32[128]{0:T(128)} %param.13) | copy-start | bytes 1540
  15.1 34.5 %collective-permute-start.6 = (bf16[288,2048]{1,0:T(8,128)(2,1)}, bf16[288,2048]{1,0:T(8,128)(2,1)}, u32[]{:S(2)}, u32[]{:S(2)}) collective-permute-start(bf16[288,2048]{1,0:T(8,128)(2,1)} %pad_maximum_fusion.2), channel_id=1, source_target_pairs={{0,16},{1,17},{2,18},{3,19},{4,20},{5,21},{6,22},{7,23},{8,24},{9,... | collective-permute-start | bytes 3538952 | tf_op jit(solution)/shard_map/ppermute | solution.py:37
  16.7 32.9 %collective-permute-start.7 = (bf16[288,2048]{1,0:T(8,128)(2,1)}, bf16[288,2048]{1,0:T(8,128)(2,1)}, u32[]{:S(2)}, u32[]{:S(2)}) collective-permute-start(bf16[288,2048]{1,0:T(8,128)(2,1)} %pad_maximum_fusion.3), channel_id=1, source_target_pairs={{0,28},{1,29},{2,30},{3,31},{4,24},{5,25},{6,26},{7,27},{8,20},{9,... | collective-permute-start | bytes 3538952 | tf_op jit(solution)/shard_map/ppermute | solution.py:37
  21.9 3.7 %copy-start.2 = (bf16[528,512]{1,0:T(8,128)(2,1)}, bf16[528,512]{1,0:T(8,128)(2,1)S(1)}, u32[]{:S(2)}) copy-start(bf16[528,512]{1,0:T(8,128)(2,1)S(1)} %collective-permute-done.refs_1_) | copy-start | bytes 1622020
  23.3 2.3 %copy-start = (bf16[512,768]{1,0:T(8,128)(2,1)}, bf16[512,768]{1,0:T(8,128)(2,1)S(1)}, u32[]{:S(2)}) copy-start(bf16[512,768]{1,0:T(8,128)(2,1)S(1)} %collective-permute-done.2.refs_3_) | copy-start | bytes 2359300
  23.3 25.1 %collective-permute-start.5 = (bf16[288,2048]{1,0:T(8,128)(2,1)S(1)}, bf16[288,2048]{1,0:T(8,128)(2,1)S(1)}, u32[]{:S(2)}, u32[]{:S(2)}) collective-permute-start(bf16[288,2048]{1,0:T(8,128)(2,1)S(1)} %pad_maximum_fusion), channel_id=1, source_target_pairs={{0,8},{1,9},{2,10},{3,11},{4,12},{5,13},{6,14},{7,15},{8,0},{9,1},... | collective-permute-start | bytes 3538952 | tf_op jit(solution)/shard_map/ppermute | solution.py:37
  25.4 4.5 %copy-start.15 = (bf16[288,512]{1,0:T(8,128)(2,1)S(1)}, bf16[288,512]{1,0:T(8,128)(2,1)}, u32[]{:S(2)}) copy-start(bf16[288,512]{1,0:T(8,128)(2,1)} %get-tuple-element.43) | copy-start | bytes 884740
  25.5 4.5 %copy-start.16 = (bf16[288,512]{1,0:T(8,128)(2,1)S(1)}, bf16[288,512]{1,0:T(8,128)(2,1)}, u32[]{:S(2)}) copy-start(bf16[288,512]{1,0:T(8,128)(2,1)} %get-tuple-element.44) | copy-start | bytes 884740
  25.5 4.4 %copy-start.17 = (bf16[288,512]{1,0:T(8,128)(2,1)S(1)}, bf16[288,512]{1,0:T(8,128)(2,1)}, u32[]{:S(2)}) copy-start(bf16[288,512]{1,0:T(8,128)(2,1)} %get-tuple-element.45) | copy-start | bytes 884740
  25.5 4.4 %copy-start.18 = (bf16[288,512]{1,0:T(8,128)(2,1)S(1)}, bf16[288,512]{1,0:T(8,128)(2,1)}, u32[]{:S(2)}) copy-start(bf16[288,512]{1,0:T(8,128)(2,1)} %get-tuple-element.46) | copy-start | bytes 884740
  25.6 22.7 %copy-start.1 = (bf16[512,768]{1,0:T(8,128)(2,1)S(1)}, bf16[512,768]{1,0:T(8,128)(2,1)}, u32[]{:S(2)}) copy-start(bf16[512,768]{1,0:T(8,128)(2,1)} %copy-done) | copy-start | bytes 2359300
  25.7 22.7 %collective-permute-start.3 = (bf16[896,512]{1,0:T(8,128)(2,1)S(1)}, bf16[896,512]{1,0:T(8,128)(2,1)S(1)}, u32[]{:S(2)}, u32[]{:S(2)}) collective-permute-start(bf16[896,512]{1,0:T(8,128)(2,1)S(1)} %get-tuple-element.56), channel_id=1, source_target_pairs={{0,32},{1,33},{2,34},{3,35},{4,36},{5,37},{6,38},{7,39},{8,40},{9,... | collective-permute-start | bytes 2752520 | tf_op jit(solution)/shard_map/ppermute | solution.py:37
  25.9 22.5 %collective-permute-start.4 = (bf16[896,512]{1,0:T(8,128)(2,1)S(1)}, bf16[896,512]{1,0:T(8,128)(2,1)S(1)}, u32[]{:S(2)}, u32[]{:S(2)}) collective-permute-start(bf16[896,512]{1,0:T(8,128)(2,1)S(1)} %get-tuple-element.55), channel_id=1, source_target_pairs={{0,96},{1,97},{2,98},{3,99},{4,100},{5,101},{6,102},{7,103},{8,104... | collective-permute-start | bytes 2752520 | tf_op jit(solution)/shard_map/ppermute | solution.py:37
  30.1 26.4 %copy-start.5 = (bf16[288,2048]{1,0:T(8,128)(2,1)}, bf16[288,2048]{1,0:T(8,128)(2,1)S(1)}, u32[]{:S(2)}) copy-start(bf16[288,2048]{1,0:T(8,128)(2,1)S(1)} %pad_maximum_fusion.1.refs_0_) | copy-start | bytes 3538948
  49.6 6.8 %collective-permute-start.8 = (bf16[288,768]{1,0:T(8,128)(2,1)S(1)}, bf16[288,768]{1,0:T(8,128)(2,1)S(1)}, u32[]{:S(2)}, u32[]{:S(2)}) collective-permute-start(bf16[288,768]{1,0:T(8,128)(2,1)S(1)} %shard_map.82), channel_id=1, source_target_pairs={{0,8},{1,9},{2,10},{3,11},{4,12},{5,13},{6,14},{7,15},{8,0},{9,1},... | collective-permute-start | bytes 1327112 | tf_op jit(solution)/shard_map/ppermute | solution.py:37
  53.5 7.9 %collective-permute-start.10 = (bf16[288,768]{1,0:T(8,128)(2,1)S(1)}, bf16[288,768]{1,0:T(8,128)(2,1)S(1)}, u32[]{:S(2)}, u32[]{:S(2)}) collective-permute-start(bf16[288,768]{1,0:T(8,128)(2,1)S(1)} %shard_map.84), channel_id=1, source_target_pairs={{0,8},{1,9},{2,10},{3,11},{4,12},{5,13},{6,14},{7,15},{8,0},{9,1},... | collective-permute-start | bytes 1327112 | tf_op jit(solution)/shard_map/ppermute | solution.py:37
  53.6 11.8 %collective-permute-start.12 = (bf16[256,512]{1,0:T(8,128)(2,1)S(1)}, bf16[256,512]{1,0:T(8,128)(2,1)S(1)}, u32[]{:S(2)}, u32[]{:S(2)}) collective-permute-start(bf16[256,512]{1,0:T(8,128)(2,1)S(1)} %slice.86), channel_id=1, source_target_pairs={{0,32},{1,33},{2,34},{3,35},{4,36},{5,37},{6,38},{7,39},{8,40},{9,... | collective-permute-start | bytes 786440 | tf_op jit(solution)/shard_map/ppermute | solution.py:37
  54.0 11.5 %collective-permute-start.13 = (bf16[256,512]{1,0:T(8,128)(2,1)S(1)}, bf16[256,512]{1,0:T(8,128)(2,1)S(1)}, u32[]{:S(2)}, u32[]{:S(2)}) collective-permute-start(bf16[256,512]{1,0:T(8,128)(2,1)S(1)} %slice.87), channel_id=1, source_target_pairs={{0,96},{1,97},{2,98},{3,99},{4,100},{5,101},{6,102},{7,103},{8,104... | collective-permute-start | bytes 786440 | tf_op jit(solution)/shard_map/ppermute | solution.py:37
  58.4 7.0 %copy-start.3 = (bf16[528,512]{1,0:T(8,128)(2,1)S(1)}, bf16[528,512]{1,0:T(8,128)(2,1)}, u32[]{:S(2)}) copy-start(bf16[528,512]{1,0:T(8,128)(2,1)} %copy-done.2) | copy-start | bytes 1622020
  58.4 28.2 %collective-permute-start.9 = (bf16[288,768]{1,0:T(8,128)(2,1)}, bf16[288,768]{1,0:T(8,128)(2,1)}, u32[]{:S(2)}, u32[]{:S(2)}) collective-permute-start(bf16[288,768]{1,0:T(8,128)(2,1)} %shard_map.83), channel_id=1, source_target_pairs={{0,4},{1,5},{2,6},{3,7},{4,0},{5,1},{6,2},{7,3},{8,12},{9,13},{10,... | collective-permute-start | bytes 1327112 | tf_op jit(solution)/shard_map/ppermute | solution.py:37
  64.6 22.0 %collective-permute-start.11 = (bf16[288,768]{1,0:T(8,128)(2,1)}, bf16[288,768]{1,0:T(8,128)(2,1)}, u32[]{:S(2)}, u32[]{:S(2)}) collective-permute-start(bf16[288,768]{1,0:T(8,128)(2,1)} %shard_map.85), channel_id=1, source_target_pairs={{0,20},{1,21},{2,22},{3,23},{4,16},{5,17},{6,18},{7,19},{8,28},{9,... | collective-permute-start | bytes 1327112 | tf_op jit(solution)/shard_map/ppermute | solution.py:37
  65.4 5.8 %copy-start.7 = (bf16[256,512]{1,0:T(8,128)(2,1)}, bf16[256,512]{1,0:T(8,128)(2,1)S(1)}, u32[]{:S(2)}) copy-start(bf16[256,512]{1,0:T(8,128)(2,1)S(1)} %collective-permute-done.12.refs_4_) | copy-start | bytes 786436
  65.4 5.8 %copy-start.9 = (bf16[256,512]{1,0:T(8,128)(2,1)}, bf16[256,512]{1,0:T(8,128)(2,1)S(1)}, u32[]{:S(2)}) copy-start(bf16[256,512]{1,0:T(8,128)(2,1)S(1)} %collective-permute-done.13.refs_5_) | copy-start | bytes 786436
  67.0 10.7 %collective-permute-start.14 = (bf16[288,512]{1,0:T(8,128)(2,1)}, bf16[288,512]{1,0:T(8,128)(2,1)}, u32[]{:S(2)}, u32[]{:S(2)}) collective-permute-start(bf16[288,512]{1,0:T(8,128)(2,1)} %shard_map.86), channel_id=1, source_target_pairs={{0,8},{1,9},{2,10},{3,11},{4,12},{5,13},{6,14},{7,15},{8,0},{9,1},... | collective-permute-start | bytes 884744 | tf_op jit(solution)/shard_map/ppermute | solution.py:37
  71.2 6.4 %copy-start.4 = (bf16[528,512]{1,0:T(8,128)(2,1)S(1)}, bf16[528,512]{1,0:T(8,128)(2,1)}, u32[]{:S(2)}) copy-start(bf16[528,512]{1,0:T(8,128)(2,1)} %copy-done.2) | copy-start | bytes 1622020
  71.3 6.4 %copy-start.6 = (bf16[288,2048]{1,0:T(8,128)(2,1)S(1)}, bf16[288,2048]{1,0:T(8,128)(2,1)}, u32[]{:S(2)}) copy-start(bf16[288,2048]{1,0:T(8,128)(2,1)} %copy-done.5) | copy-start | bytes 3538948
  71.3 10.8 %collective-permute-start.15 = (bf16[288,512]{1,0:T(8,128)(2,1)}, bf16[288,512]{1,0:T(8,128)(2,1)}, u32[]{:S(2)}, u32[]{:S(2)}) collective-permute-start(bf16[288,512]{1,0:T(8,128)(2,1)} %shard_map.88), channel_id=1, source_target_pairs={{0,16},{1,17},{2,18},{3,19},{4,20},{5,21},{6,22},{7,23},{8,24},{9,... | collective-permute-start | bytes 884744 | tf_op jit(solution)/shard_map/ppermute | solution.py:37
  74.2 12.5 %collective-permute-start.16 = (bf16[288,512]{1,0:T(8,128)(2,1)}, bf16[288,512]{1,0:T(8,128)(2,1)}, u32[]{:S(2)}, u32[]{:S(2)}) collective-permute-start(bf16[288,512]{1,0:T(8,128)(2,1)} %shard_map.89), channel_id=1, source_target_pairs={{0,24},{1,25},{2,26},{3,27},{4,28},{5,29},{6,30},{7,31},{8,16},{9,... | collective-permute-start | bytes 884744 | tf_op jit(solution)/shard_map/ppermute | solution.py:37
  77.7 1.0 copy-start.8
  78.6 0.9 copy-start.10
  79.6 0.7 copy-start.14
  80.3 6.4 %copy-start.11 = (f32[288,256]{1,0:T(8,128)S(1)}, f32[288,256]{1,0:T(8,128)}, u32[]{:S(2)}) copy-start(f32[288,256]{1,0:T(8,128)} %pad_maximum_fusion.7) | copy-start | bytes 884740
  80.3 6.4 %copy-start.12 = (bf16[256,256]{1,0:T(8,128)(2,1)S(1)}, bf16[256,256]{1,0:T(8,128)(2,1)}, u32[]{:S(2)}) copy-start(bf16[256,256]{1,0:T(8,128)(2,1)} %maximum_maximum_fusion.turn) | copy-start | bytes 393220
  80.3 6.4 %copy-start.13 = (s32[144,1]{1,0:T(8,128)S(1)}, s32[144,1]{1,0:T(8,128)}, u32[]{:S(2)}) copy-start(s32[144,1]{1,0:T(8,128)} %copy.13.lengths) | copy-start | bytes 1732
